TPU v7x, 512 devices: a whole 4x4x16 slice. The times are simulated.
512 devices in a mesh: lon: 32 (over z, core), lat: 16 (over y, x).
Axes of the slice: x: 4, y: 4, z: 16, core: 2. Of those that a mesh axis runs over, the one named last changes fastest.
Arguments:
- wind_u: float32 [2, 5760, 2048], P(None, 'lon', 'lat'), may hold values from -6 to 6
- wind_v: float32 [2, 5760, 2048], P(None, 'lon', 'lat'), may hold values from -6 to 6
- thickness: float32 [2, 5760, 2048], P(None, 'lon', 'lat'), may hold values from 0.5 to 1.5
Outputs:
- wind_u_next: float32 [2, 5760, 2048], P(None, 'lon', 'lat')
- wind_v_next: float32 [2, 5760, 2048], P(None, 'lon', 'lat')
- thickness_next: float32 [2, 5760, 2048], P(None, 'lon', 'lat')
All inputs are finite; a program needn't handle non-finite values.
Results may differ from a plain program's by a relative error of at most 0.000073.
Values sent between devices are 32-bit elements; how exact they have to be, the bound alone decides.
No kernel may reach another device: no remote copies, remote signals or barrier semaphores. Data moves between devices by JAX's collectives and lax.ppermute only.
A program may use at most 64 MiB of HBM per device.

v0:
```python
import math

import jax
import jax.numpy as jnp
from jax import lax
from jax.sharding import PartitionSpec as P

HIGH = lax.Precision.HIGHEST


def from_partner(value, axis, apart):
    mask = 2**apart
    pairs = [(source, source ^ mask) for source in range(lax.axis_size(axis))]
    return lax.ppermute(value, axis, pairs)


def with_halo(cells, sides, width, closed):
    for axis, dim in sides:
        count = lax.axis_size(axis)
        ends = count if closed else count - 1
        head = lax.slice_in_dim(cells, 0, width, axis=dim)
        tail = lax.slice_in_dim(cells, cells.shape[dim] - width, cells.shape[dim], axis=dim)
        cells = jnp.concatenate(
            [
                lax.ppermute(tail, axis, [(i, (i + 1) % count) for i in range(ends)]),
                cells,
                lax.ppermute(head, axis, [((i + 1) % count, i) for i in range(ends)]),
            ],
            axis=dim,
        )
    return cells


def row_latitude(row_index, nlat_all):
    return -0.5 * math.pi + (row_index.astype(jnp.float32) + 0.5) * (math.pi / nlat_all)


def damping(lat_index, wave_index, nlat_all, nlon_all):
    ratio = jnp.cos(row_latitude(lat_index, nlat_all)) / math.cos(0.25 * math.pi)
    sine = jnp.sin(wave_index.astype(jnp.float32) * (math.pi / nlon_all))
    return ratio**2 / jnp.maximum(sine**2, ratio**2)


def dft_tables(length):
    counter = jnp.arange(length, dtype=jnp.int32)
    product = (counter[:, None] * counter[None, :] % length).astype(jnp.float32)
    angle = product * (2.0 * math.pi / length)
    return (jnp.cos(angle), jnp.sin(angle))


def forward_local(real_part, imag_part, cos_table, sin_table):
    out_real = jnp.dot(real_part, cos_table, precision=HIGH) + jnp.dot(
        imag_part, sin_table, precision=HIGH
    )
    out_imag = jnp.dot(imag_part, cos_table, precision=HIGH) - jnp.dot(
        real_part, sin_table, precision=HIGH
    )
    return (out_real, out_imag)


def inverse_local(real_part, imag_part, cos_table, sin_table):
    scale = 1.0 / cos_table.shape[0]
    out_real = (
        jnp.dot(real_part, cos_table, precision=HIGH)
        - jnp.dot(imag_part, sin_table, precision=HIGH)
    ) * scale
    out_imag = (
        jnp.dot(imag_part, cos_table, precision=HIGH)
        + jnp.dot(real_part, sin_table, precision=HIGH)
    ) * scale
    return (out_real, out_imag)


def partner(stacked, level):
    return from_partner(stacked, "lon", level)


def butterfly(values, lat_index, nlat_all, nlon_all):
    lon_cols = values.shape[-1]
    lon_parts = lax.axis_size("lon")
    depth = lon_parts.bit_length() - 1
    place = lax.axis_index("lon")
    real_part = values
    imag_part = jnp.zeros_like(values)
    for level in range(depth - 1, -1, -1):
        half_span = 1 << level
        offset = place % (2 * half_span)
        lower = offset < half_span
        twist = (offset % half_span).astype(jnp.float32) * (-2.0 * math.pi / (2 * half_span))
        cos_t = jnp.cos(twist)
        sin_t = jnp.sin(twist)
        other = partner(jnp.stack([real_part, imag_part]), level)
        diff_real = other[0] - real_part
        diff_imag = other[1] - imag_part
        new_real = jnp.where(lower, real_part + other[0], diff_real * cos_t - diff_imag * sin_t)
        new_imag = jnp.where(lower, imag_part + other[1], diff_real * sin_t + diff_imag * cos_t)
        real_part, imag_part = (new_real, new_imag)
    wave_low = jnp.zeros((), jnp.int32)
    for bit_pos in range(depth):
        wave_low = wave_low + place // 2**bit_pos % 2 * 2 ** (depth - 1 - bit_pos)
    column = jnp.arange(lon_cols, dtype=jnp.int32)
    tw_angle = (column * wave_low).astype(jnp.float32) * (-2.0 * math.pi / nlon_all)
    tw_cos = jnp.cos(tw_angle)
    tw_sin = jnp.sin(tw_angle)
    shifted_real = real_part * tw_cos - imag_part * tw_sin
    shifted_imag = real_part * tw_sin + imag_part * tw_cos
    cos_table, sin_table = dft_tables(lon_cols)
    spec_real, spec_imag = forward_local(shifted_real, shifted_imag, cos_table, sin_table)
    factor = damping(lat_index[:, None], wave_low + lon_parts * column[None, :], nlat_all, nlon_all)
    spec_real = spec_real * factor
    spec_imag = spec_imag * factor
    back_real, back_imag = inverse_local(spec_real, spec_imag, cos_table, sin_table)
    real_part = back_real * tw_cos + back_imag * tw_sin
    imag_part = back_imag * tw_cos - back_real * tw_sin
    for level in range(depth):
        half_span = 1 << level
        offset = place % (2 * half_span)
        lower = offset < half_span
        twist = (offset % half_span).astype(jnp.float32) * (2.0 * math.pi / (2 * half_span))
        cos_t = jnp.cos(twist)
        sin_t = jnp.sin(twist)
        other = partner(jnp.stack([real_part, imag_part]), level)
        other_rot_real = other[0] * cos_t - other[1] * sin_t
        other_rot_imag = other[0] * sin_t + other[1] * cos_t
        mine_rot_real = real_part * cos_t - imag_part * sin_t
        mine_rot_imag = real_part * sin_t + imag_part * cos_t
        new_real = jnp.where(lower, real_part + other_rot_real, other[0] - mine_rot_real) * 0.5
        new_imag = jnp.where(lower, imag_part + other_rot_imag, other[1] - mine_rot_imag) * 0.5
        real_part, imag_part = (new_real, new_imag)
    return real_part


def spectral(values, lat_index, nlat_all, nlon_all):
    return butterfly(values, lat_index, nlat_all, nlon_all)


def filter_pair(stacked, row_index, nlat_all, nlon_all):
    return spectral(stacked, row_index, nlat_all, nlon_all)


def lon_rim(values):
    return with_halo(values, (("lon", 2),), 1, True)


def lat_rim(values):
    return with_halo(values, (("lat", 1),), 1, False)


def row_step(wind_u, wind_v, thickness):
    levels, lat_rows, lon_cols = wind_u.shape
    nlat_all = lat_rows * lax.axis_size("lat")
    nlon_all = lon_cols * lax.axis_size("lon")
    row_index = lax.axis_index("lat") * lat_rows + jnp.arange(lat_rows, dtype=jnp.int32)
    latitude = row_latitude(row_index, nlat_all)
    lat_step = math.pi / nlat_all
    lon_step = 2.0 * math.pi / nlon_all
    time_step = 0.25 * lat_step
    coslat = jnp.cos(latitude)[:, None]
    rotation = (0.3 * jnp.sin(latitude))[:, None]
    fluxes = filter_pair(
        jnp.stack([wind_u * thickness, wind_v * thickness * coslat]), row_index, nlat_all, nlon_all
    )
    wide_x = lon_rim(fluxes[0])
    tall_y = lat_rim(fluxes[1])
    x_coef = time_step / (2.0 * lon_step * coslat)
    y_coef = time_step / (2.0 * lat_step * coslat)
    new_mass = thickness - x_coef * (wide_x[:, :, 2:] - wide_x[:, :, :-2])
    new_mass = new_mass - y_coef * (tall_y[:, 2:] - tall_y[:, :-2])
    wide_mass = lon_rim(new_mass)
    tall_mass = lat_rim(new_mass)
    push_u = -x_coef * (wide_mass[:, :, 2:] - wide_mass[:, :, :-2]) + rotation * wind_v
    push_v = (
        -(time_step / (2.0 * lat_step)) * (tall_mass[:, 2:] - tall_mass[:, :-2]) - rotation * wind_u
    )
    pushed = filter_pair(jnp.stack([push_u, push_v]), row_index, nlat_all, nlon_all)
    return (wind_u + pushed[0], wind_v + pushed[1], new_mass)


def shards(wind_u, wind_v, thickness):
    wind_u = jnp.swapaxes(wind_u, 1, 2)
    wind_v = jnp.swapaxes(wind_v, 1, 2)
    thickness = jnp.swapaxes(thickness, 1, 2)
    next_u, next_v, new_mass = row_step(wind_u, wind_v, thickness)
    return (jnp.swapaxes(next_u, 1, 2), jnp.swapaxes(next_v, 1, 2), jnp.swapaxes(new_mass, 1, 2))


def solution(mesh):
    return jax.shard_map(
        shards,
        mesh=mesh,
        in_specs=(P(None, "lon", "lat"), P(None, "lon", "lat"), P(None, "lon", "lat")),
        out_specs=(P(None, "lon", "lat"), P(None, "lon", "lat"), P(None, "lon", "lat")),
        check_vma=False,
    )
```

profile of v0, /device:TPU:153, one launch (start us, length us, event | category | flops | bytes accessed | tf_op | source)
XLA Modules:
  0.0 856.3 jit_solution(1742876964311579892)
XLA Ops:
  3.0 10.6 %collective-permute-start = (f32[2,2,2,128,180]{3,2,4,1,0:T(2,128)S(1)}, f32[2,2,2,128,180]{3,2,4,1,0:T(2,128)S(1)}, u32[]{:S(2)}, u32[]{:S(2)}) collective-permute-start(f32[2,2,2,128,180]{3,2,4,1,0:T(2,128)S(1)} %stack.176.clone), channel_id=1, source_target_pairs={{0,256},{16,272},{32,288},{48,304},{64,320},{80,336},{96,352},{112... | collective-permute-start | bytes 2211848 | tf_op jit(solution)/shard_map/ppermute | solution.py:14
  13.8 55.7 %collective-permute-done = f32[2,2,2,128,180]{3,2,4,1,0:T(2,128)S(1)} collective-permute-done((f32[2,2,2,128,180]{3,2,4,1,0:T(2,128)S(1)}, f32[2,2,2,128,180]{3,2,4,1,0:T(2,128)S(1)}, u32[]{:S(2)}, u32[]{:S(2)}) %collective-permute-start) | collective-permute-done | bytes 737312 | tf_op jit(solution)/shard_map/ppermute | solution.py:14
  72.9 66.1 %collective-permute-done.1 = f32[2,2,2,128,180]{3,2,4,1,0:T(2,128)S(1)} collective-permute-done((f32[2,2,2,128,180]{3,2,4,1,0:T(2,128)S(1)}, f32[2,2,2,128,180]{3,2,4,1,0:T(2,128)S(1)}, u32[]{:S(2)}, u32[]{:S(2)}) %collective-permute-start.1) | collective-permute-done | bytes 737312 | tf_op jit(solution)/shard_map/ppermute | solution.py:14
  141.8 34.0 %collective-permute-done.2 = f32[2,2,2,128,180]{3,2,4,1,0:T(2,128)S(1)} collective-permute-done((f32[2,2,2,128,180]{3,2,4,1,0:T(2,128)S(1)}, f32[2,2,2,128,180]{3,2,4,1,0:T(2,128)S(1)}, u32[]{:S(2)}, u32[]{:S(2)}) %collective-permute-start.2) | collective-permute-done | bytes 737312 | tf_op jit(solution)/shard_map/ppermute | solution.py:14
  179.7 16.5 %collective-permute-done.3 = f32[2,2,2,128,180]{3,2,4,1,0:T(2,128)} collective-permute-done((f32[2,2,2,128,180]{3,2,4,1,0:T(2,128)}, f32[2,2,2,128,180]{3,2,4,1,0:T(2,128)}, u32[]{:S(2)}, u32[]{:S(2)}) %collective-permute-start.3) | collective-permute-done | bytes 737312 | tf_op jit(solution)/shard_map/ppermute | solution.py:14
  222.5 17.5 %collective-permute-done.6 = f32[2,2,2,128,180]{3,2,4,1,0:T(2,128)S(1)} collective-permute-done((f32[2,2,2,128,180]{3,2,4,1,0:T(2,128)S(1)}, f32[2,2,2,128,180]{3,2,4,1,0:T(2,128)S(1)}, u32[]{:S(2)}, u32[]{:S(2)}) %collective-permute-start.6) | collective-permute-done | bytes 737312 | tf_op jit(solution)/shard_map/ppermute | solution.py:14
  243.5 34.1 %collective-permute-done.7 = f32[2,2,2,128,180]{3,2,4,1,0:T(2,128)S(1)} collective-permute-done((f32[2,2,2,128,180]{3,2,4,1,0:T(2,128)S(1)}, f32[2,2,2,128,180]{3,2,4,1,0:T(2,128)S(1)}, u32[]{:S(2)}, u32[]{:S(2)}) %collective-permute-start.7) | collective-permute-done | bytes 737312 | tf_op jit(solution)/shard_map/ppermute | solution.py:14
  278.4 6.7 collective-permute-start.8
  285.2 77.8 %collective-permute-done.8 = f32[2,2,2,128,180]{3,2,4,1,0:T(2,128)S(1)} collective-permute-done((f32[2,2,2,128,180]{3,2,4,1,0:T(2,128)S(1)}, f32[2,2,2,128,180]{3,2,4,1,0:T(2,128)S(1)}, u32[]{:S(2)}, u32[]{:S(2)}) %collective-permute-start.8) | collective-permute-done | bytes 737312 | tf_op jit(solution)/shard_map/ppermute | solution.py:14
  363.8 9.1 %collective-permute-start.9 = (f32[2,2,2,128,180]{3,2,4,1,0:T(2,128)S(1)}, f32[2,2,2,128,180]{3,2,4,1,0:T(2,128)S(1)}, u32[]{:S(2)}, u32[]{:S(2)}) collective-permute-start(f32[2,2,2,128,180]{3,2,4,1,0:T(2,128)S(1)} %copy.42), channel_id=1, source_target_pairs={{0,256},{16,272},{32,288},{48,304},{64,320},{80,336},{96,352},{112... | collective-permute-start | bytes 2211848 | tf_op jit(solution)/shard_map/ppermute | solution.py:14
  373.1 47.0 %collective-permute-done.9 = f32[2,2,2,128,180]{3,2,4,1,0:T(2,128)S(1)} collective-permute-done((f32[2,2,2,128,180]{3,2,4,1,0:T(2,128)S(1)}, f32[2,2,2,128,180]{3,2,4,1,0:T(2,128)S(1)}, u32[]{:S(2)}, u32[]{:S(2)}) %collective-permute-start.9) | collective-permute-done | bytes 737312 | tf_op jit(solution)/shard_map/ppermute | solution.py:14
  422.3 4.6 collective-permute-start.12
  429.4 5.9 collective-permute-done.13
  450.0 14.2 %collective-permute-start.18 = (f32[2,2,2,128,180]{3,2,4,1,0:T(2,128)S(1)}, f32[2,2,2,128,180]{3,2,4,1,0:T(2,128)S(1)}, u32[]{:S(2)}, u32[]{:S(2)}) collective-permute-start(f32[2,2,2,128,180]{3,2,4,1,0:T(2,128)S(1)} %stack.203.clone), channel_id=1, source_target_pairs={{0,256},{16,272},{32,288},{48,304},{64,320},{80,336},{96,352},{112... | collective-permute-start | bytes 2211848 | tf_op jit(solution)/shard_map/ppermute | solution.py:14
  464.2 49.2 %collective-permute-done.18 = f32[2,2,2,128,180]{3,2,4,1,0:T(2,128)S(1)} collective-permute-done((f32[2,2,2,128,180]{3,2,4,1,0:T(2,128)S(1)}, f32[2,2,2,128,180]{3,2,4,1,0:T(2,128)S(1)}, u32[]{:S(2)}, u32[]{:S(2)}) %collective-permute-start.18) | collective-permute-done | bytes 737312 | tf_op jit(solution)/shard_map/ppermute | solution.py:14
  516.0 59.6 %collective-permute-done.19 = f32[2,2,2,128,180]{3,2,4,1,0:T(2,128)S(1)} collective-permute-done((f32[2,2,2,128,180]{3,2,4,1,0:T(2,128)S(1)}, f32[2,2,2,128,180]{3,2,4,1,0:T(2,128)S(1)}, u32[]{:S(2)}, u32[]{:S(2)}) %collective-permute-start.19) | collective-permute-done | bytes 737312 | tf_op jit(solution)/shard_map/ppermute | solution.py:14
  578.3 34.3 %collective-permute-done.20 = f32[2,2,2,128,180]{3,2,4,1,0:T(2,128)S(1)} collective-permute-done((f32[2,2,2,128,180]{3,2,4,1,0:T(2,128)S(1)}, f32[2,2,2,128,180]{3,2,4,1,0:T(2,128)S(1)}, u32[]{:S(2)}, u32[]{:S(2)}) %collective-permute-start.20) | collective-permute-done | bytes 737312 | tf_op jit(solution)/shard_map/ppermute | solution.py:14
  615.1 16.6 %collective-permute-done.21 = f32[2,2,2,128,180]{3,2,4,1,0:T(2,128)S(1)} collective-permute-done((f32[2,2,2,128,180]{3,2,4,1,0:T(2,128)S(1)}, f32[2,2,2,128,180]{3,2,4,1,0:T(2,128)S(1)}, u32[]{:S(2)}, u32[]{:S(2)}) %collective-permute-start.21) | collective-permute-done | bytes 737312 | tf_op jit(solution)/shard_map/ppermute | solution.py:14
  632.5 4.5 collective-permute-start.22
  656.8 17.7 %collective-permute-done.24 = f32[2,2,2,128,180]{3,2,4,1,0:T(2,128)S(1)} collective-permute-done((f32[2,2,2,128,180]{3,2,4,1,0:T(2,128)S(1)}, f32[2,2,2,128,180]{3,2,4,1,0:T(2,128)S(1)}, u32[]{:S(2)}, u32[]{:S(2)}) %collective-permute-start.24) | collective-permute-done | bytes 737312 | tf_op jit(solution)/shard_map/ppermute | solution.py:14
  677.7 34.2 %collective-permute-done.25 = f32[2,2,2,128,180]{3,2,4,1,0:T(2,128)S(1)} collective-permute-done((f32[2,2,2,128,180]{3,2,4,1,0:T(2,128)S(1)}, f32[2,2,2,128,180]{3,2,4,1,0:T(2,128)S(1)}, u32[]{:S(2)}, u32[]{:S(2)}) %collective-permute-start.25) | collective-permute-done | bytes 737312 | tf_op jit(solution)/shard_map/ppermute | solution.py:14
  716.1 78.0 %collective-permute-done.26 = f32[2,2,2,128,180]{3,2,4,1,0:T(2,128)S(1)} collective-permute-done((f32[2,2,2,128,180]{3,2,4,1,0:T(2,128)S(1)}, f32[2,2,2,128,180]{3,2,4,1,0:T(2,128)S(1)}, u32[]{:S(2)}, u32[]{:S(2)}) %collective-permute-start.26) | collective-permute-done | bytes 737312 | tf_op jit(solution)/shard_map/ppermute | solution.py:14
  794.9 7.2 collective-permute-start.27
  802.8 51.5 %collective-permute-done.27 = f32[2,2,2,128,180]{3,2,4,1,0:T(2,128)S(1)} collective-permute-done((f32[2,2,2,128,180]{3,2,4,1,0:T(2,128)S(1)}, f32[2,2,2,128,180]{3,2,4,1,0:T(2,128)S(1)}, u32[]{:S(2)}, u32[]{:S(2)}) %collective-permute-start.27) | collective-permute-done | bytes 737312 | tf_op jit(solution)/shard_map/ppermute | solution.py:14
  (172 shorter events, 100.2 us)
Async XLA Ops:
  3.0 66.6 %collective-permute-start = (f32[2,2,2,128,180]{3,2,4,1,0:T(2,128)S(1)}, f32[2,2,2,128,180]{3,2,4,1,0:T(2,128)S(1)}, u32[]{:S(2)}, u32[]{:S(2)}) collective-permute-start(f32[2,2,2,128,180]{3,2,4,1,0:T(2,128)S(1)} %stack.176.clone), channel_id=1, source_target_pairs={{0,256},{16,272},{32,288},{48,304},{64,320},{80,336},{96,352},{112... | collective-permute-start | bytes 2211848 | tf_op jit(solution)/shard_map/ppermute | solution.py:14
  70.8 68.2 %collective-permute-start.1 = (f32[2,2,2,128,180]{3,2,4,1,0:T(2,128)S(1)}, f32[2,2,2,128,180]{3,2,4,1,0:T(2,128)S(1)}, u32[]{:S(2)}, u32[]{:S(2)}) collective-permute-start(f32[2,2,2,128,180]{3,2,4,1,0:T(2,128)S(1)} %copy.18), channel_id=1, source_target_pairs={{0,128},{16,144},{32,160},{48,176},{64,192},{80,208},{96,224},{112... | collective-permute-start | bytes 2211848 | tf_op jit(solution)/shard_map/ppermute | solution.py:14
  139.7 36.2 %collective-permute-start.2 = (f32[2,2,2,128,180]{3,2,4,1,0:T(2,128)S(1)}, f32[2,2,2,128,180]{3,2,4,1,0:T(2,128)S(1)}, u32[]{:S(2)}, u32[]{:S(2)}) collective-permute-start(f32[2,2,2,128,180]{3,2,4,1,0:T(2,128)S(1)} %copy.21), channel_id=1, source_target_pairs={{0,64},{16,80},{32,96},{48,112},{64,0},{80,16},{96,32},{112,48},{1... | collective-permute-start | bytes 2211848 | tf_op jit(solution)/shard_map/ppermute | solution.py:14
  177.4 18.8 %collective-permute-start.3 = (f32[2,2,2,128,180]{3,2,4,1,0:T(2,128)}, f32[2,2,2,128,180]{3,2,4,1,0:T(2,128)}, u32[]{:S(2)}, u32[]{:S(2)}) collective-permute-start(f32[2,2,2,128,180]{3,2,4,1,0:T(2,128)} %copy.24), channel_id=1, source_target_pairs={{0,32},{16,48},{32,0},{48,16},{64,96},{80,112},{96,64},{112,80},{1... | collective-permute-start | bytes 2211848 | tf_op jit(solution)/shard_map/ppermute | solution.py:14
  198.1 6.0 collective-permute-start.4
  220.4 19.6 %collective-permute-start.6 = (f32[2,2,2,128,180]{3,2,4,1,0:T(2,128)S(1)}, f32[2,2,2,128,180]{3,2,4,1,0:T(2,128)S(1)}, u32[]{:S(2)}, u32[]{:S(2)}) collective-permute-start(f32[2,2,2,128,180]{3,2,4,1,0:T(2,128)S(1)} %copy.33), channel_id=1, source_target_pairs={{0,32},{16,48},{32,0},{48,16},{64,96},{80,112},{96,64},{112,80},{1... | collective-permute-start | bytes 2211848 | tf_op jit(solution)/shard_map/ppermute | solution.py:14
  240.9 36.7 %collective-permute-start.7 = (f32[2,2,2,128,180]{3,2,4,1,0:T(2,128)S(1)}, f32[2,2,2,128,180]{3,2,4,1,0:T(2,128)S(1)}, u32[]{:S(2)}, u32[]{:S(2)}) collective-permute-start(f32[2,2,2,128,180]{3,2,4,1,0:T(2,128)S(1)} %copy.36), channel_id=1, source_target_pairs={{0,64},{16,80},{32,96},{48,112},{64,0},{80,16},{96,32},{112,48},{1... | collective-permute-start | bytes 2211848 | tf_op jit(solution)/shard_map/ppermute | solution.py:14
  278.4 84.6 %collective-permute-start.8 = (f32[2,2,2,128,180]{3,2,4,1,0:T(2,128)S(1)}, f32[2,2,2,128,180]{3,2,4,1,0:T(2,128)S(1)}, u32[]{:S(2)}, u32[]{:S(2)}) collective-permute-start(f32[2,2,2,128,180]{3,2,4,1,0:T(2,128)S(1)} %copy.39), channel_id=1, source_target_pairs={{0,128},{16,144},{32,160},{48,176},{64,192},{80,208},{96,224},{112... | collective-permute-start | bytes 2211848 | tf_op jit(solution)/shard_map/ppermute | solution.py:14
  363.8 56.3 %collective-permute-start.9 = (f32[2,2,2,128,180]{3,2,4,1,0:T(2,128)S(1)}, f32[2,2,2,128,180]{3,2,4,1,0:T(2,128)S(1)}, u32[]{:S(2)}, u32[]{:S(2)}) collective-permute-start(f32[2,2,2,128,180]{3,2,4,1,0:T(2,128)S(1)} %copy.42), channel_id=1, source_target_pairs={{0,256},{16,272},{32,288},{48,304},{64,320},{80,336},{96,352},{112... | collective-permute-start | bytes 2211848 | tf_op jit(solution)/shard_map/ppermute | solution.py:14
  420.4 8.4 collective-permute-start.10
  421.0 7.9 collective-permute-start.11
  422.3 7.1 collective-permute-start.12
  426.9 8.4 collective-permute-start.13
  435.7 8.6 %collective-permute-start.14 = (f32[2,128,1]{1,2,0:T(1,128)S(1)}, f32[2,128,1]{1,2,0:T(1,128)S(1)}, u32[]{:S(2)}, u32[]{:S(2)}) collective-permute-start(f32[2,128,1]{1,2,0:T(1,128)S(1)} %get-tuple-element.140), channel_id=1, source_target_pairs={{16,0},{32,16},{48,32},{64,48},{80,64},{96,80},{112,96},{128,112},... | collective-permute-start | bytes 3080 | tf_op jit(solution)/shard_map/ppermute | solution.py:27
  439.0 6.3 collective-permute-start.16
  440.9 8.4 collective-permute-start.17
  450.0 63.4 %collective-permute-start.18 = (f32[2,2,2,128,180]{3,2,4,1,0:T(2,128)S(1)}, f32[2,2,2,128,180]{3,2,4,1,0:T(2,128)S(1)}, u32[]{:S(2)}, u32[]{:S(2)}) collective-permute-start(f32[2,2,2,128,180]{3,2,4,1,0:T(2,128)S(1)} %stack.203.clone), channel_id=1, source_target_pairs={{0,256},{16,272},{32,288},{48,304},{64,320},{80,336},{96,352},{112... | collective-permute-start | bytes 2211848 | tf_op jit(solution)/shard_map/ppermute | solution.py:14
  514.1 61.6 %collective-permute-start.19 = (f32[2,2,2,128,180]{3,2,4,1,0:T(2,128)S(1)}, f32[2,2,2,128,180]{3,2,4,1,0:T(2,128)S(1)}, u32[]{:S(2)}, u32[]{:S(2)}) collective-permute-start(f32[2,2,2,128,180]{3,2,4,1,0:T(2,128)S(1)} %copy.48), channel_id=1, source_target_pairs={{0,128},{16,144},{32,160},{48,176},{64,192},{80,208},{96,224},{112... | collective-permute-start | bytes 2211848 | tf_op jit(solution)/shard_map/ppermute | solution.py:14
  576.3 36.2 %collective-permute-start.20 = (f32[2,2,2,128,180]{3,2,4,1,0:T(2,128)S(1)}, f32[2,2,2,128,180]{3,2,4,1,0:T(2,128)S(1)}, u32[]{:S(2)}, u32[]{:S(2)}) collective-permute-start(f32[2,2,2,128,180]{3,2,4,1,0:T(2,128)S(1)} %copy.51), channel_id=1, source_target_pairs={{0,64},{16,80},{32,96},{48,112},{64,0},{80,16},{96,32},{112,48},{1... | collective-permute-start | bytes 2211848 | tf_op jit(solution)/shard_map/ppermute | solution.py:14
  613.2 18.6 %collective-permute-start.21 = (f32[2,2,2,128,180]{3,2,4,1,0:T(2,128)S(1)}, f32[2,2,2,128,180]{3,2,4,1,0:T(2,128)S(1)}, u32[]{:S(2)}, u32[]{:S(2)}) collective-permute-start(f32[2,2,2,128,180]{3,2,4,1,0:T(2,128)S(1)} %copy.54), channel_id=1, source_target_pairs={{0,32},{16,48},{32,0},{48,16},{64,96},{80,112},{96,64},{112,80},{1... | collective-permute-start | bytes 2211848 | tf_op jit(solution)/shard_map/ppermute | solution.py:14
  654.8 19.6 %collective-permute-start.24 = (f32[2,2,2,128,180]{3,2,4,1,0:T(2,128)S(1)}, f32[2,2,2,128,180]{3,2,4,1,0:T(2,128)S(1)}, u32[]{:S(2)}, u32[]{:S(2)}) collective-permute-start(f32[2,2,2,128,180]{3,2,4,1,0:T(2,128)S(1)} %copy.63), channel_id=1, source_target_pairs={{0,32},{16,48},{32,0},{48,16},{64,96},{80,112},{96,64},{112,80},{1... | collective-permute-start | bytes 2211848 | tf_op jit(solution)/shard_map/ppermute | solution.py:14
  675.2 36.7 %collective-permute-start.25 = (f32[2,2,2,128,180]{3,2,4,1,0:T(2,128)S(1)}, f32[2,2,2,128,180]{3,2,4,1,0:T(2,128)S(1)}, u32[]{:S(2)}, u32[]{:S(2)}) collective-permute-start(f32[2,2,2,128,180]{3,2,4,1,0:T(2,128)S(1)} %copy.66), channel_id=1, source_target_pairs={{0,64},{16,80},{32,96},{48,112},{64,0},{80,16},{96,32},{112,48},{1... | collective-permute-start | bytes 2211848 | tf_op jit(solution)/shard_map/ppermute | solution.py:14
  712.7 81.3 %collective-permute-start.26 = (f32[2,2,2,128,180]{3,2,4,1,0:T(2,128)S(1)}, f32[2,2,2,128,180]{3,2,4,1,0:T(2,128)S(1)}, u32[]{:S(2)}, u32[]{:S(2)}) collective-permute-start(f32[2,2,2,128,180]{3,2,4,1,0:T(2,128)S(1)} %copy.69), channel_id=1, source_target_pairs={{0,128},{16,144},{32,160},{48,176},{64,192},{80,208},{96,224},{112... | collective-permute-start | bytes 2211848 | tf_op jit(solution)/shard_map/ppermute | solution.py:14
  794.9 59.5 %collective-permute-start.27 = (f32[2,2,2,128,180]{3,2,4,1,0:T(2,128)S(1)}, f32[2,2,2,128,180]{3,2,4,1,0:T(2,128)S(1)}, u32[]{:S(2)}, u32[]{:S(2)}) collective-permute-start(f32[2,2,2,128,180]{3,2,4,1,0:T(2,128)S(1)} %copy.72), channel_id=1, source_target_pairs={{0,256},{16,272},{32,288},{48,304},{64,320},{80,336},{96,352},{112... | collective-permute-start | bytes 2211848 | tf_op jit(solution)/shard_map/ppermute | solution.py:14
  (13 other events, 77.3 us)
where the time goes:
time: 861 us; the launch traced here: 856 us
  waiting for transfers between devices  707 us (82%)
  starting transfers between devices  102 us (12%)
  matrix products  21 us (2%)
  local copies, waits for them, and re-layouts  14.5 us (2%)
  other arithmetic  8.75 us (1%)
    ppermute x20, waiting for transfers between devices, from_partner(): return lax.ppermute(value, axis, pairs)  695 us
    ppermute x20, starting transfers between devices, from_partner(): return lax.ppermute(value, axis, pairs)  85.2 us
  transfers between devices with their start and end apart: 28, of which 24 were waited for; matrix products, arithmetic and copies ran while one was open for 0% of the time, Pallas kernels for 0%

commit v1 on v0

v1 whole, which is shorter than its diff:
```python
import functools
import math

import jax
import jax.numpy as jnp
import numpy as np
from jax import lax
from jax.experimental import pallas as pl
from jax.experimental.pallas import tpu as pltpu
from jax.sharding import PartitionSpec as P

HIGH = lax.Precision.HIGHEST

NLON = 5760
NLAT = 2048
PARTS = 32
SEG = 180
LANES = 128
TAIL = SEG - LANES
HALF = 64
ROWS = 8
WAVES = PARTS // 2 + 1
WIDE = 2 * LANES
SCALE = 1.0 / NLON
CHUNK = 5 * ROWS


def places(variant):
    b = np.arange(SEG)
    return np.where(b < LANES, b, b + variant * HALF)


def dft_tables():
    b = np.arange(SEG)
    angle = (np.outer(b, b) % SEG) * (2.0 * math.pi / SEG)
    cos, sin = np.cos(angle), np.sin(angle)
    forward, inverse = [], []
    for variant in (0, 1):
        at = places(variant)
        table = np.zeros((2 * WIDE, 2 * WIDE))
        table[np.ix_(at, b)] = cos
        table[np.ix_(at, WIDE + b)] = -sin
        table[np.ix_(WIDE + at, b)] = sin
        table[np.ix_(WIDE + at, WIDE + b)] = cos
        forward.append(table)
        table = np.zeros((2 * WIDE, 2 * WIDE))
        table[np.ix_(b, at)] = cos
        table[np.ix_(b, WIDE + at)] = sin
        table[np.ix_(WIDE + b, at)] = -sin
        table[np.ix_(WIDE + b, WIDE + at)] = cos
        inverse.append(table)
    return np.stack(forward).astype(np.float32), np.stack(inverse).astype(np.float32)


def twiddle_table():
    angle = np.zeros((WAVES, WIDE))
    turn = np.outer(np.arange(WAVES), np.arange(SEG)) * (2.0 * math.pi / NLON)
    for variant in (0, 1):
        angle[:, places(variant)] = turn
    return np.concatenate([np.cos(angle), np.sin(angle)]).astype(np.float32)


def wave_table():
    k = np.arange(WAVES)[:, None] + PARTS * np.arange(SEG)[None, :]
    step = np.float32(math.pi / NLON)
    here = np.sin(k.astype(np.float32) * step) ** 2
    there = np.sin(((NLON - k) % NLON).astype(np.float32) * step) ** 2
    slope = 2.0 * np.sin(2.0 * math.pi * k / NLON)
    table = np.zeros((3 * WAVES, WIDE), np.float32)
    table[:, :SEG] = np.concatenate([here, there, slope])
    return table


def row_table():
    j = np.arange(-1, NLAT + 1)
    phi = np.float32(-0.5 * math.pi) + (j.astype(np.float32) + np.float32(0.5)) * np.float32(math.pi / NLAT)
    phi = phi.astype(np.float64)
    lat_step, lon_step = math.pi / NLAT, 2.0 * math.pi / NLON
    time_step = 0.25 * lat_step
    cos = np.cos(phi)
    y_coef = time_step / (2.0 * lat_step * cos)
    y_coef[0] = y_coef[-1] = 0.0
    table = np.zeros((NLAT, LANES))
    table[:, 0] = (cos / math.cos(0.25 * math.pi))[1:-1] ** 2
    table[:, 1] = (time_step / (2.0 * lon_step * cos))[1:-1]
    table[:, 2] = y_coef[1:-1]
    table[:, 3] = 0.3 * np.sin(phi)[1:-1]
    table[:, 4] = cos[1:-1]
    table[:, 5] = np.repeat(y_coef[0:NLAT:ROWS], ROWS)
    table[:, 6] = np.repeat(y_coef[ROWS + 1 :: ROWS], ROWS)
    return table.reshape(NLAT // ROWS, ROWS, LANES).astype(np.float32)


PUSH_COEF = 0.25 / 2.0


def add(x, y):
    if x is None:
        return y
    return x if y is None else x + y


def sub(x, y):
    if y is None:
        return x
    return -y if x is None else x - y


def times(z, cos, sin):
    re, im = z
    if abs(sin) < 1e-15:
        return (re * cos, None if im is None else im * cos)
    if im is None:
        return (re * cos, re * sin)
    return (re * cos - im * sin, re * sin + im * cos)


def real_fft(values):
    n = len(values)
    if n == 2:
        return [(values[0] + values[1], None), (values[0] - values[1], None)]
    even, odd = real_fft(values[0::2]), real_fft(values[1::2])
    out = [None] * (n // 2 + 1)
    out[0] = (even[0][0] + odd[0][0], None)
    out[n // 2] = (even[0][0] - odd[0][0], None)
    for k in range(1, n // 4):
        re, im = times(odd[k], math.cos(2 * math.pi * k / n), -math.sin(2 * math.pi * k / n))
        out[k] = (add(even[k][0], re), add(even[k][1], im))
        out[n // 2 - k] = (sub(even[k][0], re), sub(im, even[k][1]))
    out[n // 4] = (even[n // 4][0], -odd[n // 4][0])
    return out


def real_ifft(waves):
    n = 2 * (len(waves) - 1)
    if n == 2:
        return [waves[0][0] + waves[1][0], waves[0][0] - waves[1][0]]
    even, odd = [None] * (n // 4 + 1), [None] * (n // 4 + 1)
    even[0] = (waves[0][0] + waves[n // 2][0], None)
    odd[0] = (waves[0][0] - waves[n // 2][0], None)
    for k in range(1, n // 4):
        (re, im), (far_re, far_im) = waves[k], waves[n // 2 - k]
        even[k] = (re + far_re, im - far_im)
        odd[k] = times((re - far_re, im + far_im), math.cos(2 * math.pi * k / n), math.sin(2 * math.pi * k / n))
    even[n // 4] = (2.0 * waves[n // 4][0], None)
    odd[n // 4] = (-2.0 * waves[n // 4][1], None)
    out = [None] * n
    out[0::2], out[1::2] = real_ifft(even), real_ifft(odd)
    return out


def pack_kernel(u_ref, v_ref, h_ref, out_ref, tail_ref):
    tail_ref[...] = jnp.zeros_like(tail_ref)
    for level in range(2):
        span = slice(level * 16, level * 16 + 16)
        for f, ref in enumerate((u_ref, v_ref, h_ref)):
            out_ref[span, f * ROWS : (f + 1) * ROWS, :] = ref[level, :LANES, :].T.reshape(16, ROWS, LANES)
        for f, pair in ((3, (u_ref, v_ref)), (4, (h_ref, h_ref))):
            for half, ref in enumerate(pair):
                tail_ref[half * HALF : half * HALF + TAIL, :] = ref[level, LANES:, :]
            out_ref[span, f * ROWS : (f + 1) * ROWS, :] = tail_ref[...].T.reshape(16, ROWS, LANES)


def unpack_kernel(in_ref, u_ref, v_ref, h_ref, u_out, v_out, h_out):
    for level in range(2):
        span = slice(level * 16, level * 16 + 16)

        def back(f):
            return in_ref[span, f * ROWS : (f + 1) * ROWS, :].reshape(LANES, LANES).T

        tails = (back(3), back(4))
        for f, (ref, out) in enumerate(((u_ref, u_out), (v_ref, v_out), (h_ref, h_out))):
            out[level, :LANES, :] = ref[level, :LANES, :] + back(f)
            half = HALF * (f == 1)
            out[level, LANES:, :] = ref[level, LANES:, :] + tails[f // 2][half : half + TAIL]


def dot(x, y):
    return jnp.dot(x, y, precision=HIGH, preferred_element_type=jnp.float32)


H, U, UH, V, VH = range(5)
BLOCK = WAVES * ROWS


def forward_kernel(x_ref, table_ref, twiddle_ref, wave_ref, row_ref, spec_ref, up_ref, down_ref, left_ref):
    def tile(a, f):
        return x_ref[a, f * ROWS : (f + 1) * ROWS, :]

    def product(f, g):
        return lambda a: tile(a, f) * tile(a, g)

    columns = (
        (lambda a: tile(a, 0), 0, (U,)),
        (lambda a: tile(a, 1), 0, (V,)),
        (lambda a: tile(a, 2), 0, (H,)),
        (product(0, 2), 0, (UH,)),
        (product(1, 2), 0, (VH,)),
        (lambda a: tile(a, 3), 1, (U, V)),
        (lambda a: tile(a, 4), 1, (H,)),
        (product(3, 4), 1, (UH, VH)),
    )
    for get, part, fields in columns:
        lanes = slice(part * LANES, (part + 1) * LANES)
        late = slice(WIDE + part * LANES, WIDE + (part + 1) * LANES)
        for k1, (re, im) in enumerate(real_fft([get(a) for a in range(PARTS)])):
            cos = twiddle_ref[k1 : k1 + 1, lanes]
            sin = twiddle_ref[WAVES + k1 : WAVES + k1 + 1, lanes]
            if im is None:
                new_re, new_im = re * cos, -re * sin
            else:
                new_re, new_im = re * cos + im * sin, im * cos - re * sin
            for f in fields:
                rows = slice(f * BLOCK + k1 * ROWS, f * BLOCK + (k1 + 1) * ROWS)
                left_ref[rows, lanes] = new_re
                left_ref[rows, late] = new_im
    spec_ref[: V * BLOCK, :] = dot(left_ref[: V * BLOCK, :], table_ref[0])
    spec_ref[V * BLOCK :, :] = dot(left_ref[V * BLOCK :, :], table_ref[1])

    row = row_ref[0]
    ratio2, x_coef, coslat = row[:, 0:1], row[:, 1:2], row[:, 4:5]
    real, imag = slice(0, WIDE), slice(WIDE, 2 * WIDE)
    zeros = jnp.zeros((2, WIDE), jnp.float32)
    for k1 in range(WAVES):
        here, there, slope = (wave_ref[i * WAVES + k1 : i * WAVES + k1 + 1, :] for i in range(3))
        damp = 0.5 * (ratio2 / jnp.maximum(here, ratio2) + ratio2 / jnp.maximum(there, ratio2))

        def rows(f):
            return slice(f * BLOCK + k1 * ROWS, f * BLOCK + (k1 + 1) * ROWS)

        across = x_coef * slope * damp
        gain_re = across * spec_ref[rows(UH), imag]
        gain_im = -across * spec_ref[rows(UH), real]
        spec_ref[rows(UH), real] = gain_re
        spec_ref[rows(UH), imag] = gain_im
        mass_re = spec_ref[rows(H), real] + gain_re
        mass_im = spec_ref[rows(H), imag] + gain_im
        scale = damp * coslat
        flux_re = scale * spec_ref[rows(VH), real]
        flux_im = scale * spec_ref[rows(VH), imag]
        spec_ref[rows(VH), real] = flux_re
        spec_ref[rows(VH), imag] = flux_im
        up_ref[k1] = jnp.concatenate([mass_re[7:8], mass_im[7:8], flux_re[6:8], flux_im[6:8], zeros], axis=0)
        down_ref[k1] = jnp.concatenate([mass_re[0:1], mass_im[0:1], flux_re[0:2], flux_im[0:2], zeros], axis=0)


def inverse_kernel(spec_ref, below_ref, above_ref, table_ref, twiddle_ref, wave_ref, row_ref, out_ref, left_ref, right_ref):
    row = row_ref[0]
    ratio2, x_coef, y_coef, rotation = (row[:, i : i + 1] for i in range(4))
    y_below, y_above = row[0:1, 5:6], row[0:1, 6:7]
    spans = (slice(0, WIDE), slice(WIDE, 2 * WIDE))
    for k1 in range(WAVES):
        here, there, slope = (wave_ref[i * WAVES + k1 : i * WAVES + k1 + 1, :] for i in range(3))
        damp = (0.5 * SCALE) * (ratio2 / jnp.maximum(here, ratio2) + ratio2 / jnp.maximum(there, ratio2))

        def rows(f):
            return slice(f * BLOCK + k1 * ROWS, f * BLOCK + (k1 + 1) * ROWS)

        mass = []
        for part, span in enumerate(spans):
            flux = spec_ref[rows(VH), span]
            gain = spec_ref[rows(UH), span]
            mass_below, mass_above = below_ref[k1, part : part + 1, :], above_ref[k1, part : part + 1, :]
            fluxes_below = below_ref[k1, 2 + 2 * part : 4 + 2 * part, :]
            fluxes_above = above_ref[k1, 2 + 2 * part : 4 + 2 * part, :]
            prev = jnp.concatenate([fluxes_below[1:2], flux[:-1]], axis=0)
            following = jnp.concatenate([flux[1:], fluxes_above[0:1]], axis=0)
            change = gain - y_coef * (following - prev)
            new = spec_ref[rows(H), span] + change
            new_below = mass_below - y_below * (flux[0:1] - fluxes_below[0:1])
            new_above = mass_above - y_above * (fluxes_above[1:2] - flux[7:8])
            mass.append(new)
            prev = jnp.concatenate([new_below, new[:-1]], axis=0)
            following = jnp.concatenate([new[1:], new_above], axis=0)
            push = -PUSH_COEF * (following - prev) - rotation * spec_ref[rows(U), span]
            left_ref[rows(2), span] = damp * push
            left_ref[rows(0), span] = SCALE * change
        across = x_coef * slope
        left_ref[rows(1), spans[0]] = damp * (across * mass[1] + rotation * spec_ref[rows(V), spans[0]])
        left_ref[rows(1), spans[1]] = damp * (rotation * spec_ref[rows(V), spans[1]] - across * mass[0])
    right_ref[: 2 * BLOCK, :] = dot(left_ref[: 2 * BLOCK, :], table_ref[0])
    right_ref[2 * BLOCK :, :] = dot(left_ref[2 * BLOCK :, :], table_ref[1])
    for f, part, fields in ((0, 0, (1,)), (1, 0, (2,)), (2, 0, (0,)), (3, 1, (1, 2)), (4, 1, (0,))):
        lanes = slice(part * LANES, (part + 1) * LANES)
        late = slice(WIDE + part * LANES, WIDE + (part + 1) * LANES)
        waves = []
        for k1 in range(WAVES):
            cos = twiddle_ref[k1 : k1 + 1, lanes]
            sin = twiddle_ref[WAVES + k1 : WAVES + k1 + 1, lanes]
            spots = [slice(g * BLOCK + k1 * ROWS, g * BLOCK + (k1 + 1) * ROWS) for g in fields]
            re = functools.reduce(lambda x, y: x + y, [right_ref[s, lanes] for s in spots])
            im = functools.reduce(lambda x, y: x + y, [right_ref[s, late] for s in spots])
            waves.append((re * cos - im * sin, None if k1 in (0, WAVES - 1) else im * cos + re * sin))
        for a, value in enumerate(real_ifft(waves)):
            out_ref[a, f * ROWS : (f + 1) * ROWS, :] = value


def in_vmem():
    return pl.BlockSpec(memory_space=pltpu.VMEM)


PARAMS = pltpu.CompilerParams(vmem_limit_bytes=40 * 2**20)


def like(*shape):
    return jax.ShapeDtypeStruct(shape, jnp.float32)


def neighbour_pairs(up):
    pairs = []
    for lat in range(16):
        for level in range(2):
            for r in range(15):
                pairs.append(((level * 16 + r) * 16 + lat, (level * 16 + r + 1) * 16 + lat))
            if lat < 15:
                pairs.append(((level * 16 + 15) * 16 + lat, level * 16 * 16 + lat + 1))
    return pairs if up else [(b, a) for a, b in pairs]


def pack(u, v, h):
    return pl.pallas_call(
        pack_kernel,
        out_shape=like(PARTS, CHUNK, LANES),
        in_specs=[in_vmem()] * 3,
        out_specs=in_vmem(),
        scratch_shapes=[pltpu.VMEM((LANES, LANES), jnp.float32)],
        compiler_params=PARAMS,
        name="pack",
    )(u, v, h)


def forward(whole, row):
    return pl.pallas_call(
        forward_kernel,
        out_shape=(like(5 * BLOCK, 2 * WIDE), like(WAVES, ROWS, WIDE), like(WAVES, ROWS, WIDE)),
        in_specs=[in_vmem()] * 5,
        out_specs=(in_vmem(),) * 3,
        scratch_shapes=[pltpu.VMEM((5 * BLOCK, 2 * WIDE), jnp.float32)],
        compiler_params=PARAMS,
        name="forward",
    )(whole, dft_tables()[0], twiddle_table(), wave_table(), row)


def inverse(spec, below, above, row):
    return pl.pallas_call(
        inverse_kernel,
        out_shape=like(PARTS, CHUNK, LANES),
        in_specs=[in_vmem()] * 7,
        out_specs=in_vmem(),
        scratch_shapes=[pltpu.VMEM((3 * BLOCK, 2 * WIDE), jnp.float32)] * 2,
        compiler_params=PARAMS,
        name="inverse",
    )(spec, below, above, dft_tables()[1], twiddle_table(), wave_table(), row)


def unpack(back, u, v, h):
    return pl.pallas_call(
        unpack_kernel,
        out_shape=(like(2, SEG, LANES),) * 3,
        in_specs=[in_vmem()] * 4,
        out_specs=(in_vmem(),) * 3,
        compiler_params=PARAMS,
        name="unpack",
    )(back, u, v, h)


def row_of(group):
    return lax.dynamic_slice_in_dim(jnp.asarray(row_table()), group, 1, axis=0)


def step(u, v, h):
    row = row_of(lax.axis_index("lat") * 16 + lax.axis_index("lon") % 16)
    whole = lax.all_to_all(pack(u, v, h), "lon", 0, 0, tiled=True)
    spec, up, down = forward(whole, row)
    below = lax.ppermute(up, ("lon", "lat"), neighbour_pairs(True))
    above = lax.ppermute(down, ("lon", "lat"), neighbour_pairs(False))
    back = lax.all_to_all(inverse(spec, below, above, row), "lon", 0, 0, tiled=True)
    return unpack(back, u, v, h)


def solution(mesh):
    spec = P(None, "lon", "lat")
    return jax.shard_map(step, mesh=mesh, in_specs=(spec,) * 3, out_specs=(spec,) * 3, check_vma=False)
```

time: 861 us -> 137 us (0.16)
  the two profiles are of different devices: /device:TPU:153 before, /device:TPU:1 now
where the time goes in v1:
time: 137 us; the launch traced here: 136 us
  blocking collectives  57.2 us (42%)
  waiting for transfers between devices  42.8 us (31%)
  starting transfers between devices  21.2 us (15%)
  local copies, waits for them, and re-layouts  7.45 us (5%)
  Pallas kernels  6.34 us (5%)
    all_to_all x1, blocking collectives, step(): lax.all_to_all(inverse(spec, below, above, row), 'lon', 0, 0, tiled=True)  57.2 us
    all_to_all x1, waiting for transfers between devices, step(): whole = lax.all_to_all(pack(u, v, h), 'lon', 0, 0, tiled=True)  38.4 us
    all_to_all x1, starting transfers between devices, step(): whole = lax.all_to_all(pack(u, v, h), 'lon', 0, 0, tiled=True)  16.9 us
    unnamed x11, local copies, waits for them, and re-layouts  4.45 us
    ppermute x1, waiting for transfers between devices, step(): above = lax.ppermute(down, ('lon', 'lat'), neighbour_pairs(False))  4.37 us
    pallas_call x1, Pallas kernels, forward(): pl.pallas_call(forward_kernel, out_shape=(like(5 * BLOCK, 2 * WIDE), like...  2.84 us
  transfers between devices with their start and end apart: 3, of which 2 were waited for; matrix products, arithmetic and copies ran while one was open for 1% of the time, Pallas kernels for 0%

profile of v1, /device:TPU:1, one launch (start us, length us, event | category | flops | bytes accessed | tf_op | source)
XLA Modules:
  0.0 135.7 jit_solution(5435713483987319309)
XLA Ops:
  0.6 0.0 copy-start.2
  0.6 0.0 copy-start.3
  0.7 1.0 copy.13.u_ref
  1.6 0.9 copy.14.v_ref
  2.6 0.9 copy.15.h_ref
  3.5 1.1 pack.1
  4.6 16.9 %all-to-all-start = ((f32[32,40,128]{2,1,0:T(8,128)}), f32[32,40,128]{2,1,0:T(8,128)S(1)}, u32[]{:S(2)}, u32[]{:S(2)}) async-start(f32[32,40,128]{2,1,0:T(8,128)} %pack.1), calls=%async_computation | async-start | bytes 1310720 | tf_op jit(solution)/shard_map/all_to_all | solution.py:373
  21.5 0.7 constant_dynamic-slice_fusion.row_ref
  22.2 38.4 %all-to-all-done.x_ref = f32[32,40,128]{2,1,0:T(8,128)S(1)} async-done(((f32[32,40,128]{2,1,0:T(8,128)}), f32[32,40,128]{2,1,0:T(8,128)S(1)}, u32[]{:S(2)}, u32[]{:S(2)}) %all-to-all-start) | async-done | bytes 655392 | tf_op jit(solution)/shard_map/all_to_all | solution.py:373
  60.6 0.0 copy-done.2
  60.6 0.0 copy-done.3
  60.6 1.6 %copy-done.1 = f32[2,512,512]{2,1,0:T(8,128)S(1)} copy-done((f32[2,512,512]{2,1,0:T(8,128)S(1)}, f32[2,512,512]{2,1,0:T(8,128)}, u32[]{:S(2)}) %copy-start.1) | copy-done | bytes 2097176
  62.2 2.8 %forward.1 = (f32[680,512]{1,0:T(8,128)S(1)}, f32[17,8,256]{2,1,0:T(8,128)S(1)}, f32[17,8,256]{2,1,0:T(8,128)S(1)}) custom-call(f32[32,40,128]{2,1,0:T(8,128)S(1)} %all-to-all-done.x_ref, f32[2,512,512]{2,1,0:T(8,128)S(1)} %copy-done.1, f32[34,256]{1,0:T(8,128)S(1)} %copy-done.3, f32[51,256]{1,0:T(8,128)S(1)} %copy-done.2, ...), custom_call_target="tpu_custom_call" | custom-call | tf_op jit(solution)/shard_map/forward/pallas_call | solution.py:333
  65.0 2.3 %collective-permute-start = (f32[17,8,256]{2,1,0:T(8,128)S(1)}, f32[17,8,256]{2,1,0:T(8,128)S(1)}, u32[]{:S(2)}, u32[]{:S(2)}) collective-permute-start(f32[17,8,256]{2,1,0:T(8,128)S(1)} %get-tuple-element.7), channel_id=1, source_target_pairs={{0,16},{16,32},{32,48},{48,64},{64,80},{80,96},{96,112},{112,128},... | collective-permute-start | bytes 417800 | tf_op jit(solution)/shard_map/ppermute | solution.py:375
  67.4 2.0 %collective-permute-start.1 = (f32[17,8,256]{2,1,0:T(8,128)S(1)}, f32[17,8,256]{2,1,0:T(8,128)S(1)}, u32[]{:S(2)}, u32[]{:S(2)}) collective-permute-start(f32[17,8,256]{2,1,0:T(8,128)S(1)} %get-tuple-element.8), channel_id=1, source_target_pairs={{16,0},{32,16},{48,32},{64,48},{80,64},{96,80},{112,96},{128,112},... | collective-permute-start | bytes 417800 | tf_op jit(solution)/shard_map/ppermute | solution.py:376
  69.4 0.0 collective-permute-done.below_ref
  69.4 4.4 %collective-permute-done.1.above_ref = f32[17,8,256]{2,1,0:T(8,128)S(1)} collective-permute-done((f32[17,8,256]{2,1,0:T(8,128)S(1)}, f32[17,8,256]{2,1,0:T(8,128)S(1)}, u32[]{:S(2)}, u32[]{:S(2)}) %collective-permute-start.1) | collective-permute-done | bytes 139296 | tf_op jit(solution)/shard_map/ppermute | solution.py:376
  73.7 0.0 copy-done
  73.7 2.2 %inverse.1 = f32[32,40,128]{2,1,0:T(8,128)S(1)} custom-call(f32[680,512]{1,0:T(8,128)S(1)} %get-tuple-element.6.spec_ref, f32[17,8,256]{2,1,0:T(8,128)S(1)} %collective-permute-done.below_ref, f32[17,8,256]{2,1,0:T(8,128)S(1)} %collective-permute-done.1.above_ref, f32[2,512,512]{2,1,0:T(8,128)S(1)} %copy-done, f32[34,256]{1,0:T(8,128)S(1)} %copy-done.3, ...), custom_call_target="tpu_custom_call" | custom-call | tf_op jit(solution)/shard_map/inverse/pallas_call | solution.py:345
  75.9 57.2 %all_to_all.10.in_ref = f32[32,40,128]{2,1,0:T(8,128)S(1)} all-to-all(f32[32,40,128]{2,1,0:T(8,128)S(1)} %inverse.1), channel_id=1, replica_groups=mesh['lon'=32,'lat'=16] {'lon'}, dimensions={0} | all-to-all | bytes 1310720 | tf_op jit(solution)/shard_map/all_to_all | solution.py:377
  133.1 0.2 unpack.1
  133.4 0.8 copy.19
  134.1 0.8 copy.20
  134.9 0.8 copy.21
  (2 shorter events, 0.0 us)
Async XLA Ops:
  0.6 59.9 %copy-start.2 = (f32[51,256]{1,0:T(8,128)S(1)}, f32[51,256]{1,0:T(8,128)}, u32[]{:S(2)}) copy-start(f32[51,256]{1,0:T(8,128)} %constant.38.clone.wave_ref) | copy-start | bytes 156676
  0.6 59.9 %copy-start.3 = (f32[34,256]{1,0:T(8,128)S(1)}, f32[34,256]{1,0:T(8,128)}, u32[]{:S(2)}) copy-start(f32[34,256]{1,0:T(8,128)} %constant.37.clone.twiddle_ref) | copy-start | bytes 104452
  4.6 69.2 %copy-start = (f32[2,512,512]{2,1,0:T(8,128)S(1)}, f32[2,512,512]{2,1,0:T(8,128)}, u32[]{:S(2)}) copy-start(f32[2,512,512]{2,1,0:T(8,128)} %constant.39.clone.table_ref) | copy-start | bytes 6291460
  4.6 56.0 %all-to-all-start = ((f32[32,40,128]{2,1,0:T(8,128)}), f32[32,40,128]{2,1,0:T(8,128)S(1)}, u32[]{:S(2)}, u32[]{:S(2)}) async-start(f32[32,40,128]{2,1,0:T(8,128)} %pack.1), calls=%async_computation | async-start | bytes 1310720 | tf_op jit(solution)/shard_map/all_to_all | solution.py:373
  60.6 1.6 %copy-start.1 = (f32[2,512,512]{2,1,0:T(8,128)S(1)}, f32[2,512,512]{2,1,0:T(8,128)}, u32[]{:S(2)}) copy-start(f32[2,512,512]{2,1,0:T(8,128)} %constant.36.clone.table_ref) | copy-start | bytes 6291460
  65.0 4.4 %collective-permute-start = (f32[17,8,256]{2,1,0:T(8,128)S(1)}, f32[17,8,256]{2,1,0:T(8,128)S(1)}, u32[]{:S(2)}, u32[]{:S(2)}) collective-permute-start(f32[17,8,256]{2,1,0:T(8,128)S(1)} %get-tuple-element.7), channel_id=1, source_target_pairs={{0,16},{16,32},{32,48},{48,64},{64,80},{80,96},{96,112},{112,128},... | collective-permute-start | bytes 417800 | tf_op jit(solution)/shard_map/ppermute | solution.py:375
  67.4 6.4 %collective-permute-start.1 = (f32[17,8,256]{2,1,0:T(8,128)S(1)}, f32[17,8,256]{2,1,0:T(8,128)S(1)}, u32[]{:S(2)}, u32[]{:S(2)}) collective-permute-start(f32[17,8,256]{2,1,0:T(8,128)S(1)} %get-tuple-element.8), channel_id=1, source_target_pairs={{16,0},{32,16},{48,32},{64,48},{80,64},{96,80},{112,96},{128,112},... | collective-permute-start | bytes 417800 | tf_op jit(solution)/shard_map/ppermute | solution.py:376

commit v2 on v1

--- a/solution.py
+++ b/solution.py
@@ -22,41 +22,33 @@
 WAVES = PARTS // 2 + 1
 WIDE = 2 * LANES
 SCALE = 1.0 / NLON
-CHUNK = 5 * ROWS
-
-
-def places(variant):
+CHUNK = 4 * ROWS + ROWS // 2
+
+
+def places(half):
     b = np.arange(SEG)
-    return np.where(b < LANES, b, b + variant * HALF)
-
-
-def dft_tables():
+    return np.where(b < LANES, b, b + half * HALF)
+
+
+def dft_table():
     b = np.arange(SEG)
     angle = (np.outer(b, b) % SEG) * (2.0 * math.pi / SEG)
     cos, sin = np.cos(angle), np.sin(angle)
-    forward, inverse = [], []
-    for variant in (0, 1):
-        at = places(variant)
-        table = np.zeros((2 * WIDE, 2 * WIDE))
+    table = np.zeros((2 * WIDE, 2 * WIDE))
+    for half in (0, 1):
+        at = places(half)
         table[np.ix_(at, b)] = cos
         table[np.ix_(at, WIDE + b)] = -sin
         table[np.ix_(WIDE + at, b)] = sin
         table[np.ix_(WIDE + at, WIDE + b)] = cos
-        forward.append(table)
-        table = np.zeros((2 * WIDE, 2 * WIDE))
-        table[np.ix_(b, at)] = cos
-        table[np.ix_(b, WIDE + at)] = sin
-        table[np.ix_(WIDE + b, at)] = -sin
-        table[np.ix_(WIDE + b, WIDE + at)] = cos
-        inverse.append(table)
-    return np.stack(forward).astype(np.float32), np.stack(inverse).astype(np.float32)
+    return table.astype(np.float32)
 
 
 def twiddle_table():
     angle = np.zeros((WAVES, WIDE))
     turn = np.outer(np.arange(WAVES), np.arange(SEG)) * (2.0 * math.pi / NLON)
-    for variant in (0, 1):
-        angle[:, places(variant)] = turn
+    for half in (0, 1):
+        angle[:, places(half)] = turn
     return np.concatenate([np.cos(angle), np.sin(angle)]).astype(np.float32)
 
 
@@ -149,34 +141,61 @@
     return out
 
 
-def pack_kernel(u_ref, v_ref, h_ref, out_ref, tail_ref):
+def first_half(shape):
+    return lax.broadcasted_iota(jnp.int32, shape, 1) < HALF
+
+
+def spot(level, r, turned):
+    return CHUNK * (level * 16 + (15 - r if turned else r))
+
+
+def pack_kernel(turn_ref, u_ref, v_ref, h_ref, out_ref, tail_ref):
     tail_ref[...] = jnp.zeros_like(tail_ref)
     for level in range(2):
-        span = slice(level * 16, level * 16 + 16)
-        for f, ref in enumerate((u_ref, v_ref, h_ref)):
-            out_ref[span, f * ROWS : (f + 1) * ROWS, :] = ref[level, :LANES, :].T.reshape(16, ROWS, LANES)
-        for f, pair in ((3, (u_ref, v_ref)), (4, (h_ref, h_ref))):
+        tiles = [ref[pl.ds(level, LANES, 2), :].T for ref in (u_ref, v_ref, h_ref)]
+        for pair in ((u_ref, v_ref), (h_ref, h_ref)):
             for half, ref in enumerate(pair):
-                tail_ref[half * HALF : half * HALF + TAIL, :] = ref[level, LANES:, :]
-            out_ref[span, f * ROWS : (f + 1) * ROWS, :] = tail_ref[...].T.reshape(16, ROWS, LANES)
-
-
-def unpack_kernel(in_ref, u_ref, v_ref, h_ref, u_out, v_out, h_out):
+                tail_ref[half * HALF : half * HALF + TAIL, :] = ref[pl.ds(2 * LANES + level, TAIL, 2), :]
+            tiles.append(tail_ref[...].T)
+        for turned in (False, True):
+
+            @pl.when(turn_ref[0] == int(turned))
+            def _():
+                for r in range(16):
+                    at = spot(level, r, turned)
+                    for f in range(4):
+                        out_ref[at + f * ROWS : at + (f + 1) * ROWS, :] = tiles[f][r * ROWS : (r + 1) * ROWS]
+                    low, high = tiles[4][r * ROWS : r * ROWS + 4], tiles[4][r * ROWS + 4 : (r + 1) * ROWS]
+                    out_ref[at + 4 * ROWS : at + CHUNK, :] = jnp.where(first_half(low.shape), low, high)
+
+
+def unpack_kernel(turn_ref, in_ref, u_ref, v_ref, h_ref, u_out, v_out, h_out, tile_ref):
     for level in range(2):
-        span = slice(level * 16, level * 16 + 16)
-
-        def back(f):
-            return in_ref[span, f * ROWS : (f + 1) * ROWS, :].reshape(LANES, LANES).T
-
-        tails = (back(3), back(4))
+        for turned in (False, True):
+
+            @pl.when(turn_ref[0] == int(turned))
+            def _():
+                for r in range(16):
+                    at = spot(level, r, turned)
+                    for f in range(4):
+                        tile_ref[f, r * ROWS : (r + 1) * ROWS, :] = in_ref[at + f * ROWS : at + (f + 1) * ROWS, :]
+                    tail = in_ref[at + 4 * ROWS : at + CHUNK, :]
+                    tile_ref[4, r * ROWS : (r + 1) * ROWS, :] = jnp.concatenate([tail, tail], axis=0)
+
+        tails = tile_ref[3].T, tile_ref[4].T
+        early = lax.broadcasted_iota(jnp.int32, (TAIL, LANES), 1) % ROWS < ROWS // 2
+        tails = (tails[0][:TAIL], tails[0][HALF : HALF + TAIL], jnp.where(early, tails[1][:TAIL], tails[1][HALF : HALF + TAIL]))
         for f, (ref, out) in enumerate(((u_ref, u_out), (v_ref, v_out), (h_ref, h_out))):
-            out[level, :LANES, :] = ref[level, :LANES, :] + back(f)
-            half = HALF * (f == 1)
-            out[level, LANES:, :] = ref[level, LANES:, :] + tails[f // 2][half : half + TAIL]
-
-
-def dot(x, y):
-    return jnp.dot(x, y, precision=HIGH, preferred_element_type=jnp.float32)
+            here = pl.ds(level, LANES, 2)
+            out[here, :] = ref[here, :] + tile_ref[f].T
+            here = pl.ds(2 * LANES + level, TAIL, 2)
+            out[here, :] = ref[here, :] + tails[f]
+
+
+def dot(x, y, contract):
+    return lax.dot_general(
+        x, y, (((1,), (contract,)), ((), ())), precision=HIGH, preferred_element_type=jnp.float32
+    )
 
 
 H, U, UH, V, VH = range(5)
@@ -185,7 +204,14 @@
 
 def forward_kernel(x_ref, table_ref, twiddle_ref, wave_ref, row_ref, spec_ref, up_ref, down_ref, left_ref):
     def tile(a, f):
-        return x_ref[a, f * ROWS : (f + 1) * ROWS, :]
+        at = a * CHUNK + f * ROWS
+        return x_ref[at : at + ROWS, :]
+
+    def tail(a):
+        here = x_ref[a * CHUNK + 4 * ROWS : (a + 1) * CHUNK, :]
+        there = pltpu.roll(here, HALF, 1)
+        first = first_half(here.shape)
+        return jnp.concatenate([jnp.where(first, here, there), jnp.where(first, there, here)], axis=0)
 
     def product(f, g):
         return lambda a: tile(a, f) * tile(a, g)
@@ -197,9 +223,10 @@
         (product(0, 2), 0, (UH,)),
         (product(1, 2), 0, (VH,)),
         (lambda a: tile(a, 3), 1, (U, V)),
-        (lambda a: tile(a, 4), 1, (H,)),
-        (product(3, 4), 1, (UH, VH)),
+        (tail, 1, (H,)),
+        (lambda a: tile(a, 3) * tail(a), 1, (UH, VH)),
     )
+    first = first_half((ROWS, LANES))
     for get, part, fields in columns:
         lanes = slice(part * LANES, (part + 1) * LANES)
         late = slice(WIDE + part * LANES, WIDE + (part + 1) * LANES)
@@ -212,10 +239,13 @@
                 new_re, new_im = re * cos + im * sin, im * cos - re * sin
             for f in fields:
                 rows = slice(f * BLOCK + k1 * ROWS, f * BLOCK + (k1 + 1) * ROWS)
-                left_ref[rows, lanes] = new_re
-                left_ref[rows, late] = new_im
-    spec_ref[: V * BLOCK, :] = dot(left_ref[: V * BLOCK, :], table_ref[0])
-    spec_ref[V * BLOCK :, :] = dot(left_ref[V * BLOCK :, :], table_ref[1])
+                if part == 0:
+                    left_ref[rows, lanes], left_ref[rows, late] = new_re, new_im
+                else:
+                    mine = jnp.logical_not(first) if f >= V else first
+                    left_ref[rows, lanes] = jnp.where(mine, new_re, 0.0)
+                    left_ref[rows, late] = jnp.where(mine, new_im, 0.0)
+    spec_ref[...] = dot(left_ref[...], table_ref[...], 0)
 
     row = row_ref[0]
     ratio2, x_coef, coslat = row[:, 0:1], row[:, 1:2], row[:, 4:5]
@@ -278,8 +308,8 @@
         across = x_coef * slope
         left_ref[rows(1), spans[0]] = damp * (across * mass[1] + rotation * spec_ref[rows(V), spans[0]])
         left_ref[rows(1), spans[1]] = damp * (rotation * spec_ref[rows(V), spans[1]] - across * mass[0])
-    right_ref[: 2 * BLOCK, :] = dot(left_ref[: 2 * BLOCK, :], table_ref[0])
-    right_ref[2 * BLOCK :, :] = dot(left_ref[2 * BLOCK :, :], table_ref[1])
+    right_ref[...] = dot(left_ref[...], table_ref[...], 1)
+    first = first_half((ROWS, LANES))
     for f, part, fields in ((0, 0, (1,)), (1, 0, (2,)), (2, 0, (0,)), (3, 1, (1, 2)), (4, 1, (0,))):
         lanes = slice(part * LANES, (part + 1) * LANES)
         late = slice(WIDE + part * LANES, WIDE + (part + 1) * LANES)
@@ -288,11 +318,17 @@
             cos = twiddle_ref[k1 : k1 + 1, lanes]
             sin = twiddle_ref[WAVES + k1 : WAVES + k1 + 1, lanes]
             spots = [slice(g * BLOCK + k1 * ROWS, g * BLOCK + (k1 + 1) * ROWS) for g in fields]
-            re = functools.reduce(lambda x, y: x + y, [right_ref[s, lanes] for s in spots])
-            im = functools.reduce(lambda x, y: x + y, [right_ref[s, late] for s in spots])
+            re, im = right_ref[spots[0], lanes], right_ref[spots[0], late]
+            if len(spots) == 2:
+                re = jnp.where(first, re, right_ref[spots[1], lanes])
+                im = jnp.where(first, im, right_ref[spots[1], late])
             waves.append((re * cos - im * sin, None if k1 in (0, WAVES - 1) else im * cos + re * sin))
         for a, value in enumerate(real_ifft(waves)):
-            out_ref[a, f * ROWS : (f + 1) * ROWS, :] = value
+            at = a * CHUNK + f * ROWS
+            if f == 4:
+                half = ROWS // 2
+                value = jnp.where(first_half((half, LANES)), value[:half], value[half:])
+            out_ref[at : at + value.shape[0], :] = value
 
 
 def in_vmem():
@@ -306,27 +342,33 @@
     return jax.ShapeDtypeStruct(shape, jnp.float32)
 
 
+def place(level, r, lat):
+    return (level * 16 + (15 - r if lat % 2 else r)) * 16 + lat
+
+
 def neighbour_pairs(up):
     pairs = []
-    for lat in range(16):
-        for level in range(2):
-            for r in range(15):
-                pairs.append(((level * 16 + r) * 16 + lat, (level * 16 + r + 1) * 16 + lat))
-            if lat < 15:
-                pairs.append(((level * 16 + 15) * 16 + lat, level * 16 * 16 + lat + 1))
+    for level in range(2):
+        for lat in range(16):
+            pairs += [(place(level, r, lat), place(level, r + 1, lat)) for r in range(15)]
+        pairs += [(place(level, 15, lat), place(level, 0, lat + 1)) for lat in range(15)]
     return pairs if up else [(b, a) for a, b in pairs]
 
 
-def pack(u, v, h):
+def in_smem():
+    return pl.BlockSpec(memory_space=pltpu.SMEM)
+
+
+def pack(turned, u, v, h):
     return pl.pallas_call(
         pack_kernel,
-        out_shape=like(PARTS, CHUNK, LANES),
-        in_specs=[in_vmem()] * 3,
+        out_shape=like(PARTS * CHUNK, LANES),
+        in_specs=[in_smem()] + [in_vmem()] * 3,
         out_specs=in_vmem(),
         scratch_shapes=[pltpu.VMEM((LANES, LANES), jnp.float32)],
         compiler_params=PARAMS,
         name="pack",
-    )(u, v, h)
+    )(turned, u, v, h)
 
 
 def forward(whole, row):
@@ -338,44 +380,54 @@
         scratch_shapes=[pltpu.VMEM((5 * BLOCK, 2 * WIDE), jnp.float32)],
         compiler_params=PARAMS,
         name="forward",
-    )(whole, dft_tables()[0], twiddle_table(), wave_table(), row)
+    )(whole, dft_table(), twiddle_table(), wave_table(), row)
 
 
 def inverse(spec, below, above, row):
     return pl.pallas_call(
         inverse_kernel,
-        out_shape=like(PARTS, CHUNK, LANES),
+        out_shape=like(PARTS * CHUNK, LANES),
         in_specs=[in_vmem()] * 7,
         out_specs=in_vmem(),
         scratch_shapes=[pltpu.VMEM((3 * BLOCK, 2 * WIDE), jnp.float32)] * 2,
         compiler_params=PARAMS,
         name="inverse",
-    )(spec, below, above, dft_tables()[1], twiddle_table(), wave_table(), row)
-
-
-def unpack(back, u, v, h):
+    )(spec, below, above, dft_table(), twiddle_table(), wave_table(), row)
+
+
+def unpack(turned, back, u, v, h):
     return pl.pallas_call(
         unpack_kernel,
-        out_shape=(like(2, SEG, LANES),) * 3,
-        in_specs=[in_vmem()] * 4,
+        out_shape=(like(2 * SEG, LANES),) * 3,
+        in_specs=[in_smem()] + [in_vmem()] * 4,
         out_specs=(in_vmem(),) * 3,
+        scratch_shapes=[pltpu.VMEM((5, LANES, LANES), jnp.float32)],
         compiler_params=PARAMS,
         name="unpack",
-    )(back, u, v, h)
+    )(turned, back, u, v, h)
 
 
 def row_of(group):
     return lax.dynamic_slice_in_dim(jnp.asarray(row_table()), group, 1, axis=0)
 
 
+def exchange(chunks):
+    moved = lax.all_to_all(chunks.reshape(PARTS, CHUNK, 1, LANES), "lon", 0, 0, tiled=True)
+    return moved.reshape(PARTS * CHUNK, LANES)
+
+
 def step(u, v, h):
-    row = row_of(lax.axis_index("lat") * 16 + lax.axis_index("lon") % 16)
-    whole = lax.all_to_all(pack(u, v, h), "lon", 0, 0, tiled=True)
-    spec, up, down = forward(whole, row)
+    lat = lax.axis_index("lat")
+    turned = lat % 2
+    r = lax.axis_index("lon") % 16
+    row = row_of(lat * 16 + jnp.where(turned == 1, 15 - r, r))
+    turned = turned.reshape(1)
+    u, v, h = (jnp.swapaxes(x, 0, 1).reshape(2 * SEG, LANES) for x in (u, v, h))
+    spec, up, down = forward(exchange(pack(turned, u, v, h)), row)
     below = lax.ppermute(up, ("lon", "lat"), neighbour_pairs(True))
     above = lax.ppermute(down, ("lon", "lat"), neighbour_pairs(False))
-    back = lax.all_to_all(inverse(spec, below, above, row), "lon", 0, 0, tiled=True)
-    return unpack(back, u, v, h)
+    outs = unpack(turned, exchange(inverse(spec, below, above, row)), u, v, h)
+    return tuple(jnp.swapaxes(x.reshape(SEG, 2, LANES), 0, 1) for x in outs)
 
 
 def solution(mesh):

time: 137 us -> 115 us (0.84)
  blocking collectives: 57.2 us -> 41.5 us
  local copies, waits for them, and re-layouts: 7.45 us -> 3.57 us
  waiting for transfers between devices: 42.8 us -> 39.8 us
    all_to_all x1, blocking collectives: 57.2 us -> 41.5 us  [exchange(): lax.all_to_all(chunks.reshape(PARTS, CHUNK, 1, LANES), 'lon', 0, 0, tiled...]
    all_to_all x1, waiting for transfers between devices: 38.4 us -> 35.6 us  [exchange(): lax.all_to_all(chunks.reshape(PARTS, CHUNK, 1, LANES), 'lon', 0, 0, tiled...]
    pallas_call x3 -> x0, local copies, waits for them, and re-layouts: 2.3 us -> none  [unpack(): pl.pallas_call(unpack_kernel, out_shape=(like(2, SEG, LANES),) * 3, in_sp...]
    unnamed x11 -> x18, local copies, waits for them, and re-layouts: 4.45 us -> 2.87 us
where the time goes in v2:
time: 115 us; the launch traced here: 114 us
  blocking collectives  41.5 us (36%)
  waiting for transfers between devices  39.8 us (35%)
  starting transfers between devices  21.1 us (18%)
  Pallas kernels  7.23 us (6%)
  local copies, waits for them, and re-layouts  3.57 us (3%)
    all_to_all x1, blocking collectives, exchange(): lax.all_to_all(chunks.reshape(PARTS, CHUNK, 1, LANES), 'lon', 0, 0, tiled...  41.5 us
    all_to_all x1, waiting for transfers between devices, exchange(): lax.all_to_all(chunks.reshape(PARTS, CHUNK, 1, LANES), 'lon', 0, 0, tiled...  35.6 us
    all_to_all x1, starting transfers between devices, exchange(): lax.all_to_all(chunks.reshape(PARTS, CHUNK, 1, LANES), 'lon', 0, 0, tiled...  16.8 us
    ppermute x1, waiting for transfers between devices, step(): above = lax.ppermute(down, ('lon', 'lat'), neighbour_pairs(False))  4.26 us
    unnamed x18, local copies, waits for them, and re-layouts  2.87 us
    pallas_call x1, Pallas kernels, forward(): pl.pallas_call(forward_kernel, out_shape=(like(5 * BLOCK, 2 * WIDE), like...  2.84 us
  transfers between devices with their start and end apart: 3, of which 2 were waited for; matrix products, arithmetic and copies ran while one was open for 1% of the time, Pallas kernels for 0%

profile of v2, /device:TPU:1, one launch (start us, length us, event | category | flops | bytes accessed | tf_op | source)
XLA Modules:
  0.0 114.0 jit_solution(12232428702728494598)
XLA Ops:
  0.6 0.0 copy-start
  0.7 0.0 copy-start.1
  0.7 1.0 copy-done.1
  1.7 0.0 copy-start.3
  1.7 0.9 copy-done.3
  2.6 0.9 copy-done.5
  3.5 1.2 %pack.1 = f32[1152,128]{1,0:T(8,128)} custom-call(s32[1]{0:T(128)} %bitcast.turn_ref, f32[360,128]{1,0:T(8,128)S(1)} %bitcast.26, f32[360,128]{1,0:T(8,128)S(1)} %bitcast.28, f32[360,128]{1,0:T(8,128)S(1)} %bitcast.30), custom_call_target="tpu_custom_call" | custom-call | tf_op jit(solution)/shard_map/pack/pallas_call | solution.py:363
  4.7 16.8 %all-to-all-start = ((f32[32,36,1,128]{3,2,1,0:T(1,128)}), f32[32,36,1,128]{3,2,1,0:T(1,128)S(1)}, u32[]{:S(2)}, u32[]{:S(2)}) async-start(f32[32,36,1,128]{3,2,1,0:T(1,128)} %bitcast.7), calls=%async_computation | async-start | bytes 1179648 | tf_op jit(solution)/shard_map/all_to_all | solution.py:415
  21.5 0.7 constant_dynamic-slice_fusion.row_ref
  22.2 35.6 %all-to-all-done = f32[32,36,1,128]{3,2,1,0:T(1,128)S(1)} async-done(((f32[32,36,1,128]{3,2,1,0:T(1,128)}), f32[32,36,1,128]{3,2,1,0:T(1,128)S(1)}, u32[]{:S(2)}, u32[]{:S(2)}) %all-to-all-start) | async-done | bytes 589856 | tf_op jit(solution)/shard_map/all_to_all | solution.py:415
  57.8 0.0 copy-done
  57.8 0.0 copy-done.7
  57.8 0.0 copy-done.8
  57.8 2.8 %forward.1 = (f32[680,512]{1,0:T(8,128)S(1)}, f32[17,8,256]{2,1,0:T(8,128)S(1)}, f32[17,8,256]{2,1,0:T(8,128)S(1)}) custom-call(f32[1152,128]{1,0:T(8,128)S(1)} %bitcast.23, f32[512,512]{1,0:T(8,128)S(1)} %copy-done, f32[34,256]{1,0:T(8,128)S(1)} %copy-done.8, f32[51,256]{1,0:T(8,128)S(1)} %copy-done.7, f32[1,8,128]{2,1,0:T(8,128)S(1)} %constant_dynamic-slice_fusion.row_ref), custom_call_target="tpu_custom_call" | custom-call | tf_op jit(solution)/shard_map/forward/pallas_call | solution.py:375
  60.6 2.2 %collective-permute-start = (f32[17,8,256]{2,1,0:T(8,128)S(1)}, f32[17,8,256]{2,1,0:T(8,128)S(1)}, u32[]{:S(2)}, u32[]{:S(2)}) collective-permute-start(f32[17,8,256]{2,1,0:T(8,128)S(1)} %get-tuple-element.10), channel_id=1, source_target_pairs={{0,16},{16,32},{32,48},{48,64},{64,80},{80,96},{96,112},{112,128},... | collective-permute-start | bytes 417800 | tf_op jit(solution)/shard_map/ppermute | solution.py:427
  62.9 2.1 %collective-permute-start.1 = (f32[17,8,256]{2,1,0:T(8,128)S(1)}, f32[17,8,256]{2,1,0:T(8,128)S(1)}, u32[]{:S(2)}, u32[]{:S(2)}) collective-permute-start(f32[17,8,256]{2,1,0:T(8,128)S(1)} %get-tuple-element.11), channel_id=1, source_target_pairs={{16,0},{32,16},{48,32},{64,48},{80,64},{96,80},{112,96},{128,112},... | collective-permute-start | bytes 417800 | tf_op jit(solution)/shard_map/ppermute | solution.py:428
  65.0 0.0 collective-permute-done.below_ref
  65.0 4.3 %collective-permute-done.1.above_ref = f32[17,8,256]{2,1,0:T(8,128)S(1)} collective-permute-done((f32[17,8,256]{2,1,0:T(8,128)S(1)}, f32[17,8,256]{2,1,0:T(8,128)S(1)}, u32[]{:S(2)}, u32[]{:S(2)}) %collective-permute-start.1) | collective-permute-done | bytes 139296 | tf_op jit(solution)/shard_map/ppermute | solution.py:428
  69.2 2.0 %inverse.1 = f32[1152,128]{1,0:T(8,128)S(1)} custom-call(f32[680,512]{1,0:T(8,128)S(1)} %get-tuple-element.9.spec_ref, f32[17,8,256]{2,1,0:T(8,128)S(1)} %collective-permute-done.below_ref, f32[17,8,256]{2,1,0:T(8,128)S(1)} %collective-permute-done.1.above_ref, f32[512,512]{1,0:T(8,128)S(1)} %copy-done, f32[34,256]{1,0:T(8,128)S(1)} %copy-done.8, ...), custom_call_target="tpu_custom_call" | custom-call | tf_op jit(solution)/shard_map/inverse/pallas_call | solution.py:387
  71.3 41.5 %all_to_all.10 = f32[32,36,1,128]{3,2,1,0:T(1,128)S(1)} all-to-all(f32[32,36,1,128]{3,2,1,0:T(1,128)S(1)} %bitcast.25), channel_id=1, replica_groups=mesh['lon'=32,'lat'=16] {'lon'}, dimensions={0} | all-to-all | bytes 1179648 | tf_op jit(solution)/shard_map/all_to_all | solution.py:415
  112.8 0.0 copy-done.2
  112.8 0.0 copy-done.4
  112.8 0.0 copy-done.6
  112.8 1.1 %unpack.1 = (f32[360,128]{1,0:T(8,128)}, f32[360,128]{1,0:T(8,128)}, f32[360,128]{1,0:T(8,128)}) custom-call(s32[1]{0:T(128)} %bitcast.turn_ref, f32[1152,128]{1,0:T(8,128)S(1)} %bitcast.24, f32[360,128]{1,0:T(8,128)S(1)} %bitcast.27, f32[360,128]{1,0:T(8,128)S(1)} %bitcast.29, f32[360,128]{1,0:T(8,128)S(1)} %bitcast.31), custom_call_target="tpu_custom_call" | custom-call | tf_op jit(solution)/shard_map/unpack/pallas_call | solution.py:399
  (6 shorter events, 0.0 us)
Async XLA Ops:
  0.6 57.1 %copy-start = (f32[512,512]{1,0:T(8,128)S(1)}, f32[512,512]{1,0:T(8,128)}, u32[]{:S(2)}) copy-start(f32[512,512]{1,0:T(8,128)} %constant.46.clone.table_ref) | copy-start | bytes 3145732
  0.7 1.0 copy-start.1
  1.7 0.9 copy-start.3
  2.6 0.9 copy-start.5
  3.5 54.2 %copy-start.7 = (f32[51,256]{1,0:T(8,128)S(1)}, f32[51,256]{1,0:T(8,128)}, u32[]{:S(2)}) copy-start(f32[51,256]{1,0:T(8,128)} %constant.48.clone.wave_ref) | copy-start | bytes 156676
  3.5 54.2 %copy-start.8 = (f32[34,256]{1,0:T(8,128)S(1)}, f32[34,256]{1,0:T(8,128)}, u32[]{:S(2)}) copy-start(f32[34,256]{1,0:T(8,128)} %constant.47.clone.twiddle_ref) | copy-start | bytes 104452
  4.7 53.0 %all-to-all-start = ((f32[32,36,1,128]{3,2,1,0:T(1,128)}), f32[32,36,1,128]{3,2,1,0:T(1,128)S(1)}, u32[]{:S(2)}, u32[]{:S(2)}) async-start(f32[32,36,1,128]{3,2,1,0:T(1,128)} %bitcast.7), calls=%async_computation | async-start | bytes 1179648 | tf_op jit(solution)/shard_map/all_to_all | solution.py:415
  60.6 4.3 %collective-permute-start = (f32[17,8,256]{2,1,0:T(8,128)S(1)}, f32[17,8,256]{2,1,0:T(8,128)S(1)}, u32[]{:S(2)}, u32[]{:S(2)}) collective-permute-start(f32[17,8,256]{2,1,0:T(8,128)S(1)} %get-tuple-element.10), channel_id=1, source_target_pairs={{0,16},{16,32},{32,48},{48,64},{64,80},{80,96},{96,112},{112,128},... | collective-permute-start | bytes 417800 | tf_op jit(solution)/shard_map/ppermute | solution.py:427
  62.9 6.4 %collective-permute-start.1 = (f32[17,8,256]{2,1,0:T(8,128)S(1)}, f32[17,8,256]{2,1,0:T(8,128)S(1)}, u32[]{:S(2)}, u32[]{:S(2)}) collective-permute-start(f32[17,8,256]{2,1,0:T(8,128)S(1)} %get-tuple-element.11), channel_id=1, source_target_pairs={{16,0},{32,16},{48,32},{64,48},{80,64},{96,80},{112,96},{128,112},... | collective-permute-start | bytes 417800 | tf_op jit(solution)/shard_map/ppermute | solution.py:428
  69.2 43.6 %copy-start.2 = (f32[2,180,128]{2,0,1:T(2,128)S(1)}, f32[2,180,128]{2,0,1:T(2,128)}, u32[]{:S(2)}) copy-start(f32[2,180,128]{2,0,1:T(2,128)} %param.10) | copy-start | bytes 552964
  69.2 43.6 %copy-start.4 = (f32[2,180,128]{2,0,1:T(2,128)S(1)}, f32[2,180,128]{2,0,1:T(2,128)}, u32[]{:S(2)}) copy-start(f32[2,180,128]{2,0,1:T(2,128)} %param.11) | copy-start | bytes 552964
  69.2 43.6 %copy-start.6 = (f32[2,180,128]{2,0,1:T(2,128)S(1)}, f32[2,180,128]{2,0,1:T(2,128)}, u32[]{:S(2)}) copy-start(f32[2,180,128]{2,0,1:T(2,128)} %param.12) | copy-start | bytes 552964

commit v3 on v2

--- a/solution.py
+++ b/solution.py
@@ -8,8 +8,6 @@
 from jax.experimental import pallas as pl
 from jax.experimental.pallas import tpu as pltpu
 from jax.sharding import PartitionSpec as P
-
-HIGH = lax.Precision.HIGHEST
 
 NLON = 5760
 NLAT = 2048
@@ -149,8 +147,16 @@
     return CHUNK * (level * 16 + (15 - r if turned else r))
 
 
-def pack_kernel(turn_ref, u_ref, v_ref, h_ref, out_ref, tail_ref):
+def pack_kernel(turn_ref, u_hbm, v_hbm, h_hbm, out_ref, u_ref, v_ref, h_ref, tail_ref, sems):
+    moves = [
+        pltpu.make_async_copy(src, dst, sems.at[i])
+        for i, (src, dst) in enumerate(((u_hbm, u_ref), (v_hbm, v_ref), (h_hbm, h_ref)))
+    ]
+    for move in moves:
+        move.start()
     tail_ref[...] = jnp.zeros_like(tail_ref)
+    for move in moves:
+        move.wait()
     for level in range(2):
         tiles = [ref[pl.ds(level, LANES, 2), :].T for ref in (u_ref, v_ref, h_ref)]
         for pair in ((u_ref, v_ref), (h_ref, h_ref)):
@@ -192,61 +198,86 @@
             out[here, :] = ref[here, :] + tails[f]
 
 
-def dot(x, y, contract):
-    return lax.dot_general(
-        x, y, (((1,), (contract,)), ((), ())), precision=HIGH, preferred_element_type=jnp.float32
-    )
-
-
-H, U, UH, V, VH = range(5)
+def halves(x):
+    high = x.astype(jnp.bfloat16)
+    return high, (x - high.astype(jnp.float32)).astype(jnp.bfloat16)
+
+
+def dot(x, table, contract):
+    def product(a, b):
+        return lax.dot_general(a, b, (((1,), (contract,)), ((), ())), preferred_element_type=jnp.float32)
+
+    (high, low), (table_high, table_low) = halves(x), halves(table)
+    return product(high, table_high) + (product(high, table_low) + product(low, table_high))
+
+
 BLOCK = WAVES * ROWS
 
 
-def forward_kernel(x_ref, table_ref, twiddle_ref, wave_ref, row_ref, spec_ref, up_ref, down_ref, left_ref):
-    def tile(a, f):
-        at = a * CHUNK + f * ROWS
-        return x_ref[at : at + ROWS, :]
-
-    def tail(a):
-        here = x_ref[a * CHUNK + 4 * ROWS : (a + 1) * CHUNK, :]
-        there = pltpu.roll(here, HALF, 1)
-        first = first_half(here.shape)
-        return jnp.concatenate([jnp.where(first, here, there), jnp.where(first, there, here)], axis=0)
-
-    def product(f, g):
-        return lambda a: tile(a, f) * tile(a, g)
-
-    columns = (
-        (lambda a: tile(a, 0), 0, (U,)),
-        (lambda a: tile(a, 1), 0, (V,)),
-        (lambda a: tile(a, 2), 0, (H,)),
-        (product(0, 2), 0, (UH,)),
-        (product(1, 2), 0, (VH,)),
-        (lambda a: tile(a, 3), 1, (U, V)),
-        (tail, 1, (H,)),
-        (lambda a: tile(a, 3) * tail(a), 1, (UH, VH)),
-    )
+def padded(fields):
+    return -(-fields * BLOCK // 16) * 16
+
+
+def transform(x_ref, table_ref, twiddle_ref, spec_ref, left_ref, columns):
     first = first_half((ROWS, LANES))
     for get, part, fields in columns:
         lanes = slice(part * LANES, (part + 1) * LANES)
         late = slice(WIDE + part * LANES, WIDE + (part + 1) * LANES)
-        for k1, (re, im) in enumerate(real_fft([get(a) for a in range(PARTS)])):
+        for k1, (re, im) in enumerate(real_fft([get(x_ref, a) for a in range(PARTS)])):
             cos = twiddle_ref[k1 : k1 + 1, lanes]
             sin = twiddle_ref[WAVES + k1 : WAVES + k1 + 1, lanes]
             if im is None:
                 new_re, new_im = re * cos, -re * sin
             else:
                 new_re, new_im = re * cos + im * sin, im * cos - re * sin
-            for f in fields:
+            for f, half in fields:
                 rows = slice(f * BLOCK + k1 * ROWS, f * BLOCK + (k1 + 1) * ROWS)
                 if part == 0:
                     left_ref[rows, lanes], left_ref[rows, late] = new_re, new_im
                 else:
-                    mine = jnp.logical_not(first) if f >= V else first
+                    mine = jnp.logical_not(first) if half else first
                     left_ref[rows, lanes] = jnp.where(mine, new_re, 0.0)
                     left_ref[rows, late] = jnp.where(mine, new_im, 0.0)
     spec_ref[...] = dot(left_ref[...], table_ref[...], 0)
 
+
+def tile(f):
+    def get(x_ref, a):
+        at = a * CHUNK + f * ROWS
+        return x_ref[at : at + ROWS, :]
+
+    return get
+
+
+def tail(x_ref, a):
+    here = x_ref[a * CHUNK + 4 * ROWS : (a + 1) * CHUNK, :]
+    there = pltpu.roll(here, HALF, 1)
+    first = first_half(here.shape)
+    return jnp.concatenate([jnp.where(first, here, there), jnp.where(first, there, here)], axis=0)
+
+
+def times_h(get, h):
+    return lambda x_ref, a: get(x_ref, a) * h(x_ref, a)
+
+
+H, UH, VH = range(3)
+U, V = range(2)
+MASS_COLUMNS = (
+    (tile(2), 0, ((H, 0),)),
+    (times_h(tile(0), tile(2)), 0, ((UH, 0),)),
+    (times_h(tile(1), tile(2)), 0, ((VH, 0),)),
+    (tail, 1, ((H, 0),)),
+    (times_h(tile(3), tail), 1, ((UH, 0), (VH, 1))),
+)
+WIND_COLUMNS = ((tile(0), 0, ((U, 0),)), (tile(1), 0, ((V, 0),)), (tile(3), 1, ((U, 0), (V, 1))))
+
+
+def wind_kernel(x_ref, table_ref, twiddle_ref, spec_ref, left_ref):
+    transform(x_ref, table_ref, twiddle_ref, spec_ref, left_ref, WIND_COLUMNS)
+
+
+def mass_kernel(x_ref, table_ref, twiddle_ref, wave_ref, row_ref, spec_ref, up_ref, down_ref, left_ref):
+    transform(x_ref, table_ref, twiddle_ref, spec_ref, left_ref, MASS_COLUMNS)
     row = row_ref[0]
     ratio2, x_coef, coslat = row[:, 0:1], row[:, 1:2], row[:, 4:5]
     real, imag = slice(0, WIDE), slice(WIDE, 2 * WIDE)
@@ -274,7 +305,9 @@
         down_ref[k1] = jnp.concatenate([mass_re[0:1], mass_im[0:1], flux_re[0:2], flux_im[0:2], zeros], axis=0)
 
 
-def inverse_kernel(spec_ref, below_ref, above_ref, table_ref, twiddle_ref, wave_ref, row_ref, out_ref, left_ref, right_ref):
+def inverse_kernel(
+    spec_ref, wind_ref, below_ref, above_ref, table_ref, twiddle_ref, wave_ref, row_ref, out_ref, left_ref, right_ref
+):
     row = row_ref[0]
     ratio2, x_coef, y_coef, rotation = (row[:, i : i + 1] for i in range(4))
     y_below, y_above = row[0:1, 5:6], row[0:1, 6:7]
@@ -302,12 +335,12 @@
             mass.append(new)
             prev = jnp.concatenate([new_below, new[:-1]], axis=0)
             following = jnp.concatenate([new[1:], new_above], axis=0)
-            push = -PUSH_COEF * (following - prev) - rotation * spec_ref[rows(U), span]
+            push = -PUSH_COEF * (following - prev) - rotation * wind_ref[rows(U), span]
             left_ref[rows(2), span] = damp * push
             left_ref[rows(0), span] = SCALE * change
         across = x_coef * slope
-        left_ref[rows(1), spans[0]] = damp * (across * mass[1] + rotation * spec_ref[rows(V), spans[0]])
-        left_ref[rows(1), spans[1]] = damp * (rotation * spec_ref[rows(V), spans[1]] - across * mass[0])
+        left_ref[rows(1), spans[0]] = damp * (across * mass[1] + rotation * wind_ref[rows(V), spans[0]])
+        left_ref[rows(1), spans[1]] = damp * (rotation * wind_ref[rows(V), spans[1]] - across * mass[0])
     right_ref[...] = dot(left_ref[...], table_ref[...], 1)
     first = first_half((ROWS, LANES))
     for f, part, fields in ((0, 0, (1,)), (1, 0, (2,)), (2, 0, (0,)), (3, 1, (1, 2)), (4, 1, (0,))):
@@ -363,36 +396,57 @@
     return pl.pallas_call(
         pack_kernel,
         out_shape=like(PARTS * CHUNK, LANES),
-        in_specs=[in_smem()] + [in_vmem()] * 3,
+        in_specs=[in_smem()] + [pl.BlockSpec(memory_space=pltpu.HBM)] * 3,
         out_specs=in_vmem(),
-        scratch_shapes=[pltpu.VMEM((LANES, LANES), jnp.float32)],
-        compiler_params=PARAMS,
+        scratch_shapes=[pltpu.VMEM((2 * SEG, LANES), jnp.float32)] * 3
+        + [pltpu.VMEM((LANES, LANES), jnp.float32), pltpu.SemaphoreType.DMA((3,))],
+        compiler_params=pltpu.CompilerParams(vmem_limit_bytes=56 * 2**20),
         name="pack",
     )(turned, u, v, h)
 
 
-def forward(whole, row):
+def cost(fields):
+    size = padded(fields) * 2 * WIDE
+    return pl.CostEstimate(flops=6 * size * 2 * WIDE, bytes_accessed=8 * size, transcendentals=0)
+
+
+def forward_mass(whole, row):
     return pl.pallas_call(
-        forward_kernel,
-        out_shape=(like(5 * BLOCK, 2 * WIDE), like(WAVES, ROWS, WIDE), like(WAVES, ROWS, WIDE)),
+        mass_kernel,
+        out_shape=(like(padded(3), 2 * WIDE), like(WAVES, ROWS, WIDE), like(WAVES, ROWS, WIDE)),
         in_specs=[in_vmem()] * 5,
         out_specs=(in_vmem(),) * 3,
-        scratch_shapes=[pltpu.VMEM((5 * BLOCK, 2 * WIDE), jnp.float32)],
+        scratch_shapes=[pltpu.VMEM((padded(3), 2 * WIDE), jnp.float32)],
         compiler_params=PARAMS,
-        name="forward",
+        cost_estimate=cost(3),
+        name="forward_mass",
     )(whole, dft_table(), twiddle_table(), wave_table(), row)
 
 
-def inverse(spec, below, above, row):
+def forward_wind(whole):
+    return pl.pallas_call(
+        wind_kernel,
+        out_shape=like(padded(2), 2 * WIDE),
+        in_specs=[in_vmem()] * 3,
+        out_specs=in_vmem(),
+        scratch_shapes=[pltpu.VMEM((padded(2), 2 * WIDE), jnp.float32)],
+        compiler_params=PARAMS,
+        cost_estimate=cost(2),
+        name="forward_wind",
+    )(whole, dft_table(), twiddle_table())
+
+
+def inverse(spec, wind, below, above, row):
     return pl.pallas_call(
         inverse_kernel,
         out_shape=like(PARTS * CHUNK, LANES),
-        in_specs=[in_vmem()] * 7,
+        in_specs=[in_vmem()] * 8,
         out_specs=in_vmem(),
-        scratch_shapes=[pltpu.VMEM((3 * BLOCK, 2 * WIDE), jnp.float32)] * 2,
+        scratch_shapes=[pltpu.VMEM((padded(3), 2 * WIDE), jnp.float32)] * 2,
         compiler_params=PARAMS,
+        cost_estimate=cost(3),
         name="inverse",
-    )(spec, below, above, dft_table(), twiddle_table(), wave_table(), row)
+    )(spec, wind, below, above, dft_table(), twiddle_table(), wave_table(), row)
 
 
 def unpack(turned, back, u, v, h):
@@ -423,10 +477,12 @@
     row = row_of(lat * 16 + jnp.where(turned == 1, 15 - r, r))
     turned = turned.reshape(1)
     u, v, h = (jnp.swapaxes(x, 0, 1).reshape(2 * SEG, LANES) for x in (u, v, h))
-    spec, up, down = forward(exchange(pack(turned, u, v, h)), row)
+    whole = exchange(pack(turned, u, v, h))
+    spec, up, down = forward_mass(whole, row)
     below = lax.ppermute(up, ("lon", "lat"), neighbour_pairs(True))
     above = lax.ppermute(down, ("lon", "lat"), neighbour_pairs(False))
-    outs = unpack(turned, exchange(inverse(spec, below, above, row)), u, v, h)
+    wind = forward_wind(whole)
+    outs = unpack(turned, exchange(inverse(spec, wind, below, above, row)), u, v, h)
     return tuple(jnp.swapaxes(x.reshape(SEG, 2, LANES), 0, 1) for x in outs)
 
 

time: 115 us -> 112 us (0.974)
  local copies, waits for them, and re-layouts: 3.57 us -> 0.73 us
    unnamed x18 -> x12, local copies, waits for them, and re-layouts: 2.87 us -> 0.04 us
    pallas_call x1, Pallas kernels: 1.2 us -> 2.39 us  [pack(): pl.pallas_call(pack_kernel, out_shape=like(PARTS * CHUNK, LANES), in_spec...]
    pallas_call x1 -> x2, Pallas kernels: 2.84 us -> 1.92 us  [the longest x1 1.19 us: forward_mass(): pl.pallas_call(mass_kernel, out_shape=(like(padded(3), 2 * WIDE), like(WA...]
  transfers between devices with their start and end apart: 3 -> 3, of which waited for: 2 -> 2; matrix products, arithmetic and copies ran while one was open for 1% -> 1% of each run, Pallas kernels for 0% -> 1%
where the time goes in v3:
time: 112 us; the launch traced here: 110 us
  blocking collectives  41.7 us (37%)
  waiting for transfers between devices  39.1 us (35%)
  starting transfers between devices  21.2 us (19%)
  Pallas kernels  6.87 us (6%)
    all_to_all x1, blocking collectives, exchange(): lax.all_to_all(chunks.reshape(PARTS, CHUNK, 1, LANES), 'lon', 0, 0, tiled...  41.7 us
    all_to_all x1, waiting for transfers between devices, exchange(): lax.all_to_all(chunks.reshape(PARTS, CHUNK, 1, LANES), 'lon', 0, 0, tiled...  35.5 us
    all_to_all x1, starting transfers between devices, exchange(): lax.all_to_all(chunks.reshape(PARTS, CHUNK, 1, LANES), 'lon', 0, 0, tiled...  16.9 us
    ppermute x1, waiting for transfers between devices, step(): above = lax.ppermute(down, ('lon', 'lat'), neighbour_pairs(False))  3.52 us
    pallas_call x1, Pallas kernels, pack(): pl.pallas_call(pack_kernel, out_shape=like(PARTS * CHUNK, LANES), in_spec...  2.39 us
  transfers between devices with their start and end apart: 3, of which 2 were waited for; matrix products, arithmetic and copies ran while one was open for 1% of the time, Pallas kernels for 1%

profile of v3, /device:TPU:1, one launch (start us, length us, event | category | flops | bytes accessed | tf_op | source)
XLA Modules:
  0.0 110.3 jit_solution(13133300983469131640)
XLA Ops:
  0.6 0.0 copy-start
  0.7 2.4 %pack.1 = f32[1152,128]{1,0:T(8,128)} custom-call(s32[1]{0:T(128)} %bitcast.turn_ref, f32[360,128]{1,0:T(8,128)} %bitcast.27, f32[360,128]{1,0:T(8,128)} %bitcast.29, f32[360,128]{1,0:T(8,128)} %bitcast.31), custom_call_target="tpu_custom_call" | custom-call | tf_op jit(solution)/shard_map/pack/pallas_call | solution.py:396
  3.1 0.0 copy-start.5
  3.1 16.9 %all-to-all-start = ((f32[32,36,1,128]{3,2,1,0:T(1,128)}), f32[32,36,1,128]{3,2,1,0:T(1,128)S(1)}, u32[]{:S(2)}, u32[]{:S(2)}) async-start(f32[32,36,1,128]{3,2,1,0:T(1,128)} %bitcast.33), calls=%async_computation | async-start | bytes 1179648 | tf_op jit(solution)/shard_map/all_to_all | solution.py:469
  20.0 0.0 copy-start.4
  20.0 0.7 constant_dynamic-slice_fusion.row_ref
  20.7 35.5 %all-to-all-done = f32[32,36,1,128]{3,2,1,0:T(1,128)S(1)} async-done(((f32[32,36,1,128]{3,2,1,0:T(1,128)}), f32[32,36,1,128]{3,2,1,0:T(1,128)S(1)}, u32[]{:S(2)}, u32[]{:S(2)}) %all-to-all-start) | async-done | bytes 589856 | tf_op jit(solution)/shard_map/all_to_all | solution.py:469
  56.2 0.0 copy-done
  56.2 0.0 copy-done.5
  56.2 0.0 copy-done.4
  56.3 1.2 %forward_mass.1 = (f32[416,512]{1,0:T(8,128)S(1)}, f32[17,8,256]{2,1,0:T(8,128)S(1)}, f32[17,8,256]{2,1,0:T(8,128)S(1)}) custom-call(f32[1152,128]{1,0:T(8,128)S(1)} %bitcast.24, f32[512,512]{1,0:T(8,128)S(1)} %copy-done, f32[34,256]{1,0:T(8,128)S(1)} %copy-done.4, f32[51,256]{1,0:T(8,128)S(1)} %copy-done.5, f32[1,8,128]{2,1,0:T(8,128)S(1)} %constant_dynamic-slice_fusion.row_ref), custom_call_target="tpu_custom_call" | custom-call | flops 654311424 | bytes 1703936 | tf_op jit(solution)/shard_map/forward_mass/pallas_call | solution.py:414
  57.5 2.2 %collective-permute-start = (f32[17,8,256]{2,1,0:T(8,128)S(1)}, f32[17,8,256]{2,1,0:T(8,128)S(1)}, u32[]{:S(2)}, u32[]{:S(2)}) collective-permute-start(f32[17,8,256]{2,1,0:T(8,128)S(1)} %get-tuple-element.10), channel_id=1, source_target_pairs={{0,16},{16,32},{32,48},{48,64},{64,80},{80,96},{96,112},{112,128},... | collective-permute-start | bytes 417800 | tf_op jit(solution)/shard_map/ppermute | solution.py:482
  59.7 2.1 %collective-permute-start.1 = (f32[17,8,256]{2,1,0:T(8,128)S(1)}, f32[17,8,256]{2,1,0:T(8,128)S(1)}, u32[]{:S(2)}, u32[]{:S(2)}) collective-permute-start(f32[17,8,256]{2,1,0:T(8,128)S(1)} %get-tuple-element.11), channel_id=1, source_target_pairs={{16,0},{32,16},{48,32},{64,48},{80,64},{96,80},{112,96},{128,112},... | collective-permute-start | bytes 417800 | tf_op jit(solution)/shard_map/ppermute | solution.py:483
  61.8 0.7 forward_wind.1.wind_ref
  62.5 0.0 collective-permute-done.below_ref
  62.5 3.5 %collective-permute-done.1.above_ref = f32[17,8,256]{2,1,0:T(8,128)S(1)} collective-permute-done((f32[17,8,256]{2,1,0:T(8,128)S(1)}, f32[17,8,256]{2,1,0:T(8,128)S(1)}, u32[]{:S(2)}, u32[]{:S(2)}) %collective-permute-start.1) | collective-permute-done | bytes 139296 | tf_op jit(solution)/shard_map/ppermute | solution.py:483
  66.1 1.4 %inverse.1 = f32[1152,128]{1,0:T(8,128)S(1)} custom-call(f32[416,512]{1,0:T(8,128)S(1)} %get-tuple-element.9.spec_ref, f32[272,512]{1,0:T(8,128)S(1)} %forward_wind.1.wind_ref, f32[17,8,256]{2,1,0:T(8,128)S(1)} %collective-permute-done.below_ref, f32[17,8,256]{2,1,0:T(8,128)S(1)} %collective-permute-done.1.above_ref, f32[512,512]{1,0:T(8,128)S(1)} %copy-done, ...), custom_call_target="tpu_custom_call" | custom-call | flops 654311424 | bytes 1703936 | tf_op jit(solution)/shard_map/inverse/pallas_call | solution.py:440
  67.5 0.0 copy-start.1
  67.5 0.0 copy-start.2
  67.5 0.0 copy-start.3
  67.5 41.7 %all_to_all.10 = f32[32,36,1,128]{3,2,1,0:T(1,128)S(1)} all-to-all(f32[32,36,1,128]{3,2,1,0:T(1,128)S(1)} %bitcast.26), channel_id=1, replica_groups=mesh['lon'=32,'lat'=16] {'lon'}, dimensions={0} | all-to-all | bytes 1179648 | tf_op jit(solution)/shard_map/all_to_all | solution.py:469
  109.2 0.0 copy-done.1
  109.2 0.0 copy-done.3
  109.2 1.1 %unpack.1 = (f32[360,128]{1,0:T(8,128)}, f32[360,128]{1,0:T(8,128)}, f32[360,128]{1,0:T(8,128)}) custom-call(s32[1]{0:T(128)} %bitcast.turn_ref, f32[1152,128]{1,0:T(8,128)S(1)} %bitcast.23, f32[360,128]{1,0:T(8,128)S(1)} %bitcast.28, f32[360,128]{1,0:T(8,128)S(1)} %bitcast.30, f32[360,128]{1,0:T(8,128)S(1)} %bitcast.32), custom_call_target="tpu_custom_call" | custom-call | tf_op jit(solution)/shard_map/unpack/pallas_call | solution.py:453
  (1 shorter events, 0.0 us)
Async XLA Ops:
  0.6 55.6 %copy-start = (f32[512,512]{1,0:T(8,128)S(1)}, f32[512,512]{1,0:T(8,128)}, u32[]{:S(2)}) copy-start(f32[512,512]{1,0:T(8,128)} %constant.46.clone.table_ref) | copy-start | bytes 3145732
  3.1 53.2 %copy-start.5 = (f32[51,256]{1,0:T(8,128)S(1)}, f32[51,256]{1,0:T(8,128)}, u32[]{:S(2)}) copy-start(f32[51,256]{1,0:T(8,128)} %constant.48.clone.wave_ref) | copy-start | bytes 156676
  3.1 53.2 %all-to-all-start = ((f32[32,36,1,128]{3,2,1,0:T(1,128)}), f32[32,36,1,128]{3,2,1,0:T(1,128)S(1)}, u32[]{:S(2)}, u32[]{:S(2)}) async-start(f32[32,36,1,128]{3,2,1,0:T(1,128)} %bitcast.33), calls=%async_computation | async-start | bytes 1179648 | tf_op jit(solution)/shard_map/all_to_all | solution.py:469
  20.0 36.3 %copy-start.4 = (f32[34,256]{1,0:T(8,128)S(1)}, f32[34,256]{1,0:T(8,128)}, u32[]{:S(2)}) copy-start(f32[34,256]{1,0:T(8,128)} %constant.47.clone.twiddle_ref) | copy-start | bytes 104452
  57.5 5.1 %collective-permute-start = (f32[17,8,256]{2,1,0:T(8,128)S(1)}, f32[17,8,256]{2,1,0:T(8,128)S(1)}, u32[]{:S(2)}, u32[]{:S(2)}) collective-permute-start(f32[17,8,256]{2,1,0:T(8,128)S(1)} %get-tuple-element.10), channel_id=1, source_target_pairs={{0,16},{16,32},{32,48},{48,64},{64,80},{80,96},{96,112},{112,128},... | collective-permute-start | bytes 417800 | tf_op jit(solution)/shard_map/ppermute | solution.py:482
  59.7 6.4 %collective-permute-start.1 = (f32[17,8,256]{2,1,0:T(8,128)S(1)}, f32[17,8,256]{2,1,0:T(8,128)S(1)}, u32[]{:S(2)}, u32[]{:S(2)}) collective-permute-start(f32[17,8,256]{2,1,0:T(8,128)S(1)} %get-tuple-element.11), channel_id=1, source_target_pairs={{16,0},{32,16},{48,32},{64,48},{80,64},{96,80},{112,96},{128,112},... | collective-permute-start | bytes 417800 | tf_op jit(solution)/shard_map/ppermute | solution.py:483
  67.5 41.7 %copy-start.1 = (f32[2,180,128]{2,0,1:T(2,128)S(1)}, f32[2,180,128]{2,0,1:T(2,128)}, u32[]{:S(2)}) copy-start(f32[2,180,128]{2,0,1:T(2,128)} %param.12) | copy-start | bytes 552964
  67.5 41.7 %copy-start.2 = (f32[2,180,128]{2,0,1:T(2,128)S(1)}, f32[2,180,128]{2,0,1:T(2,128)}, u32[]{:S(2)}) copy-start(f32[2,180,128]{2,0,1:T(2,128)} %param.13) | copy-start | bytes 552964
  67.5 41.7 %copy-start.3 = (f32[2,180,128]{2,0,1:T(2,128)S(1)}, f32[2,180,128]{2,0,1:T(2,128)}, u32[]{:S(2)}) copy-start(f32[2,180,128]{2,0,1:T(2,128)} %param.14) | copy-start | bytes 552964

commit v4 on v3

--- a/solution.py
+++ b/solution.py
@@ -78,6 +78,7 @@
     table[:, 4] = cos[1:-1]
     table[:, 5] = np.repeat(y_coef[0:NLAT:ROWS], ROWS)
     table[:, 6] = np.repeat(y_coef[ROWS + 1 :: ROWS], ROWS)
+    table[:, 7] = np.arange(NLAT) // ROWS % 2
     return table.reshape(NLAT // ROWS, ROWS, LANES).astype(np.float32)
 
 
@@ -276,12 +277,13 @@
     transform(x_ref, table_ref, twiddle_ref, spec_ref, left_ref, WIND_COLUMNS)
 
 
-def mass_kernel(x_ref, table_ref, twiddle_ref, wave_ref, row_ref, spec_ref, up_ref, down_ref, left_ref):
+def mass_kernel(x_ref, table_ref, twiddle_ref, wave_ref, row_ref, spec_ref, near_ref, far_ref, left_ref):
     transform(x_ref, table_ref, twiddle_ref, spec_ref, left_ref, MASS_COLUMNS)
     row = row_ref[0]
     ratio2, x_coef, coslat = row[:, 0:1], row[:, 1:2], row[:, 4:5]
     real, imag = slice(0, WIDE), slice(WIDE, 2 * WIDE)
     zeros = jnp.zeros((2, WIDE), jnp.float32)
+    odd = row[:, 7:8] > 0.5
     for k1 in range(WAVES):
         here, there, slope = (wave_ref[i * WAVES + k1 : i * WAVES + k1 + 1, :] for i in range(3))
         damp = 0.5 * (ratio2 / jnp.maximum(here, ratio2) + ratio2 / jnp.maximum(there, ratio2))
@@ -301,16 +303,19 @@
         flux_im = scale * spec_ref[rows(VH), imag]
         spec_ref[rows(VH), real] = flux_re
         spec_ref[rows(VH), imag] = flux_im
-        up_ref[k1] = jnp.concatenate([mass_re[7:8], mass_im[7:8], flux_re[6:8], flux_im[6:8], zeros], axis=0)
-        down_ref[k1] = jnp.concatenate([mass_re[0:1], mass_im[0:1], flux_re[0:2], flux_im[0:2], zeros], axis=0)
+        up = jnp.concatenate([mass_re[7:8], mass_im[7:8], flux_re[6:8], flux_im[6:8], zeros], axis=0)
+        down = jnp.concatenate([mass_re[0:1], mass_im[0:1], flux_re[0:2], flux_im[0:2], zeros], axis=0)
+        near_ref[k1] = jnp.where(odd, down, up)
+        far_ref[k1] = jnp.where(odd, up, down)
 
 
 def inverse_kernel(
-    spec_ref, wind_ref, below_ref, above_ref, table_ref, twiddle_ref, wave_ref, row_ref, out_ref, left_ref, right_ref
+    spec_ref, wind_ref, near_ref, far_ref, table_ref, twiddle_ref, wave_ref, row_ref, out_ref, left_ref, right_ref
 ):
     row = row_ref[0]
     ratio2, x_coef, y_coef, rotation = (row[:, i : i + 1] for i in range(4))
     y_below, y_above = row[0:1, 5:6], row[0:1, 6:7]
+    odd = row[:, 7:8] > 0.5
     spans = (slice(0, WIDE), slice(WIDE, 2 * WIDE))
     for k1 in range(WAVES):
         here, there, slope = (wave_ref[i * WAVES + k1 : i * WAVES + k1 + 1, :] for i in range(3))
@@ -320,12 +325,13 @@
             return slice(f * BLOCK + k1 * ROWS, f * BLOCK + (k1 + 1) * ROWS)
 
         mass = []
+        below = jnp.where(odd, near_ref[k1], far_ref[k1])
+        above = jnp.where(odd, far_ref[k1], near_ref[k1])
         for part, span in enumerate(spans):
             flux = spec_ref[rows(VH), span]
             gain = spec_ref[rows(UH), span]
-            mass_below, mass_above = below_ref[k1, part : part + 1, :], above_ref[k1, part : part + 1, :]
-            fluxes_below = below_ref[k1, 2 + 2 * part : 4 + 2 * part, :]
-            fluxes_above = above_ref[k1, 2 + 2 * part : 4 + 2 * part, :]
+            mass_below, mass_above = below[part : part + 1], above[part : part + 1]
+            fluxes_below, fluxes_above = below[2 + 2 * part : 4 + 2 * part], above[2 + 2 * part : 4 + 2 * part]
             prev = jnp.concatenate([fluxes_below[1:2], flux[:-1]], axis=0)
             following = jnp.concatenate([flux[1:], fluxes_above[0:1]], axis=0)
             change = gain - y_coef * (following - prev)
@@ -379,13 +385,14 @@
     return (level * 16 + (15 - r if lat % 2 else r)) * 16 + lat
 
 
-def neighbour_pairs(up):
+def swaps(odd):
     pairs = []
     for level in range(2):
         for lat in range(16):
-            pairs += [(place(level, r, lat), place(level, r + 1, lat)) for r in range(15)]
-        pairs += [(place(level, 15, lat), place(level, 0, lat + 1)) for lat in range(15)]
-    return pairs if up else [(b, a) for a, b in pairs]
+            pairs += [(place(level, r, lat), place(level, r + 1, lat)) for r in range(odd, 15, 2)]
+            if odd and lat < 15:
+                pairs.append((place(level, 15, lat), place(level, 0, lat + 1)))
+    return pairs + [(b, a) for a, b in pairs]
 
 
 def in_smem():
@@ -436,7 +443,7 @@
     )(whole, dft_table(), twiddle_table())
 
 
-def inverse(spec, wind, below, above, row):
+def inverse(spec, wind, near, far, row):
     return pl.pallas_call(
         inverse_kernel,
         out_shape=like(PARTS * CHUNK, LANES),
@@ -446,7 +453,7 @@
         compiler_params=PARAMS,
         cost_estimate=cost(3),
         name="inverse",
-    )(spec, wind, below, above, dft_table(), twiddle_table(), wave_table(), row)
+    )(spec, wind, near, far, dft_table(), twiddle_table(), wave_table(), row)
 
 
 def unpack(turned, back, u, v, h):
@@ -478,11 +485,11 @@
     turned = turned.reshape(1)
     u, v, h = (jnp.swapaxes(x, 0, 1).reshape(2 * SEG, LANES) for x in (u, v, h))
     whole = exchange(pack(turned, u, v, h))
-    spec, up, down = forward_mass(whole, row)
-    below = lax.ppermute(up, ("lon", "lat"), neighbour_pairs(True))
-    above = lax.ppermute(down, ("lon", "lat"), neighbour_pairs(False))
+    spec, near, far = forward_mass(whole, row)
+    near = lax.ppermute(near, ("lon", "lat"), swaps(0))
+    far = lax.ppermute(far, ("lon", "lat"), swaps(1))
     wind = forward_wind(whole)
-    outs = unpack(turned, exchange(inverse(spec, wind, below, above, row)), u, v, h)
+    outs = unpack(turned, exchange(inverse(spec, wind, near, far, row)), u, v, h)
     return tuple(jnp.swapaxes(x.reshape(SEG, 2, LANES), 0, 1) for x in outs)
 
 

time: 112 us -> 110 us (0.982)
  the two profiles are of different devices: /device:TPU:1 before, /device:TPU:22 now
where the time goes in v4:
time: 110 us
  waiting for transfers between devices  41 us (37%)
  blocking collectives  39.9 us (36%)
  starting transfers between devices  20.6 us (19%)
  Pallas kernels  6.93 us (6%)
    all_to_all x1, blocking collectives, exchange(): lax.all_to_all(chunks.reshape(PARTS, CHUNK, 1, LANES), 'lon', 0, 0, tiled...  39.9 us
    all_to_all x1, waiting for transfers between devices, exchange(): lax.all_to_all(chunks.reshape(PARTS, CHUNK, 1, LANES), 'lon', 0, 0, tiled...  35.8 us
    all_to_all x1, starting transfers between devices, exchange(): lax.all_to_all(chunks.reshape(PARTS, CHUNK, 1, LANES), 'lon', 0, 0, tiled...  15.6 us
    ppermute x1, waiting for transfers between devices, step(): far = lax.ppermute(far, ('lon', 'lat'), swaps(1))  5.22 us
    ppermute x1, starting transfers between devices, step(): far = lax.ppermute(far, ('lon', 'lat'), swaps(1))  3.08 us
    pallas_call x1, Pallas kernels, pack(): pl.pallas_call(pack_kernel, out_shape=like(PARTS * CHUNK, LANES), in_spec...  2.41 us
  transfers between devices with their start and end apart: 3, of which 2 were waited for; matrix products, arithmetic and copies ran while one was open for 1% of the time, Pallas kernels for 1%

profile of v4, /device:TPU:22, one launch (start us, length us, event | category | flops | bytes accessed | tf_op | source)
XLA Modules:
  0.0 110.0 jit_solution(10696674742234086370)
XLA Ops:
  0.6 0.0 copy-start
  0.7 2.4 %pack.1 = f32[1152,128]{1,0:T(8,128)} custom-call(s32[1]{0:T(128)} %bitcast.turn_ref, f32[360,128]{1,0:T(8,128)} %bitcast.27, f32[360,128]{1,0:T(8,128)} %bitcast.29, f32[360,128]{1,0:T(8,128)} %bitcast.31), custom_call_target="tpu_custom_call" | custom-call | tf_op jit(solution)/shard_map/pack/pallas_call | solution.py:403
  3.1 0.0 copy-start.5
  3.1 15.6 %all-to-all-start = ((f32[32,36,1,128]{3,2,1,0:T(1,128)}), f32[32,36,1,128]{3,2,1,0:T(1,128)S(1)}, u32[]{:S(2)}, u32[]{:S(2)}) async-start(f32[32,36,1,128]{3,2,1,0:T(1,128)} %bitcast.33), calls=%async_computation | async-start | bytes 1179648 | tf_op jit(solution)/shard_map/all_to_all | solution.py:476
  18.7 0.0 copy-start.4
  18.7 0.7 constant_dynamic-slice_fusion.row_ref
  19.4 35.8 %all-to-all-done = f32[32,36,1,128]{3,2,1,0:T(1,128)S(1)} async-done(((f32[32,36,1,128]{3,2,1,0:T(1,128)}), f32[32,36,1,128]{3,2,1,0:T(1,128)S(1)}, u32[]{:S(2)}, u32[]{:S(2)}) %all-to-all-start) | async-done | bytes 589856 | tf_op jit(solution)/shard_map/all_to_all | solution.py:476
  55.2 0.0 copy-done
  55.2 0.0 copy-done.5
  55.2 0.0 copy-done.4
  55.2 1.2 %forward_mass.1 = (f32[416,512]{1,0:T(8,128)S(1)}, f32[17,8,256]{2,1,0:T(8,128)S(1)}, f32[17,8,256]{2,1,0:T(8,128)S(1)}) custom-call(f32[1152,128]{1,0:T(8,128)S(1)} %bitcast.24, f32[512,512]{1,0:T(8,128)S(1)} %copy-done, f32[34,256]{1,0:T(8,128)S(1)} %copy-done.4, f32[51,256]{1,0:T(8,128)S(1)} %copy-done.5, f32[1,8,128]{2,1,0:T(8,128)S(1)} %constant_dynamic-slice_fusion.row_ref), custom_call_target="tpu_custom_call" | custom-call | flops 654311424 | bytes 1703936 | tf_op jit(solution)/shard_map/forward_mass/pallas_call | solution.py:421
  56.5 1.9 %collective-permute-start = (f32[17,8,256]{2,1,0:T(8,128)S(1)}, f32[17,8,256]{2,1,0:T(8,128)S(1)}, u32[]{:S(2)}, u32[]{:S(2)}) collective-permute-start(f32[17,8,256]{2,1,0:T(8,128)S(1)} %get-tuple-element.10), channel_id=1, source_target_pairs={{0,16},{32,48},{64,80},{96,112},{128,144},{160,176},{192,208},{224... | collective-permute-start | bytes 417800 | tf_op jit(solution)/shard_map/ppermute | solution.py:489
  58.4 3.1 %collective-permute-start.1 = (f32[17,8,256]{2,1,0:T(8,128)S(1)}, f32[17,8,256]{2,1,0:T(8,128)S(1)}, u32[]{:S(2)}, u32[]{:S(2)}) collective-permute-start(f32[17,8,256]{2,1,0:T(8,128)S(1)} %get-tuple-element.11), channel_id=1, source_target_pairs={{16,32},{48,64},{80,96},{112,128},{144,160},{176,192},{208,224},{2... | collective-permute-start | bytes 417800 | tf_op jit(solution)/shard_map/ppermute | solution.py:490
  61.5 0.7 forward_wind.1.wind_ref
  62.2 0.0 collective-permute-done.near_ref
  62.2 5.2 %collective-permute-done.1.far_ref = f32[17,8,256]{2,1,0:T(8,128)S(1)} collective-permute-done((f32[17,8,256]{2,1,0:T(8,128)S(1)}, f32[17,8,256]{2,1,0:T(8,128)S(1)}, u32[]{:S(2)}, u32[]{:S(2)}) %collective-permute-start.1) | collective-permute-done | bytes 139296 | tf_op jit(solution)/shard_map/ppermute | solution.py:490
  67.5 1.4 %inverse.1 = f32[1152,128]{1,0:T(8,128)S(1)} custom-call(f32[416,512]{1,0:T(8,128)S(1)} %get-tuple-element.9.spec_ref, f32[272,512]{1,0:T(8,128)S(1)} %forward_wind.1.wind_ref, f32[17,8,256]{2,1,0:T(8,128)S(1)} %collective-permute-done.near_ref, f32[17,8,256]{2,1,0:T(8,128)S(1)} %collective-permute-done.1.far_ref, f32[512,512]{1,0:T(8,128)S(1)} %copy-done, ...), custom_call_target="tpu_custom_call" | custom-call | flops 654311424 | bytes 1703936 | tf_op jit(solution)/shard_map/inverse/pallas_call | solution.py:447
  68.9 0.0 copy-start.1
  68.9 0.0 copy-start.2
  68.9 0.0 copy-start.3
  68.9 39.9 %all_to_all.10 = f32[32,36,1,128]{3,2,1,0:T(1,128)S(1)} all-to-all(f32[32,36,1,128]{3,2,1,0:T(1,128)S(1)} %bitcast.26), channel_id=1, replica_groups=mesh['lon'=32,'lat'=16] {'lon'}, dimensions={0} | all-to-all | bytes 1179648 | tf_op jit(solution)/shard_map/all_to_all | solution.py:476
  108.9 0.0 copy-done.1
  108.9 0.0 copy-done.3
  108.9 1.2 %unpack.1 = (f32[360,128]{1,0:T(8,128)}, f32[360,128]{1,0:T(8,128)}, f32[360,128]{1,0:T(8,128)}) custom-call(s32[1]{0:T(128)} %bitcast.turn_ref, f32[1152,128]{1,0:T(8,128)S(1)} %bitcast.23, f32[360,128]{1,0:T(8,128)S(1)} %bitcast.28, f32[360,128]{1,0:T(8,128)S(1)} %bitcast.30, f32[360,128]{1,0:T(8,128)S(1)} %bitcast.32), custom_call_target="tpu_custom_call" | custom-call | tf_op jit(solution)/shard_map/unpack/pallas_call | solution.py:460
  (1 shorter events, 0.0 us)
Async XLA Ops:
  0.6 54.6 %copy-start = (f32[512,512]{1,0:T(8,128)S(1)}, f32[512,512]{1,0:T(8,128)}, u32[]{:S(2)}) copy-start(f32[512,512]{1,0:T(8,128)} %constant.46.clone.table_ref) | copy-start | bytes 3145732
  3.1 52.2 %copy-start.5 = (f32[51,256]{1,0:T(8,128)S(1)}, f32[51,256]{1,0:T(8,128)}, u32[]{:S(2)}) copy-start(f32[51,256]{1,0:T(8,128)} %constant.48.clone.wave_ref) | copy-start | bytes 156676
  3.1 52.2 %all-to-all-start = ((f32[32,36,1,128]{3,2,1,0:T(1,128)}), f32[32,36,1,128]{3,2,1,0:T(1,128)S(1)}, u32[]{:S(2)}, u32[]{:S(2)}) async-start(f32[32,36,1,128]{3,2,1,0:T(1,128)} %bitcast.33), calls=%async_computation | async-start | bytes 1179648 | tf_op jit(solution)/shard_map/all_to_all | solution.py:476
  18.7 36.5 %copy-start.4 = (f32[34,256]{1,0:T(8,128)S(1)}, f32[34,256]{1,0:T(8,128)}, u32[]{:S(2)}) copy-start(f32[34,256]{1,0:T(8,128)} %constant.47.clone.twiddle_ref) | copy-start | bytes 104452
  56.5 5.8 %collective-permute-start = (f32[17,8,256]{2,1,0:T(8,128)S(1)}, f32[17,8,256]{2,1,0:T(8,128)S(1)}, u32[]{:S(2)}, u32[]{:S(2)}) collective-permute-start(f32[17,8,256]{2,1,0:T(8,128)S(1)} %get-tuple-element.10), channel_id=1, source_target_pairs={{0,16},{32,48},{64,80},{96,112},{128,144},{160,176},{192,208},{224... | collective-permute-start | bytes 417800 | tf_op jit(solution)/shard_map/ppermute | solution.py:489
  58.4 9.1 %collective-permute-start.1 = (f32[17,8,256]{2,1,0:T(8,128)S(1)}, f32[17,8,256]{2,1,0:T(8,128)S(1)}, u32[]{:S(2)}, u32[]{:S(2)}) collective-permute-start(f32[17,8,256]{2,1,0:T(8,128)S(1)} %get-tuple-element.11), channel_id=1, source_target_pairs={{16,32},{48,64},{80,96},{112,128},{144,160},{176,192},{208,224},{2... | collective-permute-start | bytes 417800 | tf_op jit(solution)/shard_map/ppermute | solution.py:490
  68.9 40.0 %copy-start.1 = (f32[2,180,128]{2,0,1:T(2,128)S(1)}, f32[2,180,128]{2,0,1:T(2,128)}, u32[]{:S(2)}) copy-start(f32[2,180,128]{2,0,1:T(2,128)} %param.12) | copy-start | bytes 552964
  68.9 40.0 %copy-start.2 = (f32[2,180,128]{2,0,1:T(2,128)S(1)}, f32[2,180,128]{2,0,1:T(2,128)}, u32[]{:S(2)}) copy-start(f32[2,180,128]{2,0,1:T(2,128)} %param.13) | copy-start | bytes 552964
  68.9 40.0 %copy-start.3 = (f32[2,180,128]{2,0,1:T(2,128)S(1)}, f32[2,180,128]{2,0,1:T(2,128)}, u32[]{:S(2)}) copy-start(f32[2,180,128]{2,0,1:T(2,128)} %param.14) | copy-start | bytes 552964

commit v5 on v4

v5 whole, which is shorter than its diff:
```python
import functools
import math

import jax
import jax.numpy as jnp
import numpy as np
from jax import lax
from jax.experimental import pallas as pl
from jax.experimental.pallas import tpu as pltpu
from jax.sharding import PartitionSpec as P

NLON = 5760
NLAT = 2048
PARTS = 32
SEG = 180
LANES = 128
TAIL = SEG - LANES
HALF = 64
ROWS = 8
WAVES = PARTS // 2 + 1
WIDE = 2 * LANES
SCALE = 1.0 / NLON
SIDE = HALF - TAIL
LAST = TAIL - 2 * SIDE
QUARTER = 32
CHUNK = 4 * ROWS + 2


def placed():
    b = np.arange(SEG)
    tail, side = b[LANES:], LANES + SIDE
    last = np.concatenate([b[-LAST:], np.full(QUARTER - LAST, -1)])
    return np.concatenate([b[:LANES], tail, b[LANES:side], tail, b[side : side + SIDE], np.tile(last, 4)])


def dft_table():
    b = placed()
    angle = (np.outer(b, np.arange(SEG)) % SEG) * (2.0 * math.pi / SEG)
    cos, sin = np.cos(angle) * (b >= 0)[:, None], np.sin(angle) * (b >= 0)[:, None]
    table = np.zeros((6 * LANES, 2 * WIDE))
    for to, (re, im) in ((slice(0, SEG), (cos, sin)), (slice(WIDE, WIDE + SEG), (-sin, cos))):
        table[:WIDE, to], table[WIDE : 2 * WIDE, to] = re[:WIDE], im[:WIDE]
        table[2 * WIDE : 2 * WIDE + LANES, to], table[2 * WIDE + LANES :, to] = re[WIDE:], im[WIDE:]
    return table.astype(np.float32)


def twiddle_table():
    angle = np.outer(np.arange(WAVES), placed()) * (2.0 * math.pi / NLON)
    return np.concatenate([np.cos(angle), np.sin(angle)]).astype(np.float32)


def wave_table():
    k = np.arange(WAVES)[:, None] + PARTS * np.arange(SEG)[None, :]
    step = np.float32(math.pi / NLON)
    here = np.sin(k.astype(np.float32) * step) ** 2
    there = np.sin(((NLON - k) % NLON).astype(np.float32) * step) ** 2
    slope = 2.0 * np.sin(2.0 * math.pi * k / NLON)
    table = np.zeros((3 * WAVES, WIDE), np.float32)
    table[:, :SEG] = np.concatenate([here, there, slope])
    return table


def row_table():
    j = np.arange(-1, NLAT + 1)
    phi = np.float32(-0.5 * math.pi) + (j.astype(np.float32) + np.float32(0.5)) * np.float32(math.pi / NLAT)
    phi = phi.astype(np.float64)
    lat_step, lon_step = math.pi / NLAT, 2.0 * math.pi / NLON
    time_step = 0.25 * lat_step
    cos = np.cos(phi)
    y_coef = time_step / (2.0 * lat_step * cos)
    y_coef[0] = y_coef[-1] = 0.0
    table = np.zeros((NLAT, LANES))
    table[:, 0] = (cos / math.cos(0.25 * math.pi))[1:-1] ** 2
    table[:, 1] = (time_step / (2.0 * lon_step * cos))[1:-1]
    table[:, 2] = y_coef[1:-1]
    table[:, 3] = 0.3 * np.sin(phi)[1:-1]
    table[:, 4] = cos[1:-1]
    table[:, 5] = np.repeat(y_coef[0:NLAT:ROWS], ROWS)
    table[:, 6] = np.repeat(y_coef[ROWS + 1 :: ROWS], ROWS)
    table[:, 7] = np.arange(NLAT) // ROWS % 2
    return table.reshape(NLAT // ROWS, ROWS, LANES).astype(np.float32)


PUSH_COEF = 0.25 / 2.0


def add(x, y):
    if x is None:
        return y
    return x if y is None else x + y


def sub(x, y):
    if y is None:
        return x
    return -y if x is None else x - y


def times(z, cos, sin):
    re, im = z
    if abs(sin) < 1e-15:
        return (re * cos, None if im is None else im * cos)
    if im is None:
        return (re * cos, re * sin)
    return (re * cos - im * sin, re * sin + im * cos)


def real_fft(values):
    n = len(values)
    if n == 2:
        return [(values[0] + values[1], None), (values[0] - values[1], None)]
    even, odd = real_fft(values[0::2]), real_fft(values[1::2])
    out = [None] * (n // 2 + 1)
    out[0] = (even[0][0] + odd[0][0], None)
    out[n // 2] = (even[0][0] - odd[0][0], None)
    for k in range(1, n // 4):
        re, im = times(odd[k], math.cos(2 * math.pi * k / n), -math.sin(2 * math.pi * k / n))
        out[k] = (add(even[k][0], re), add(even[k][1], im))
        out[n // 2 - k] = (sub(even[k][0], re), sub(im, even[k][1]))
    out[n // 4] = (even[n // 4][0], -odd[n // 4][0])
    return out


def real_ifft(waves):
    n = 2 * (len(waves) - 1)
    if n == 2:
        return [waves[0][0] + waves[1][0], waves[0][0] - waves[1][0]]
    even, odd = [None] * (n // 4 + 1), [None] * (n // 4 + 1)
    even[0] = (waves[0][0] + waves[n // 2][0], None)
    odd[0] = (waves[0][0] - waves[n // 2][0], None)
    for k in range(1, n // 4):
        (re, im), (far_re, far_im) = waves[k], waves[n // 2 - k]
        even[k] = (re + far_re, im - far_im)
        odd[k] = times((re - far_re, im + far_im), math.cos(2 * math.pi * k / n), math.sin(2 * math.pi * k / n))
    even[n // 4] = (2.0 * waves[n // 4][0], None)
    odd[n // 4] = (-2.0 * waves[n // 4][1], None)
    out = [None] * n
    out[0::2], out[1::2] = real_ifft(even), real_ifft(odd)
    return out


def lane(shape):
    return lax.broadcasted_iota(jnp.int32, shape, 1)


def own_quarter(shape):
    return lane(shape) // QUARTER == lax.broadcasted_iota(jnp.int32, shape, 0) % 4


def fold(tile):
    size = tile.shape[0]
    mine = jnp.where(own_quarter(tile.shape), tile, 0.0)
    pairs = mine + pltpu.roll(mine, size - 1, 0)
    return pairs + pltpu.roll(pairs, size - 2, 0)


def spot(level, r, turned):
    return CHUNK * (level * 16 + (15 - r if turned else r))


def east(level, start, count):
    return pl.ds(2 * start + level, count, 2)


def pack_kernel(turn_ref, u_hbm, v_hbm, h_hbm, out_ref, u_ref, v_ref, h_ref, tail_ref, last_ref, sems):
    moves = [
        pltpu.make_async_copy(src, dst, sems.at[i])
        for i, (src, dst) in enumerate(((u_hbm, u_ref), (v_hbm, v_ref), (h_hbm, h_ref)))
    ]
    for move in moves:
        move.start()
    last_ref[...] = jnp.zeros_like(last_ref)
    for move in moves:
        move.wait()
    for level in range(2):
        tiles = [ref[east(level, 0, LANES), :].T for ref in (u_ref, v_ref, h_ref)]
        tail_ref[:TAIL, :] = u_ref[east(level, LANES, TAIL), :]
        tail_ref[TAIL:HALF, :] = h_ref[east(level, LANES, SIDE), :]
        tail_ref[HALF : HALF + TAIL, :] = v_ref[east(level, LANES, TAIL), :]
        tail_ref[HALF + TAIL :, :] = h_ref[east(level, LANES + SIDE, SIDE), :]
        tiles.append(tail_ref[...].T)
        last = h_ref[east(level, SEG - LAST, LAST), :]
        for g in range(4):
            last_ref[g * QUARTER : g * QUARTER + LAST, :] = last
        tail_ref[...] = fold(last_ref[...].T)
        folded = tail_ref[pl.ds(0, 32, 4), :]
        for turned in (False, True):

            @pl.when(turn_ref[0] == int(turned))
            def _():
                for r in range(16):
                    at = spot(level, r, turned)
                    for f in range(4):
                        out_ref[at + f * ROWS : at + (f + 1) * ROWS, :] = tiles[f][r * ROWS : (r + 1) * ROWS]
                    out_ref[at + 4 * ROWS : at + CHUNK, :] = folded[2 * r : 2 * r + 2]


def unpack_kernel(turn_ref, in_ref, u_ref, v_ref, h_ref, u_out, v_out, h_out, tile_ref):
    for level in range(2):
        for turned in (False, True):

            @pl.when(turn_ref[0] == int(turned))
            def _():
                for r in range(16):
                    at = spot(level, r, turned)
                    for f in range(4):
                        tile_ref[f, r * ROWS : (r + 1) * ROWS, :] = in_ref[at + f * ROWS : at + (f + 1) * ROWS, :]
                    for t in range(2):
                        row = in_ref[at + 4 * ROWS + t : at + 4 * ROWS + t + 1, :]
                        tile_ref[4, r * ROWS + 4 * t : r * ROWS + 4 * t + 4, :] = jnp.broadcast_to(row, (4, LANES))

        for f, (ref, out) in enumerate(((u_ref, u_out), (v_ref, v_out), (h_ref, h_out))):
            here = east(level, 0, LANES)
            out[here, :] = ref[here, :] + tile_ref[f].T
        mixed, quarters = tile_ref[3].T, tile_ref[4].T
        group = lane((LAST, LANES)) % 4
        last = quarters[:LAST]
        for g in range(1, 4):
            last = jnp.where(group == g, quarters[g * QUARTER : g * QUARTER + LAST], last)
        for ref, out, start, change in (
            (u_ref, u_out, LANES, mixed[:TAIL]),
            (h_ref, h_out, LANES, mixed[TAIL:HALF]),
            (v_ref, v_out, LANES, mixed[HALF : HALF + TAIL]),
            (h_ref, h_out, LANES + SIDE, mixed[HALF + TAIL :]),
            (h_ref, h_out, SEG - LAST, last),
        ):
            here = east(level, start, change.shape[0])
            out[here, :] = ref[here, :] + change


def halves(x):
    high = x.astype(jnp.bfloat16)
    return high, (x - high.astype(jnp.float32)).astype(jnp.bfloat16)


def dot(x, table, contract):
    def product(a, b):
        return lax.dot_general(a, b, (((1,), (contract,)), ((), ())), preferred_element_type=jnp.float32)

    (high, low), (table_high, table_low) = halves(x), halves(table)
    return product(high, table_high) + (product(high, table_low) + product(low, table_high))


BLOCK = WAVES * ROWS


def padded(fields):
    return -(-fields * BLOCK // 16) * 16


def transform(columns, table_ref, twiddle_ref, spec_ref, left_ref):
    at = lane((ROWS, LANES))
    own = (at < TAIL, (at >= HALF) & (at < HALF + TAIL))
    for get, part, fields in columns:
        lanes = slice(part * LANES, (part + 1) * LANES)
        late = slice(WIDE + part * LANES, WIDE + (part + 1) * LANES)
        for k1, (re, im) in enumerate(real_fft([get(a) for a in range(PARTS)])):
            cos = twiddle_ref[k1 : k1 + 1, lanes]
            sin = twiddle_ref[WAVES + k1 : WAVES + k1 + 1, lanes]
            if im is None:
                new_re, new_im = re * cos, -re * sin
            else:
                new_re, new_im = re * cos + im * sin, im * cos - re * sin
            for f, half in fields:
                rows = slice(f * BLOCK + k1 * ROWS, f * BLOCK + (k1 + 1) * ROWS)
                if part == 0:
                    left_ref[rows, lanes], left_ref[rows, late] = new_re, new_im
                else:
                    left_ref[rows, lanes] = jnp.where(own[half], new_re, 0.0)
                    left_ref[rows, late] = jnp.where(own[half], new_im, 0.0)
    spec_ref[...] = dot(left_ref[...], table_ref[: 2 * WIDE, :], 0)


def tiles_of(x_ref):
    def tile(f):
        return lambda a: x_ref[a * CHUNK + f * ROWS : a * CHUNK + (f + 1) * ROWS, :]

    return tile


def gather_tails(x_ref, tails_ref):
    at = lane((ROWS, LANES))
    place_of_four = lax.broadcasted_iota(jnp.int32, at.shape, 0) % 4
    for a in range(PARTS):
        base = a * CHUNK + 3 * ROWS
        mixed = x_ref[base : base + ROWS, :]
        rows = [jnp.broadcast_to(x_ref[base + ROWS + t : base + ROWS + t + 1, :], (4, LANES)) for t in range(2)]
        quarters, last = jnp.concatenate(rows, axis=0), None
        for g in range(4):
            moved = pltpu.roll(quarters, (2 * SIDE - g * QUARTER) % LANES, 1)
            last = moved if last is None else jnp.where(place_of_four == g, moved, last)
        beside_u, beside_v = pltpu.roll(mixed, LANES - TAIL, 1), pltpu.roll(mixed, HALF - TAIL + SIDE, 1)
        whole = jnp.where(at < SIDE, beside_u, jnp.where(at < 2 * SIDE, beside_v, last))
        tails_ref[a * ROWS : (a + 1) * ROWS, :] = jnp.where(at < HALF, whole, pltpu.roll(whole, HALF, 1))


H, UH, VH = range(3)
U, V = range(2)


def damping(row, wave_ref, k1):
    ratio2 = row[:, 0:1]
    here, there = wave_ref[k1 : k1 + 1, :], wave_ref[WAVES + k1 : WAVES + k1 + 1, :]
    return 0.5 * (ratio2 / jnp.maximum(here, ratio2) + ratio2 / jnp.maximum(there, ratio2))


REAL, IMAG = slice(0, WIDE), slice(WIDE, 2 * WIDE)


def rows_of(f, k1):
    return slice(f * BLOCK + k1 * ROWS, f * BLOCK + (k1 + 1) * ROWS)


def wind_kernel(x_ref, table_ref, twiddle_ref, wave_ref, row_ref, spec_ref, damp_ref, left_ref):
    tile = tiles_of(x_ref)
    columns = ((tile(0), 0, ((U, 0),)), (tile(1), 0, ((V, 0),)), (tile(3), 1, ((U, 0), (V, 1))))
    transform(columns, table_ref, twiddle_ref, spec_ref, left_ref)
    row = row_ref[0]
    rotation = row[:, 3:4]
    for k1 in range(WAVES):
        damp = SCALE * damping(row, wave_ref, k1)
        damp_ref[rows_of(0, k1), :] = damp
        turn = damp * rotation
        for span in (REAL, IMAG):
            spec_ref[rows_of(U, k1), span] = -turn * spec_ref[rows_of(U, k1), span]
            spec_ref[rows_of(V, k1), span] = turn * spec_ref[rows_of(V, k1), span]


def to_message(rows):
    tails = rows[:, LANES:]
    tails = jnp.where(lane((2, LANES)) < HALF, tails[:2], pltpu.roll(tails[2:], HALF, 1))
    return jnp.concatenate([rows[:, :LANES], tails, jnp.zeros((2, LANES), jnp.float32)], axis=0)


def from_message(message):
    tails = message[4:6]
    tails = jnp.concatenate([tails, pltpu.roll(tails, HALF, 1)], axis=0)
    return jnp.concatenate([message[:4], tails], axis=1)


def mass_kernel(
    x_ref, table_ref, twiddle_ref, wave_ref, row_ref, spec_ref, near_ref, far_ref, left_ref, tails_ref
):
    gather_tails(x_ref, tails_ref)
    tile = tiles_of(x_ref)

    def tail(a):
        return tails_ref[a * ROWS : (a + 1) * ROWS, :]

    def product(f, h):
        return lambda a: tile(f)(a) * h(a)

    columns = (
        (tile(2), 0, ((H, 0),)),
        (product(0, tile(2)), 0, ((UH, 0),)),
        (product(1, tile(2)), 0, ((VH, 0),)),
        (tail, 1, ((H, 0),)),
        (product(3, tail), 1, ((UH, 0), (VH, 1))),
    )
    transform(columns, table_ref, twiddle_ref, spec_ref, left_ref)
    row = row_ref[0]
    x_coef, y_coef, coslat, odd = row[:, 1:2], row[:, 2:3], row[:, 4:5], row[:4, 7:8] > 0.5
    for k1 in range(WAVES):
        damp = damping(row, wave_ref, k1)
        across = x_coef * wave_ref[2 * WAVES + k1 : 2 * WAVES + k1 + 1, :] * damp
        gain_re = across * spec_ref[rows_of(UH, k1), IMAG]
        gain_im = -across * spec_ref[rows_of(UH, k1), REAL]
        scale = damp * coslat
        up, down = [], []
        for span, gain in ((REAL, gain_re), (IMAG, gain_im)):
            spec_ref[rows_of(UH, k1), span] = gain
            mass = spec_ref[rows_of(H, k1), span] + gain
            flux = scale * spec_ref[rows_of(VH, k1), span]
            spec_ref[rows_of(VH, k1), span] = flux
            up += [flux[7:8], mass[7:8] + y_coef[7:8] * flux[6:7]]
            down += [flux[0:1], mass[0:1] - y_coef[0:1] * flux[1:2]]
        up, down = jnp.concatenate(up, axis=0), jnp.concatenate(down, axis=0)
        near_ref[rows_of(0, k1), :] = to_message(jnp.where(odd, down, up))
        far_ref[rows_of(0, k1), :] = to_message(jnp.where(odd, up, down))


def inverse_kernel(
    spec_ref, wind_ref, damp_ref, near_ref, far_ref, table_ref, twiddle_ref, wave_ref, row_ref, out_ref, left_ref,
    right_ref, last_ref
):
    row = row_ref[0]
    x_coef, y_coef = row[:, 1:2], row[:, 2:3]
    y_below, y_above = row[0:1, 5:6], row[0:1, 6:7]
    odd = row[:, 7:8] > 0.5
    for k1 in range(WAVES):
        near, far = near_ref[rows_of(0, k1), :], far_ref[rows_of(0, k1), :]
        below, above = from_message(jnp.where(odd, near, far)), from_message(jnp.where(odd, far, near))
        damp = damp_ref[rows_of(0, k1), :]
        across = damp * x_coef * wave_ref[2 * WAVES + k1 : 2 * WAVES + k1 + 1, :]
        along = -PUSH_COEF * damp
        mass = []
        for part, span in enumerate((REAL, IMAG)):
            flux = spec_ref[rows_of(VH, k1), span]
            flux_below, flux_above = below[2 * part : 2 * part + 1], above[2 * part : 2 * part + 1]
            prev = jnp.concatenate([flux_below, flux[:-1]], axis=0)
            following = jnp.concatenate([flux[1:], flux_above], axis=0)
            change = spec_ref[rows_of(UH, k1), span] - y_coef * (following - prev)
            new = spec_ref[rows_of(H, k1), span] + change
            new_below = below[2 * part + 1 : 2 * part + 2] - y_below * flux[0:1]
            new_above = above[2 * part + 1 : 2 * part + 2] + y_above * flux[7:8]
            mass.append(new)
            prev = jnp.concatenate([new_below, new[:-1]], axis=0)
            following = jnp.concatenate([new[1:], new_above], axis=0)
            left_ref[rows_of(2, k1), span] = along * (following - prev) + wind_ref[rows_of(U, k1), span]
            left_ref[rows_of(0, k1), span] = SCALE * change
        left_ref[rows_of(1, k1), REAL] = across * mass[1] + wind_ref[rows_of(V, k1), REAL]
        left_ref[rows_of(1, k1), IMAG] = wind_ref[rows_of(V, k1), IMAG] - across * mass[0]
    right_ref[...] = dot(left_ref[...], table_ref[: 2 * WIDE, :], 1)
    last_ref[...] = dot(left_ref[:BLOCK, :], table_ref[2 * WIDE :, :], 1)
    at = lane((ROWS, LANES))
    for f, part, fields in ((0, 0, (1,)), (1, 0, (2,)), (2, 0, (0,)), (3, 1, (0, 1, 2)), (4, 2, (0,))):
        lanes = slice(part * LANES, (part + 1) * LANES)
        source, start, late = (last_ref, 0, LANES) if part == 2 else (right_ref, part * LANES, WIDE + part * LANES)
        waves = []
        for k1 in range(WAVES):
            cos = twiddle_ref[k1 : k1 + 1, lanes]
            sin = twiddle_ref[WAVES + k1 : WAVES + k1 + 1, lanes]
            re = [source[rows_of(g, k1), start : start + LANES] for g in fields]
            im = [source[rows_of(g, k1), late : late + LANES] for g in fields]
            if len(fields) == 3:
                own = (at < TAIL, (at >= HALF) & (at < HALF + TAIL))
                re = [jnp.where(own[0], re[1], jnp.where(own[1], re[2], re[0]))]
                im = [jnp.where(own[0], im[1], jnp.where(own[1], im[2], im[0]))]
            re, im = re[0], im[0]
            waves.append((re * cos - im * sin, None if k1 in (0, WAVES - 1) else im * cos + re * sin))
        for a, value in enumerate(real_ifft(waves)):
            start = a * CHUNK + f * ROWS
            if f == 4:
                value = fold(value)
                value = jnp.concatenate([value[0:1], value[4:5]], axis=0)
            out_ref[start : start + value.shape[0], :] = value


def in_vmem():
    return pl.BlockSpec(memory_space=pltpu.VMEM)


PARAMS = pltpu.CompilerParams(vmem_limit_bytes=40 * 2**20)


def like(*shape):
    return jax.ShapeDtypeStruct(shape, jnp.float32)


def place(level, r, lat):
    return (level * 16 + (15 - r if lat % 2 else r)) * 16 + lat


def swaps(odd):
    pairs = []
    for level in range(2):
        for lat in range(16):
            pairs += [(place(level, r, lat), place(level, r + 1, lat)) for r in range(odd, 15, 2)]
            if odd and lat < 15:
                pairs.append((place(level, 15, lat), place(level, 0, lat + 1)))
    return pairs + [(b, a) for a, b in pairs]


def in_smem():
    return pl.BlockSpec(memory_space=pltpu.SMEM)


def pack(turned, u, v, h):
    return pl.pallas_call(
        pack_kernel,
        out_shape=like(PARTS * CHUNK, LANES),
        in_specs=[in_smem()] + [pl.BlockSpec(memory_space=pltpu.HBM)] * 3,
        out_specs=in_vmem(),
        scratch_shapes=[pltpu.VMEM((2 * SEG, LANES), jnp.float32)] * 3
        + [pltpu.VMEM((LANES, LANES), jnp.float32)] * 2
        + [pltpu.SemaphoreType.DMA((3,))],
        compiler_params=pltpu.CompilerParams(vmem_limit_bytes=56 * 2**20),
        name="pack",
    )(turned, u, v, h)


def cost(fields):
    size = padded(fields) * 2 * WIDE
    return pl.CostEstimate(flops=6 * size * 2 * WIDE, bytes_accessed=8 * size, transcendentals=0)


def forward_mass(whole, row):
    return pl.pallas_call(
        mass_kernel,
        out_shape=(like(padded(3), 2 * WIDE), like(BLOCK, LANES), like(BLOCK, LANES)),
        in_specs=[in_vmem()] * 5,
        out_specs=(in_vmem(),) * 3,
        scratch_shapes=[pltpu.VMEM((padded(3), 2 * WIDE), jnp.float32), pltpu.VMEM((PARTS * ROWS, LANES), jnp.float32)],
        compiler_params=PARAMS,
        cost_estimate=cost(3),
        name="forward_mass",
    )(whole, dft_table(), twiddle_table(), wave_table(), row)


def forward_wind(whole, row):
    return pl.pallas_call(
        wind_kernel,
        out_shape=(like(padded(2), 2 * WIDE), like(BLOCK, WIDE)),
        in_specs=[in_vmem()] * 5,
        out_specs=(in_vmem(),) * 2,
        scratch_shapes=[pltpu.VMEM((padded(2), 2 * WIDE), jnp.float32)],
        compiler_params=PARAMS,
        cost_estimate=cost(2),
        name="forward_wind",
    )(whole, dft_table(), twiddle_table(), wave_table(), row)


def inverse(spec, wind, damp, near, far, row):
    return pl.pallas_call(
        inverse_kernel,
        out_shape=like(PARTS * CHUNK, LANES),
        in_specs=[in_vmem()] * 9,
        out_specs=in_vmem(),
        scratch_shapes=[pltpu.VMEM((padded(3), 2 * WIDE), jnp.float32)] * 2 + [pltpu.VMEM((BLOCK, WIDE), jnp.float32)],
        compiler_params=PARAMS,
        cost_estimate=cost(3),
        name="inverse",
    )(spec, wind, damp, near, far, dft_table(), twiddle_table(), wave_table(), row)


def unpack(turned, back, u, v, h):
    return pl.pallas_call(
        unpack_kernel,
        out_shape=(like(2 * SEG, LANES),) * 3,
        in_specs=[in_smem()] + [in_vmem()] * 4,
        out_specs=(in_vmem(),) * 3,
        scratch_shapes=[pltpu.VMEM((5, LANES, LANES), jnp.float32)],
        compiler_params=PARAMS,
        name="unpack",
    )(turned, back, u, v, h)


def row_of(group):
    return lax.dynamic_slice_in_dim(jnp.asarray(row_table()), group, 1, axis=0)


def exchange(chunks):
    moved = lax.all_to_all(chunks.reshape(PARTS, CHUNK, 1, LANES), "lon", 0, 0, tiled=True)
    return moved.reshape(PARTS * CHUNK, LANES)


def step(u, v, h):
    lat = lax.axis_index("lat")
    turned = lat % 2
    r = lax.axis_index("lon") % 16
    row = row_of(lat * 16 + jnp.where(turned == 1, 15 - r, r))
    turned = turned.reshape(1)
    u, v, h = (jnp.swapaxes(x, 0, 1).reshape(2 * SEG, LANES) for x in (u, v, h))
    whole = exchange(pack(turned, u, v, h))
    spec, near, far = forward_mass(whole, row)
    near = lax.ppermute(near, ("lon", "lat"), swaps(0))
    far = lax.ppermute(far, ("lon", "lat"), swaps(1))
    wind, damp = forward_wind(whole, row)
    outs = unpack(turned, exchange(inverse(spec, wind, damp, near, far, row)), u, v, h)
    return tuple(jnp.swapaxes(x.reshape(SEG, 2, LANES), 0, 1) for x in outs)


def solution(mesh):
    spec = P(None, "lon", "lat")
    return jax.shard_map(step, mesh=mesh, in_specs=(spec,) * 3, out_specs=(spec,) * 3, check_vma=False)
```

time: 110 us -> 107 us (0.973)
  waiting for transfers between devices: 41 us -> 38.9 us
  blocking collectives: 39.9 us -> 38.4 us
    all_to_all x1, blocking collectives: 39.9 us -> 38.4 us  [exchange(): lax.all_to_all(chunks.reshape(PARTS, CHUNK, 1, LANES), 'lon', 0, 0, tiled...]
    all_to_all x1, waiting for transfers between devices: 35.8 us -> 34.4 us  [exchange(): lax.all_to_all(chunks.reshape(PARTS, CHUNK, 1, LANES), 'lon', 0, 0, tiled...]
where the time goes in v5:
time: 107 us
  waiting for transfers between devices  38.9 us (36%)
  blocking collectives  38.4 us (36%)
  starting transfers between devices  20.5 us (19%)
  Pallas kernels  7.52 us (7%)
    all_to_all x1, blocking collectives, exchange(): lax.all_to_all(chunks.reshape(PARTS, CHUNK, 1, LANES), 'lon', 0, 0, tiled...  38.4 us
    all_to_all x1, waiting for transfers between devices, exchange(): lax.all_to_all(chunks.reshape(PARTS, CHUNK, 1, LANES), 'lon', 0, 0, tiled...  34.4 us
    all_to_all x1, starting transfers between devices, exchange(): lax.all_to_all(chunks.reshape(PARTS, CHUNK, 1, LANES), 'lon', 0, 0, tiled...  15.5 us
    ppermute x1, waiting for transfers between devices, step(): far = lax.ppermute(far, ('lon', 'lat'), swaps(1))  4.46 us
    ppermute x1, starting transfers between devices, step(): far = lax.ppermute(far, ('lon', 'lat'), swaps(1))  3.06 us
    pallas_call x1, Pallas kernels, pack(): pl.pallas_call(pack_kernel, out_shape=like(PARTS * CHUNK, LANES), in_spec...  2.44 us
  transfers between devices with their start and end apart: 3, of which 2 were waited for; matrix products, arithmetic and copies ran while one was open for 1% of the time, Pallas kernels for 1%

profile of v5, /device:TPU:22, one launch (start us, length us, event | category | flops | bytes accessed | tf_op | source)
XLA Modules:
  0.0 106.8 jit_solution(18213283384699979180)
XLA Ops:
  0.6 0.0 copy-start.5
  0.6 0.0 copy-start.4
  0.7 0.0 copy-start
  0.7 2.4 %pack.1 = f32[1088,128]{1,0:T(8,128)} custom-call(s32[1]{0:T(128)} %bitcast.turn_ref, f32[360,128]{1,0:T(8,128)} %bitcast.27, f32[360,128]{1,0:T(8,128)} %bitcast.29, f32[360,128]{1,0:T(8,128)} %bitcast.31), custom_call_target="tpu_custom_call" | custom-call | tf_op jit(solution)/shard_map/pack/pallas_call | solution.py:469
  3.1 15.5 %all-to-all-start = ((f32[32,34,1,128]{3,2,1,0:T(1,128)}), f32[32,34,1,128]{3,2,1,0:T(1,128)S(1)}, u32[]{:S(2)}, u32[]{:S(2)}) async-start(f32[32,34,1,128]{3,2,1,0:T(1,128)} %bitcast.33), calls=%async_computation | async-start | bytes 1114112 | tf_op jit(solution)/shard_map/all_to_all | solution.py:543
  18.7 0.7 constant_dynamic-slice_fusion.row_ref
  19.3 34.4 %all-to-all-done = f32[32,34,1,128]{3,2,1,0:T(1,128)S(1)} async-done(((f32[32,34,1,128]{3,2,1,0:T(1,128)}), f32[32,34,1,128]{3,2,1,0:T(1,128)S(1)}, u32[]{:S(2)}, u32[]{:S(2)}) %all-to-all-start) | async-done | bytes 557088 | tf_op jit(solution)/shard_map/all_to_all | solution.py:543
  53.8 0.0 copy-done.5
  53.8 0.0 copy-done.4
  53.8 0.0 copy-done
  53.8 1.5 %forward_mass.1 = (f32[416,512]{1,0:T(8,128)S(1)}, f32[136,128]{1,0:T(8,128)S(1)}, f32[136,128]{1,0:T(8,128)S(1)}) custom-call(f32[1088,128]{1,0:T(8,128)S(1)} %bitcast.23, f32[768,512]{1,0:T(8,128)S(1)} %copy-done, f32[34,384]{1,0:T(8,128)S(1)} %copy-done.4, f32[51,256]{1,0:T(8,128)S(1)} %copy-done.5, f32[1,8,128]{2,1,0:T(8,128)S(1)} %constant_dynamic-slice_fusion.row_ref), custom_call_target="tpu_custom_call" | custom-call | flops 654311424 | bytes 1703936 | tf_op jit(solution)/shard_map/forward_mass/pallas_call | solution.py:488
  55.3 1.9 %collective-permute-start = (f32[136,128]{1,0:T(8,128)S(1)}, f32[136,128]{1,0:T(8,128)S(1)}, u32[]{:S(2)}, u32[]{:S(2)}) collective-permute-start(f32[136,128]{1,0:T(8,128)S(1)} %get-tuple-element.14), channel_id=1, source_target_pairs={{0,16},{32,48},{64,80},{96,112},{128,144},{160,176},{192,208},{224... | collective-permute-start | bytes 208904 | tf_op jit(solution)/shard_map/ppermute | solution.py:556
  57.3 3.1 %collective-permute-start.1 = (f32[136,128]{1,0:T(8,128)S(1)}, f32[136,128]{1,0:T(8,128)S(1)}, u32[]{:S(2)}, u32[]{:S(2)}) collective-permute-start(f32[136,128]{1,0:T(8,128)S(1)} %get-tuple-element.15), channel_id=1, source_target_pairs={{16,32},{48,64},{80,96},{112,128},{144,160},{176,192},{208,224},{2... | collective-permute-start | bytes 208904 | tf_op jit(solution)/shard_map/ppermute | solution.py:557
  60.3 0.8 forward_wind.1
  61.1 0.0 collective-permute-done.near_ref
  61.1 4.5 %collective-permute-done.1.far_ref = f32[136,128]{1,0:T(8,128)S(1)} collective-permute-done((f32[136,128]{1,0:T(8,128)S(1)}, f32[136,128]{1,0:T(8,128)S(1)}, u32[]{:S(2)}, u32[]{:S(2)}) %collective-permute-start.1) | collective-permute-done | bytes 69664 | tf_op jit(solution)/shard_map/ppermute | solution.py:557
  65.6 0.0 copy-start.1
  65.6 0.0 copy-start.2
  65.6 1.6 %inverse.1 = f32[1088,128]{1,0:T(8,128)S(1)} custom-call(f32[416,512]{1,0:T(8,128)S(1)} %get-tuple-element.11.spec_ref, f32[272,512]{1,0:T(8,128)S(1)} %get-tuple-element.12.wind_ref, f32[136,256]{1,0:T(8,128)S(1)} %get-tuple-element.13.damp_ref, f32[136,128]{1,0:T(8,128)S(1)} %collective-permute-done.near_ref, ...), custom_call_target="tpu_custom_call" | custom-call | flops 654311424 | bytes 1703936 | tf_op jit(solution)/shard_map/inverse/pallas_call | solution.py:514
  67.2 38.4 %all_to_all.10 = f32[32,34,1,128]{3,2,1,0:T(1,128)S(1)} all-to-all(f32[32,34,1,128]{3,2,1,0:T(1,128)S(1)} %bitcast.26), channel_id=1, replica_groups=mesh['lon'=32,'lat'=16] {'lon'}, dimensions={0} | all-to-all | bytes 1114112 | tf_op jit(solution)/shard_map/all_to_all | solution.py:543
  105.6 0.0 copy-done.1
  105.6 0.0 copy-done.2
  105.6 0.0 copy-done.3
  105.6 1.2 %unpack.1 = (f32[360,128]{1,0:T(8,128)}, f32[360,128]{1,0:T(8,128)}, f32[360,128]{1,0:T(8,128)}) custom-call(s32[1]{0:T(128)} %bitcast.turn_ref, f32[1088,128]{1,0:T(8,128)S(1)} %bitcast.25, f32[360,128]{1,0:T(8,128)S(1)} %bitcast.28, f32[360,128]{1,0:T(8,128)S(1)} %bitcast.30, f32[360,128]{1,0:T(8,128)S(1)} %bitcast.32), custom_call_target="tpu_custom_call" | custom-call | tf_op jit(solution)/shard_map/unpack/pallas_call | solution.py:527
  (1 shorter events, 0.0 us)
Async XLA Ops:
  0.6 53.1 %copy-start.5 = (f32[51,256]{1,0:T(8,128)S(1)}, f32[51,256]{1,0:T(8,128)}, u32[]{:S(2)}) copy-start(f32[51,256]{1,0:T(8,128)} %constant.48.clone.wave_ref) | copy-start | bytes 156676
  0.6 53.1 %copy-start.4 = (f32[34,384]{1,0:T(8,128)S(1)}, f32[34,384]{1,0:T(8,128)}, u32[]{:S(2)}) copy-start(f32[34,384]{1,0:T(8,128)} %constant.47.clone.twiddle_ref) | copy-start | bytes 156676
  0.7 53.1 %copy-start = (f32[768,512]{1,0:T(8,128)S(1)}, f32[768,512]{1,0:T(8,128)}, u32[]{:S(2)}) copy-start(f32[768,512]{1,0:T(8,128)} %constant.46.clone.table_ref) | copy-start | bytes 4718596
  3.1 50.6 %all-to-all-start = ((f32[32,34,1,128]{3,2,1,0:T(1,128)}), f32[32,34,1,128]{3,2,1,0:T(1,128)S(1)}, u32[]{:S(2)}, u32[]{:S(2)}) async-start(f32[32,34,1,128]{3,2,1,0:T(1,128)} %bitcast.33), calls=%async_computation | async-start | bytes 1114112 | tf_op jit(solution)/shard_map/all_to_all | solution.py:543
  55.3 5.8 %collective-permute-start = (f32[136,128]{1,0:T(8,128)S(1)}, f32[136,128]{1,0:T(8,128)S(1)}, u32[]{:S(2)}, u32[]{:S(2)}) collective-permute-start(f32[136,128]{1,0:T(8,128)S(1)} %get-tuple-element.14), channel_id=1, source_target_pairs={{0,16},{32,48},{64,80},{96,112},{128,144},{160,176},{192,208},{224... | collective-permute-start | bytes 208904 | tf_op jit(solution)/shard_map/ppermute | solution.py:556
  57.3 8.3 %collective-permute-start.1 = (f32[136,128]{1,0:T(8,128)S(1)}, f32[136,128]{1,0:T(8,128)S(1)}, u32[]{:S(2)}, u32[]{:S(2)}) collective-permute-start(f32[136,128]{1,0:T(8,128)S(1)} %get-tuple-element.15), channel_id=1, source_target_pairs={{16,32},{48,64},{80,96},{112,128},{144,160},{176,192},{208,224},{2... | collective-permute-start | bytes 208904 | tf_op jit(solution)/shard_map/ppermute | solution.py:557
  65.6 40.0 %copy-start.1 = (f32[2,180,128]{2,0,1:T(2,128)S(1)}, f32[2,180,128]{2,0,1:T(2,128)}, u32[]{:S(2)}) copy-start(f32[2,180,128]{2,0,1:T(2,128)} %param.13) | copy-start | bytes 552964
  65.6 40.0 %copy-start.2 = (f32[2,180,128]{2,0,1:T(2,128)S(1)}, f32[2,180,128]{2,0,1:T(2,128)}, u32[]{:S(2)}) copy-start(f32[2,180,128]{2,0,1:T(2,128)} %param.14) | copy-start | bytes 552964
  65.6 40.0 %copy-start.3 = (f32[2,180,128]{2,0,1:T(2,128)S(1)}, f32[2,180,128]{2,0,1:T(2,128)}, u32[]{:S(2)}) copy-start(f32[2,180,128]{2,0,1:T(2,128)} %param.15) | copy-start | bytes 552964

commit v6 on v5

--- a/solution.py
+++ b/solution.py
@@ -339,7 +339,7 @@
 
 
 def mass_kernel(
-    x_ref, table_ref, twiddle_ref, wave_ref, row_ref, spec_ref, near_ref, far_ref, left_ref, tails_ref
+    x_ref, table_ref, twiddle_ref, wave_ref, row_ref, spec_ref, far_ref, near_ref, left_ref, tails_ref
 ):
     gather_tails(x_ref, tails_ref)
     tile = tiles_of(x_ref)
@@ -380,7 +380,7 @@
 
 
 def inverse_kernel(
-    spec_ref, wind_ref, damp_ref, near_ref, far_ref, table_ref, twiddle_ref, wave_ref, row_ref, out_ref, left_ref,
+    spec_ref, wind_ref, damp_ref, far_ref, near_ref, table_ref, twiddle_ref, wave_ref, row_ref, out_ref, left_ref,
     right_ref, last_ref
 ):
     row = row_ref[0]
@@ -510,7 +510,7 @@
     )(whole, dft_table(), twiddle_table(), wave_table(), row)
 
 
-def inverse(spec, wind, damp, near, far, row):
+def inverse(spec, wind, damp, far, near, row):
     return pl.pallas_call(
         inverse_kernel,
         out_shape=like(PARTS * CHUNK, LANES),
@@ -520,7 +520,7 @@
         compiler_params=PARAMS,
         cost_estimate=cost(3),
         name="inverse",
-    )(spec, wind, damp, near, far, dft_table(), twiddle_table(), wave_table(), row)
+    )(spec, wind, damp, far, near, dft_table(), twiddle_table(), wave_table(), row)
 
 
 def unpack(turned, back, u, v, h):
@@ -552,11 +552,11 @@
     turned = turned.reshape(1)
     u, v, h = (jnp.swapaxes(x, 0, 1).reshape(2 * SEG, LANES) for x in (u, v, h))
     whole = exchange(pack(turned, u, v, h))
-    spec, near, far = forward_mass(whole, row)
+    spec, far, near = forward_mass(whole, row)
+    far = lax.ppermute(far, ("lon", "lat"), swaps(1))
     near = lax.ppermute(near, ("lon", "lat"), swaps(0))
-    far = lax.ppermute(far, ("lon", "lat"), swaps(1))
     wind, damp = forward_wind(whole, row)
-    outs = unpack(turned, exchange(inverse(spec, wind, damp, near, far, row)), u, v, h)
+    outs = unpack(turned, exchange(inverse(spec, wind, damp, far, near, row)), u, v, h)
     return tuple(jnp.swapaxes(x.reshape(SEG, 2, LANES), 0, 1) for x in outs)
 
 

time: 107 us -> 105 us (0.981)
  the two profiles are of different devices: /device:TPU:22 before, /device:TPU:1 now
where the time goes in v6:
time: 105 us; the launch traced here: 104 us
  blocking collectives  38.8 us (37%)
  waiting for transfers between devices  34.9 us (33%)
  starting transfers between devices  20.9 us (20%)
  Pallas kernels  7.45 us (7%)
    all_to_all x1, blocking collectives, exchange(): lax.all_to_all(chunks.reshape(PARTS, CHUNK, 1, LANES), 'lon', 0, 0, tiled...  38.8 us
    all_to_all x1, waiting for transfers between devices, exchange(): lax.all_to_all(chunks.reshape(PARTS, CHUNK, 1, LANES), 'lon', 0, 0, tiled...  34.2 us
    all_to_all x1, starting transfers between devices, exchange(): lax.all_to_all(chunks.reshape(PARTS, CHUNK, 1, LANES), 'lon', 0, 0, tiled...  16.8 us
    pallas_call x1, Pallas kernels, pack(): pl.pallas_call(pack_kernel, out_shape=like(PARTS * CHUNK, LANES), in_spec...  2.4 us
    ppermute x1, starting transfers between devices, step(): far = lax.ppermute(far, ('lon', 'lat'), swaps(1))  2.22 us
  transfers between devices with their start and end apart: 3, of which 2 were waited for; matrix products, arithmetic and copies ran while one was open for 1% of the time, Pallas kernels for 1%

profile of v6, /device:TPU:1, one launch (start us, length us, event | category | flops | bytes accessed | tf_op | source)
XLA Modules:
  0.0 103.6 jit_solution(10607565138916017802)
XLA Ops:
  0.6 0.0 copy-start.5
  0.6 0.0 copy-start.4
  0.7 0.0 copy-start
  0.7 2.4 %pack.1 = f32[1088,128]{1,0:T(8,128)} custom-call(s32[1]{0:T(128)} %bitcast.turn_ref, f32[360,128]{1,0:T(8,128)} %bitcast.27, f32[360,128]{1,0:T(8,128)} %bitcast.29, f32[360,128]{1,0:T(8,128)} %bitcast.31), custom_call_target="tpu_custom_call" | custom-call | tf_op jit(solution)/shard_map/pack/pallas_call | solution.py:469
  3.1 16.8 %all-to-all-start = ((f32[32,34,1,128]{3,2,1,0:T(1,128)}), f32[32,34,1,128]{3,2,1,0:T(1,128)S(1)}, u32[]{:S(2)}, u32[]{:S(2)}) async-start(f32[32,34,1,128]{3,2,1,0:T(1,128)} %bitcast.33), calls=%async_computation | async-start | bytes 1114112 | tf_op jit(solution)/shard_map/all_to_all | solution.py:543
  19.9 0.7 constant_dynamic-slice_fusion.row_ref
  20.6 34.2 %all-to-all-done = f32[32,34,1,128]{3,2,1,0:T(1,128)S(1)} async-done(((f32[32,34,1,128]{3,2,1,0:T(1,128)}), f32[32,34,1,128]{3,2,1,0:T(1,128)S(1)}, u32[]{:S(2)}, u32[]{:S(2)}) %all-to-all-start) | async-done | bytes 557088 | tf_op jit(solution)/shard_map/all_to_all | solution.py:543
  54.7 0.0 copy-done.5
  54.8 0.0 copy-done.4
  54.8 0.0 copy-done
  54.8 1.5 %forward_mass.1 = (f32[416,512]{1,0:T(8,128)S(1)}, f32[136,128]{1,0:T(8,128)S(1)}, f32[136,128]{1,0:T(8,128)S(1)}) custom-call(f32[1088,128]{1,0:T(8,128)S(1)} %bitcast.23, f32[768,512]{1,0:T(8,128)S(1)} %copy-done, f32[34,384]{1,0:T(8,128)S(1)} %copy-done.4, f32[51,256]{1,0:T(8,128)S(1)} %copy-done.5, f32[1,8,128]{2,1,0:T(8,128)S(1)} %constant_dynamic-slice_fusion.row_ref), custom_call_target="tpu_custom_call" | custom-call | flops 654311424 | bytes 1703936 | tf_op jit(solution)/shard_map/forward_mass/pallas_call | solution.py:488
  56.3 2.2 %collective-permute-start = (f32[136,128]{1,0:T(8,128)S(1)}, f32[136,128]{1,0:T(8,128)S(1)}, u32[]{:S(2)}, u32[]{:S(2)}) collective-permute-start(f32[136,128]{1,0:T(8,128)S(1)} %get-tuple-element.14), channel_id=1, source_target_pairs={{16,32},{48,64},{80,96},{112,128},{144,160},{176,192},{208,224},{2... | collective-permute-start | bytes 208904 | tf_op jit(solution)/shard_map/ppermute | solution.py:556
  58.5 1.9 %collective-permute-start.1 = (f32[136,128]{1,0:T(8,128)S(1)}, f32[136,128]{1,0:T(8,128)S(1)}, u32[]{:S(2)}, u32[]{:S(2)}) collective-permute-start(f32[136,128]{1,0:T(8,128)S(1)} %get-tuple-element.15), channel_id=1, source_target_pairs={{0,16},{32,48},{64,80},{96,112},{128,144},{160,176},{192,208},{224... | collective-permute-start | bytes 208904 | tf_op jit(solution)/shard_map/ppermute | solution.py:557
  60.5 0.8 forward_wind.1
  61.2 0.7 collective-permute-done.far_ref
  61.9 0.0 collective-permute-done.1.near_ref
  61.9 0.0 copy-start.1
  61.9 0.0 copy-start.2
  62.0 1.6 %inverse.1 = f32[1088,128]{1,0:T(8,128)S(1)} custom-call(f32[416,512]{1,0:T(8,128)S(1)} %get-tuple-element.11.spec_ref, f32[272,512]{1,0:T(8,128)S(1)} %get-tuple-element.12.wind_ref, f32[136,256]{1,0:T(8,128)S(1)} %get-tuple-element.13.damp_ref, f32[136,128]{1,0:T(8,128)S(1)} %collective-permute-done.far_ref, ...), custom_call_target="tpu_custom_call" | custom-call | flops 654311424 | bytes 1703936 | tf_op jit(solution)/shard_map/inverse/pallas_call | solution.py:514
  63.6 38.8 %all_to_all.10 = f32[32,34,1,128]{3,2,1,0:T(1,128)S(1)} all-to-all(f32[32,34,1,128]{3,2,1,0:T(1,128)S(1)} %bitcast.26), channel_id=1, replica_groups=mesh['lon'=32,'lat'=16] {'lon'}, dimensions={0} | all-to-all | bytes 1114112 | tf_op jit(solution)/shard_map/all_to_all | solution.py:543
  102.4 0.0 copy-done.1
  102.4 0.0 copy-done.2
  102.4 0.0 copy-done.3
  102.4 1.1 %unpack.1 = (f32[360,128]{1,0:T(8,128)}, f32[360,128]{1,0:T(8,128)}, f32[360,128]{1,0:T(8,128)}) custom-call(s32[1]{0:T(128)} %bitcast.turn_ref, f32[1088,128]{1,0:T(8,128)S(1)} %bitcast.25, f32[360,128]{1,0:T(8,128)S(1)} %bitcast.28, f32[360,128]{1,0:T(8,128)S(1)} %bitcast.30, f32[360,128]{1,0:T(8,128)S(1)} %bitcast.32), custom_call_target="tpu_custom_call" | custom-call | tf_op jit(solution)/shard_map/unpack/pallas_call | solution.py:527
  (1 shorter events, 0.0 us)
Async XLA Ops:
  0.6 54.1 %copy-start.5 = (f32[51,256]{1,0:T(8,128)S(1)}, f32[51,256]{1,0:T(8,128)}, u32[]{:S(2)}) copy-start(f32[51,256]{1,0:T(8,128)} %constant.48.clone.wave_ref) | copy-start | bytes 156676
  0.6 54.1 %copy-start.4 = (f32[34,384]{1,0:T(8,128)S(1)}, f32[34,384]{1,0:T(8,128)}, u32[]{:S(2)}) copy-start(f32[34,384]{1,0:T(8,128)} %constant.47.clone.twiddle_ref) | copy-start | bytes 156676
  0.7 54.1 %copy-start = (f32[768,512]{1,0:T(8,128)S(1)}, f32[768,512]{1,0:T(8,128)}, u32[]{:S(2)}) copy-start(f32[768,512]{1,0:T(8,128)} %constant.46.clone.table_ref) | copy-start | bytes 4718596
  3.1 51.7 %all-to-all-start = ((f32[32,34,1,128]{3,2,1,0:T(1,128)}), f32[32,34,1,128]{3,2,1,0:T(1,128)S(1)}, u32[]{:S(2)}, u32[]{:S(2)}) async-start(f32[32,34,1,128]{3,2,1,0:T(1,128)} %bitcast.33), calls=%async_computation | async-start | bytes 1114112 | tf_op jit(solution)/shard_map/all_to_all | solution.py:543
  56.3 5.6 %collective-permute-start = (f32[136,128]{1,0:T(8,128)S(1)}, f32[136,128]{1,0:T(8,128)S(1)}, u32[]{:S(2)}, u32[]{:S(2)}) collective-permute-start(f32[136,128]{1,0:T(8,128)S(1)} %get-tuple-element.14), channel_id=1, source_target_pairs={{16,32},{48,64},{80,96},{112,128},{144,160},{176,192},{208,224},{2... | collective-permute-start | bytes 208904 | tf_op jit(solution)/shard_map/ppermute | solution.py:556
  58.5 3.4 %collective-permute-start.1 = (f32[136,128]{1,0:T(8,128)S(1)}, f32[136,128]{1,0:T(8,128)S(1)}, u32[]{:S(2)}, u32[]{:S(2)}) collective-permute-start(f32[136,128]{1,0:T(8,128)S(1)} %get-tuple-element.15), channel_id=1, source_target_pairs={{0,16},{32,48},{64,80},{96,112},{128,144},{160,176},{192,208},{224... | collective-permute-start | bytes 208904 | tf_op jit(solution)/shard_map/ppermute | solution.py:557
  61.9 40.5 %copy-start.1 = (f32[2,180,128]{2,0,1:T(2,128)S(1)}, f32[2,180,128]{2,0,1:T(2,128)}, u32[]{:S(2)}) copy-start(f32[2,180,128]{2,0,1:T(2,128)} %param.13) | copy-start | bytes 552964
  61.9 40.5 %copy-start.2 = (f32[2,180,128]{2,0,1:T(2,128)S(1)}, f32[2,180,128]{2,0,1:T(2,128)}, u32[]{:S(2)}) copy-start(f32[2,180,128]{2,0,1:T(2,128)} %param.14) | copy-start | bytes 552964
  61.9 40.5 %copy-start.3 = (f32[2,180,128]{2,0,1:T(2,128)S(1)}, f32[2,180,128]{2,0,1:T(2,128)}, u32[]{:S(2)}) copy-start(f32[2,180,128]{2,0,1:T(2,128)} %param.15) | copy-start | bytes 552964

commit v7 on v6

--- a/solution.py
+++ b/solution.py
@@ -154,8 +154,12 @@
     return pairs + pltpu.roll(pairs, size - 2, 0)
 
 
+def holder(level, r, turned):
+    return level * 16 + (15 - r if turned else r)
+
+
 def spot(level, r, turned):
-    return CHUNK * (level * 16 + (15 - r if turned else r))
+    return CHUNK * holder(level, r, turned)
 
 
 def east(level, start, count):
@@ -448,7 +452,7 @@
 
 
 def place(level, r, lat):
-    return (level * 16 + (15 - r if lat % 2 else r)) * 16 + lat
+    return holder(level, r, lat % 2 == 0) * 16 + lat
 
 
 def swaps(odd):
@@ -546,7 +550,7 @@
 
 def step(u, v, h):
     lat = lax.axis_index("lat")
-    turned = lat % 2
+    turned = 1 - lat % 2
     r = lax.axis_index("lon") % 16
     row = row_of(lat * 16 + jnp.where(turned == 1, 15 - r, r))
     turned = turned.reshape(1)

time: 105 us -> 104 us (level); the launches traced: 104 us -> 104 us
  starting transfers between devices: 20.9 us -> 22.5 us
    ppermute x1, starting transfers between devices: 1.92 us -> 3.53 us  [step(): near = lax.ppermute(near, ('lon', 'lat'), swaps(0))]
where the time goes in v7:
time: 104 us
  blocking collectives  37.9 us (36%)
  waiting for transfers between devices  34.3 us (33%)
  starting transfers between devices  22.5 us (22%)
  Pallas kernels  7.52 us (7%)
    all_to_all x1, blocking collectives, exchange(): lax.all_to_all(chunks.reshape(PARTS, CHUNK, 1, LANES), 'lon', 0, 0, tiled...  37.9 us
    all_to_all x1, waiting for transfers between devices, exchange(): lax.all_to_all(chunks.reshape(PARTS, CHUNK, 1, LANES), 'lon', 0, 0, tiled...  34.2 us
    all_to_all x1, starting transfers between devices, exchange(): lax.all_to_all(chunks.reshape(PARTS, CHUNK, 1, LANES), 'lon', 0, 0, tiled...  16.8 us
    ppermute x1, starting transfers between devices, step(): near = lax.ppermute(near, ('lon', 'lat'), swaps(0))  3.53 us
    pallas_call x1, Pallas kernels, pack(): pl.pallas_call(pack_kernel, out_shape=like(PARTS * CHUNK, LANES), in_spec...  2.44 us
    ppermute x1, starting transfers between devices, step(): far = lax.ppermute(far, ('lon', 'lat'), swaps(1))  2.22 us
  transfers between devices with their start and end apart: 3, of which 2 were waited for; matrix products, arithmetic and copies ran while one was open for 1% of the time, Pallas kernels for 1%

profile of v7, /device:TPU:1, one launch (start us, length us, event | category | flops | bytes accessed | tf_op | source)
XLA Modules:
  0.0 103.7 jit_solution(6452969504976218447)
XLA Ops:
  0.6 0.0 copy-start.5
  0.6 0.0 copy-start.4
  0.7 0.0 copy-start
  0.7 2.4 %pack.1 = f32[1088,128]{1,0:T(8,128)} custom-call(s32[1]{0:T(128)} %bitcast.turn_ref, f32[360,128]{1,0:T(8,128)} %bitcast.27, f32[360,128]{1,0:T(8,128)} %bitcast.29, f32[360,128]{1,0:T(8,128)} %bitcast.31), custom_call_target="tpu_custom_call" | custom-call | tf_op jit(solution)/shard_map/pack/pallas_call | solution.py:473
  3.1 16.8 %all-to-all-start = ((f32[32,34,1,128]{3,2,1,0:T(1,128)}), f32[32,34,1,128]{3,2,1,0:T(1,128)S(1)}, u32[]{:S(2)}, u32[]{:S(2)}) async-start(f32[32,34,1,128]{3,2,1,0:T(1,128)} %bitcast.33), calls=%async_computation | async-start | bytes 1114112 | tf_op jit(solution)/shard_map/all_to_all | solution.py:547
  19.9 0.7 constant_dynamic-slice_fusion.row_ref
  20.6 34.2 %all-to-all-done = f32[32,34,1,128]{3,2,1,0:T(1,128)S(1)} async-done(((f32[32,34,1,128]{3,2,1,0:T(1,128)}), f32[32,34,1,128]{3,2,1,0:T(1,128)S(1)}, u32[]{:S(2)}, u32[]{:S(2)}) %all-to-all-start) | async-done | bytes 557088 | tf_op jit(solution)/shard_map/all_to_all | solution.py:547
  54.8 0.0 copy-done.5
  54.8 0.0 copy-done.4
  54.8 0.0 copy-done
  54.8 1.5 %forward_mass.1 = (f32[416,512]{1,0:T(8,128)S(1)}, f32[136,128]{1,0:T(8,128)S(1)}, f32[136,128]{1,0:T(8,128)S(1)}) custom-call(f32[1088,128]{1,0:T(8,128)S(1)} %bitcast.23, f32[768,512]{1,0:T(8,128)S(1)} %copy-done, f32[34,384]{1,0:T(8,128)S(1)} %copy-done.4, f32[51,256]{1,0:T(8,128)S(1)} %copy-done.5, f32[1,8,128]{2,1,0:T(8,128)S(1)} %constant_dynamic-slice_fusion.row_ref), custom_call_target="tpu_custom_call" | custom-call | flops 654311424 | bytes 1703936 | tf_op jit(solution)/shard_map/forward_mass/pallas_call | solution.py:492
  56.4 2.2 %collective-permute-start = (f32[136,128]{1,0:T(8,128)S(1)}, f32[136,128]{1,0:T(8,128)S(1)}, u32[]{:S(2)}, u32[]{:S(2)}) collective-permute-start(f32[136,128]{1,0:T(8,128)S(1)} %get-tuple-element.14), channel_id=1, source_target_pairs={{224,208},{192,176},{160,144},{128,112},{96,80},{64,48},{32,16},{0... | collective-permute-start | bytes 208904 | tf_op jit(solution)/shard_map/ppermute | solution.py:560
  58.6 3.5 %collective-permute-start.1 = (f32[136,128]{1,0:T(8,128)S(1)}, f32[136,128]{1,0:T(8,128)S(1)}, u32[]{:S(2)}, u32[]{:S(2)}) collective-permute-start(f32[136,128]{1,0:T(8,128)S(1)} %get-tuple-element.15), channel_id=1, source_target_pairs={{240,224},{208,192},{176,160},{144,128},{112,96},{80,64},{48,32},{... | collective-permute-start | bytes 208904 | tf_op jit(solution)/shard_map/ppermute | solution.py:561
  62.1 0.8 forward_wind.1
  62.9 0.0 collective-permute-done.far_ref
  62.9 0.1 collective-permute-done.1.near_ref
  63.0 0.0 copy-start.1
  63.0 0.0 copy-start.2
  63.0 1.6 %inverse.1 = f32[1088,128]{1,0:T(8,128)S(1)} custom-call(f32[416,512]{1,0:T(8,128)S(1)} %get-tuple-element.11.spec_ref, f32[272,512]{1,0:T(8,128)S(1)} %get-tuple-element.12.wind_ref, f32[136,256]{1,0:T(8,128)S(1)} %get-tuple-element.13.damp_ref, f32[136,128]{1,0:T(8,128)S(1)} %collective-permute-done.far_ref, ...), custom_call_target="tpu_custom_call" | custom-call | flops 654311424 | bytes 1703936 | tf_op jit(solution)/shard_map/inverse/pallas_call | solution.py:518
  64.6 37.9 %all_to_all.10 = f32[32,34,1,128]{3,2,1,0:T(1,128)S(1)} all-to-all(f32[32,34,1,128]{3,2,1,0:T(1,128)S(1)} %bitcast.26), channel_id=1, replica_groups=mesh['lon'=32,'lat'=16] {'lon'}, dimensions={0} | all-to-all | bytes 1114112 | tf_op jit(solution)/shard_map/all_to_all | solution.py:547
  102.6 0.0 copy-done.1
  102.6 0.0 copy-done.2
  102.6 0.0 copy-done.3
  102.6 1.2 %unpack.1 = (f32[360,128]{1,0:T(8,128)}, f32[360,128]{1,0:T(8,128)}, f32[360,128]{1,0:T(8,128)}) custom-call(s32[1]{0:T(128)} %bitcast.turn_ref, f32[1088,128]{1,0:T(8,128)S(1)} %bitcast.25, f32[360,128]{1,0:T(8,128)S(1)} %bitcast.28, f32[360,128]{1,0:T(8,128)S(1)} %bitcast.30, f32[360,128]{1,0:T(8,128)S(1)} %bitcast.32), custom_call_target="tpu_custom_call" | custom-call | tf_op jit(solution)/shard_map/unpack/pallas_call | solution.py:531
  (1 shorter events, 0.0 us)
Async XLA Ops:
  0.6 54.2 %copy-start.5 = (f32[51,256]{1,0:T(8,128)S(1)}, f32[51,256]{1,0:T(8,128)}, u32[]{:S(2)}) copy-start(f32[51,256]{1,0:T(8,128)} %constant.48.clone.wave_ref) | copy-start | bytes 156676
  0.6 54.2 %copy-start.4 = (f32[34,384]{1,0:T(8,128)S(1)}, f32[34,384]{1,0:T(8,128)}, u32[]{:S(2)}) copy-start(f32[34,384]{1,0:T(8,128)} %constant.47.clone.twiddle_ref) | copy-start | bytes 156676
  0.7 54.1 %copy-start = (f32[768,512]{1,0:T(8,128)S(1)}, f32[768,512]{1,0:T(8,128)}, u32[]{:S(2)}) copy-start(f32[768,512]{1,0:T(8,128)} %constant.46.clone.table_ref) | copy-start | bytes 4718596
  3.1 51.7 %all-to-all-start = ((f32[32,34,1,128]{3,2,1,0:T(1,128)}), f32[32,34,1,128]{3,2,1,0:T(1,128)S(1)}, u32[]{:S(2)}, u32[]{:S(2)}) async-start(f32[32,34,1,128]{3,2,1,0:T(1,128)} %bitcast.33), calls=%async_computation | async-start | bytes 1114112 | tf_op jit(solution)/shard_map/all_to_all | solution.py:547
  56.4 6.5 %collective-permute-start = (f32[136,128]{1,0:T(8,128)S(1)}, f32[136,128]{1,0:T(8,128)S(1)}, u32[]{:S(2)}, u32[]{:S(2)}) collective-permute-start(f32[136,128]{1,0:T(8,128)S(1)} %get-tuple-element.14), channel_id=1, source_target_pairs={{224,208},{192,176},{160,144},{128,112},{96,80},{64,48},{32,16},{0... | collective-permute-start | bytes 208904 | tf_op jit(solution)/shard_map/ppermute | solution.py:560
  58.6 4.4 %collective-permute-start.1 = (f32[136,128]{1,0:T(8,128)S(1)}, f32[136,128]{1,0:T(8,128)S(1)}, u32[]{:S(2)}, u32[]{:S(2)}) collective-permute-start(f32[136,128]{1,0:T(8,128)S(1)} %get-tuple-element.15), channel_id=1, source_target_pairs={{240,224},{208,192},{176,160},{144,128},{112,96},{80,64},{48,32},{... | collective-permute-start | bytes 208904 | tf_op jit(solution)/shard_map/ppermute | solution.py:561
  63.0 39.6 %copy-start.1 = (f32[2,180,128]{2,0,1:T(2,128)S(1)}, f32[2,180,128]{2,0,1:T(2,128)}, u32[]{:S(2)}) copy-start(f32[2,180,128]{2,0,1:T(2,128)} %param.13) | copy-start | bytes 552964
  63.0 39.6 %copy-start.2 = (f32[2,180,128]{2,0,1:T(2,128)S(1)}, f32[2,180,128]{2,0,1:T(2,128)}, u32[]{:S(2)}) copy-start(f32[2,180,128]{2,0,1:T(2,128)} %param.14) | copy-start | bytes 552964
  63.0 39.6 %copy-start.3 = (f32[2,180,128]{2,0,1:T(2,128)S(1)}, f32[2,180,128]{2,0,1:T(2,128)}, u32[]{:S(2)}) copy-start(f32[2,180,128]{2,0,1:T(2,128)} %param.15) | copy-start | bytes 552964

commit v8 on v7

--- a/solution.py
+++ b/solution.py
@@ -82,6 +82,8 @@
 
 
 PUSH_COEF = 0.25 / 2.0
+FIRST = 20
+ORDER = [(i + FIRST) % PARTS for i in range(PARTS)]
 
 
 def add(x, y):
@@ -154,12 +156,16 @@
     return pairs + pltpu.roll(pairs, size - 2, 0)
 
 
+def chunk_at(lon):
+    return CHUNK * ORDER.index(lon)
+
+
 def holder(level, r, turned):
     return level * 16 + (15 - r if turned else r)
 
 
 def spot(level, r, turned):
-    return CHUNK * holder(level, r, turned)
+    return chunk_at(holder(level, r, turned))
 
 
 def east(level, start, count):
@@ -174,10 +180,12 @@
     for move in moves:
         move.start()
     last_ref[...] = jnp.zeros_like(last_ref)
-    for move in moves:
+    whole = []
+    for move, ref in zip(moves, (u_ref, v_ref, h_ref)):
         move.wait()
+        whole.append([ref[east(level, 0, LANES), :].T for level in range(2)])
     for level in range(2):
-        tiles = [ref[east(level, 0, LANES), :].T for ref in (u_ref, v_ref, h_ref)]
+        tiles = [pair[level] for pair in whole]
         tail_ref[:TAIL, :] = u_ref[east(level, LANES, TAIL), :]
         tail_ref[TAIL:HALF, :] = h_ref[east(level, LANES, SIDE), :]
         tail_ref[HALF : HALF + TAIL, :] = v_ref[east(level, LANES, TAIL), :]
@@ -199,7 +207,9 @@
                     out_ref[at + 4 * ROWS : at + CHUNK, :] = folded[2 * r : 2 * r + 2]
 
 
-def unpack_kernel(turn_ref, in_ref, u_ref, v_ref, h_ref, u_out, v_out, h_out, tile_ref):
+def unpack_kernel(
+    turn_ref, in_ref, u_ref, v_ref, h_ref, u_hbm, v_hbm, h_hbm, u_out, v_out, h_out, tile_ref, sems
+):
     for level in range(2):
         for turned in (False, True):
 
@@ -207,29 +217,36 @@
             def _():
                 for r in range(16):
                     at = spot(level, r, turned)
+                    here = slice(r * ROWS, (r + 1) * ROWS)
                     for f in range(4):
-                        tile_ref[f, r * ROWS : (r + 1) * ROWS, :] = in_ref[at + f * ROWS : at + (f + 1) * ROWS, :]
+                        tile_ref[level, f, here, :] = in_ref[at + f * ROWS : at + (f + 1) * ROWS, :]
                     for t in range(2):
                         row = in_ref[at + 4 * ROWS + t : at + 4 * ROWS + t + 1, :]
-                        tile_ref[4, r * ROWS + 4 * t : r * ROWS + 4 * t + 4, :] = jnp.broadcast_to(row, (4, LANES))
-
-        for f, (ref, out) in enumerate(((u_ref, u_out), (v_ref, v_out), (h_ref, h_out))):
-            here = east(level, 0, LANES)
-            out[here, :] = ref[here, :] + tile_ref[f].T
-        mixed, quarters = tile_ref[3].T, tile_ref[4].T
-        group = lane((LAST, LANES)) % 4
-        last = quarters[:LAST]
-        for g in range(1, 4):
-            last = jnp.where(group == g, quarters[g * QUARTER : g * QUARTER + LAST], last)
-        for ref, out, start, change in (
-            (u_ref, u_out, LANES, mixed[:TAIL]),
-            (h_ref, h_out, LANES, mixed[TAIL:HALF]),
-            (v_ref, v_out, LANES, mixed[HALF : HALF + TAIL]),
-            (h_ref, h_out, LANES + SIDE, mixed[HALF + TAIL :]),
-            (h_ref, h_out, SEG - LAST, last),
-        ):
-            here = east(level, start, change.shape[0])
-            out[here, :] = ref[here, :] + change
+                        here = slice(r * ROWS + 4 * t, r * ROWS + 4 * t + 4)
+                        tile_ref[level, 4, here, :] = jnp.broadcast_to(row, (4, LANES))
+
+    mixed = [tile_ref[level, 3].T for level in range(2)]
+    moves = []
+    for f, (ref, out, hbm) in enumerate(((u_ref, u_out, u_hbm), (v_ref, v_out, v_hbm), (h_ref, h_out, h_hbm))):
+        for level in range(2):
+            if f < 2:
+                changes = ((LANES, mixed[level][f * HALF : f * HALF + TAIL]),)
+            else:
+                quarters = tile_ref[level, 4].T
+                group = lane((LAST, LANES)) % 4
+                last = quarters[:LAST]
+                for g in range(1, 4):
+                    last = jnp.where(group == g, quarters[g * QUARTER : g * QUARTER + LAST], last)
+                changes = (
+                    (LANES, mixed[level][TAIL:HALF]), (LANES + SIDE, mixed[level][HALF + TAIL :]), (SEG - LAST, last)
+                )
+            for start, change in ((0, tile_ref[level, f].T), *changes):
+                here = east(level, start, change.shape[0])
+                out[here, :] = ref[here, :] + change
+        moves.append(pltpu.make_async_copy(out, hbm, sems.at[f]))
+        moves[-1].start()
+    for move in moves:
+        move.wait()
 
 
 def halves(x):
@@ -241,7 +258,7 @@
     def product(a, b):
         return lax.dot_general(a, b, (((1,), (contract,)), ((), ())), preferred_element_type=jnp.float32)
 
-    (high, low), (table_high, table_low) = halves(x), halves(table)
+    (high, low), (table_high, table_low) = halves(x), table
     return product(high, table_high) + (product(high, table_low) + product(low, table_high))
 
 
@@ -252,7 +269,7 @@
     return -(-fields * BLOCK // 16) * 16
 
 
-def transform(columns, table_ref, twiddle_ref, spec_ref, left_ref):
+def transform(columns, high_ref, low_ref, twiddle_ref, spec_ref, left_ref):
     at = lane((ROWS, LANES))
     own = (at < TAIL, (at >= HALF) & (at < HALF + TAIL))
     for get, part, fields in columns:
@@ -272,12 +289,13 @@
                 else:
                     left_ref[rows, lanes] = jnp.where(own[half], new_re, 0.0)
                     left_ref[rows, late] = jnp.where(own[half], new_im, 0.0)
-    spec_ref[...] = dot(left_ref[...], table_ref[: 2 * WIDE, :], 0)
+    table = high_ref[: 2 * WIDE, :], low_ref[: 2 * WIDE, :]
+    spec_ref[...] = dot(left_ref[...], table, 0)
 
 
 def tiles_of(x_ref):
     def tile(f):
-        return lambda a: x_ref[a * CHUNK + f * ROWS : a * CHUNK + (f + 1) * ROWS, :]
+        return lambda a: x_ref[chunk_at(a) + f * ROWS : chunk_at(a) + (f + 1) * ROWS, :]
 
     return tile
 
@@ -286,7 +304,7 @@
     at = lane((ROWS, LANES))
     place_of_four = lax.broadcasted_iota(jnp.int32, at.shape, 0) % 4
     for a in range(PARTS):
-        base = a * CHUNK + 3 * ROWS
+        base = chunk_at(a) + 3 * ROWS
         mixed = x_ref[base : base + ROWS, :]
         rows = [jnp.broadcast_to(x_ref[base + ROWS + t : base + ROWS + t + 1, :], (4, LANES)) for t in range(2)]
         quarters, last = jnp.concatenate(rows, axis=0), None
@@ -302,12 +320,6 @@
 U, V = range(2)
 
 
-def damping(row, wave_ref, k1):
-    ratio2 = row[:, 0:1]
-    here, there = wave_ref[k1 : k1 + 1, :], wave_ref[WAVES + k1 : WAVES + k1 + 1, :]
-    return 0.5 * (ratio2 / jnp.maximum(here, ratio2) + ratio2 / jnp.maximum(there, ratio2))
-
-
 REAL, IMAG = slice(0, WIDE), slice(WIDE, 2 * WIDE)
 
 
@@ -315,16 +327,28 @@
     return slice(f * BLOCK + k1 * ROWS, f * BLOCK + (k1 + 1) * ROWS)
 
 
-def wind_kernel(x_ref, table_ref, twiddle_ref, wave_ref, row_ref, spec_ref, damp_ref, left_ref):
+def factor_kernel(table_ref, wave_ref, row_ref, high_ref, low_ref, gain_ref, flux_ref, turn_ref, across_ref, along_ref):
+    high_ref[...], low_ref[...] = halves(table_ref[...])
+    row = row_ref[0]
+    ratio2, x_coef, rotation, coslat = row[:, 0:1], row[:, 1:2], row[:, 3:4], row[:, 4:5]
+    for k1 in range(WAVES):
+        here, there, slope = (wave_ref[i * WAVES + k1 : i * WAVES + k1 + 1, :] for i in range(3))
+        damp = 0.5 * (ratio2 / jnp.maximum(here, ratio2) + ratio2 / jnp.maximum(there, ratio2))
+        across = x_coef * slope * damp
+        gain_ref[rows_of(0, k1), :] = across
+        flux_ref[rows_of(0, k1), :] = damp * coslat
+        damp = SCALE * damp
+        turn_ref[rows_of(0, k1), :] = damp * rotation
+        across_ref[rows_of(0, k1), :] = SCALE * across
+        along_ref[rows_of(0, k1), :] = -PUSH_COEF * damp
+
+
+def wind_kernel(x_ref, high_ref, low_ref, twiddle_ref, turn_ref, spec_ref, left_ref):
     tile = tiles_of(x_ref)
     columns = ((tile(0), 0, ((U, 0),)), (tile(1), 0, ((V, 0),)), (tile(3), 1, ((U, 0), (V, 1))))
-    transform(columns, table_ref, twiddle_ref, spec_ref, left_ref)
-    row = row_ref[0]
-    rotation = row[:, 3:4]
+    transform(columns, high_ref, low_ref, twiddle_ref, spec_ref, left_ref)
     for k1 in range(WAVES):
-        damp = SCALE * damping(row, wave_ref, k1)
-        damp_ref[rows_of(0, k1), :] = damp
-        turn = damp * rotation
+        turn = turn_ref[rows_of(0, k1), :]
         for span in (REAL, IMAG):
             spec_ref[rows_of(U, k1), span] = -turn * spec_ref[rows_of(U, k1), span]
             spec_ref[rows_of(V, k1), span] = turn * spec_ref[rows_of(V, k1), span]
@@ -343,7 +367,7 @@
 
 
 def mass_kernel(
-    x_ref, table_ref, twiddle_ref, wave_ref, row_ref, spec_ref, far_ref, near_ref, left_ref, tails_ref
+    x_ref, high_ref, low_ref, twiddle_ref, gain_ref, scale_ref, row_ref, spec_ref, far_ref, near_ref, left_ref, tails_ref
 ):
     gather_tails(x_ref, tails_ref)
     tile = tiles_of(x_ref)
@@ -361,15 +385,13 @@
         (tail, 1, ((H, 0),)),
         (product(3, tail), 1, ((UH, 0), (VH, 1))),
     )
-    transform(columns, table_ref, twiddle_ref, spec_ref, left_ref)
+    transform(columns, high_ref, low_ref, twiddle_ref, spec_ref, left_ref)
     row = row_ref[0]
-    x_coef, y_coef, coslat, odd = row[:, 1:2], row[:, 2:3], row[:, 4:5], row[:4, 7:8] > 0.5
+    y_coef, odd = row[:, 2:3], row[:4, 7:8] > 0.5
     for k1 in range(WAVES):
-        damp = damping(row, wave_ref, k1)
-        across = x_coef * wave_ref[2 * WAVES + k1 : 2 * WAVES + k1 + 1, :] * damp
+        across, scale = gain_ref[rows_of(0, k1), :], scale_ref[rows_of(0, k1), :]
         gain_re = across * spec_ref[rows_of(UH, k1), IMAG]
         gain_im = -across * spec_ref[rows_of(UH, k1), REAL]
-        scale = damp * coslat
         up, down = [], []
         for span, gain in ((REAL, gain_re), (IMAG, gain_im)):
             spec_ref[rows_of(UH, k1), span] = gain
@@ -384,19 +406,17 @@
 
 
 def inverse_kernel(
-    spec_ref, wind_ref, damp_ref, far_ref, near_ref, table_ref, twiddle_ref, wave_ref, row_ref, out_ref, left_ref,
-    right_ref, last_ref
+    spec_ref, wind_ref, far_ref, near_ref, high_ref, low_ref, twiddle_ref, across_ref, along_ref, row_ref, out_ref,
+    left_ref, right_ref, last_ref
 ):
     row = row_ref[0]
-    x_coef, y_coef = row[:, 1:2], row[:, 2:3]
+    y_coef = row[:, 2:3]
     y_below, y_above = row[0:1, 5:6], row[0:1, 6:7]
     odd = row[:, 7:8] > 0.5
     for k1 in range(WAVES):
         near, far = near_ref[rows_of(0, k1), :], far_ref[rows_of(0, k1), :]
         below, above = from_message(jnp.where(odd, near, far)), from_message(jnp.where(odd, far, near))
-        damp = damp_ref[rows_of(0, k1), :]
-        across = damp * x_coef * wave_ref[2 * WAVES + k1 : 2 * WAVES + k1 + 1, :]
-        along = -PUSH_COEF * damp
+        across, along = across_ref[rows_of(0, k1), :], along_ref[rows_of(0, k1), :]
         mass = []
         for part, span in enumerate((REAL, IMAG)):
             flux = spec_ref[rows_of(VH, k1), span]
@@ -414,8 +434,8 @@
             left_ref[rows_of(0, k1), span] = SCALE * change
         left_ref[rows_of(1, k1), REAL] = across * mass[1] + wind_ref[rows_of(V, k1), REAL]
         left_ref[rows_of(1, k1), IMAG] = wind_ref[rows_of(V, k1), IMAG] - across * mass[0]
-    right_ref[...] = dot(left_ref[...], table_ref[: 2 * WIDE, :], 1)
-    last_ref[...] = dot(left_ref[:BLOCK, :], table_ref[2 * WIDE :, :], 1)
+    right_ref[...] = dot(left_ref[...], (high_ref[: 2 * WIDE, :], low_ref[: 2 * WIDE, :]), 1)
+    last_ref[...] = dot(left_ref[:BLOCK, :], (high_ref[2 * WIDE :, :], low_ref[2 * WIDE :, :]), 1)
     at = lane((ROWS, LANES))
     for f, part, fields in ((0, 0, (1,)), (1, 0, (2,)), (2, 0, (0,)), (3, 1, (0, 1, 2)), (4, 2, (0,))):
         lanes = slice(part * LANES, (part + 1) * LANES)
@@ -433,7 +453,7 @@
             re, im = re[0], im[0]
             waves.append((re * cos - im * sin, None if k1 in (0, WAVES - 1) else im * cos + re * sin))
         for a, value in enumerate(real_ifft(waves)):
-            start = a * CHUNK + f * ROWS
+            start = chunk_at(a) + f * ROWS
             if f == 4:
                 value = fold(value)
                 value = jnp.concatenate([value[0:1], value[4:5]], axis=0)
@@ -488,43 +508,56 @@
     return pl.CostEstimate(flops=6 * size * 2 * WIDE, bytes_accessed=8 * size, transcendentals=0)
 
 
-def forward_mass(whole, row):
+def factors(row):
+    table = jax.ShapeDtypeStruct((6 * LANES, 2 * WIDE), jnp.bfloat16)
+    return pl.pallas_call(
+        factor_kernel,
+        out_shape=(table, table) + (like(BLOCK, WIDE),) * 5,
+        in_specs=[in_vmem()] * 3,
+        out_specs=(in_vmem(),) * 7,
+        compiler_params=PARAMS,
+        cost_estimate=pl.CostEstimate(flops=2**24, bytes_accessed=2**24, transcendentals=0),
+        name="factors",
+    )(dft_table(), wave_table(), row)
+
+
+def forward_mass(whole, high, low, gain, scale, row):
     return pl.pallas_call(
         mass_kernel,
         out_shape=(like(padded(3), 2 * WIDE), like(BLOCK, LANES), like(BLOCK, LANES)),
-        in_specs=[in_vmem()] * 5,
+        in_specs=[in_vmem()] * 7,
         out_specs=(in_vmem(),) * 3,
         scratch_shapes=[pltpu.VMEM((padded(3), 2 * WIDE), jnp.float32), pltpu.VMEM((PARTS * ROWS, LANES), jnp.float32)],
         compiler_params=PARAMS,
         cost_estimate=cost(3),
         name="forward_mass",
-    )(whole, dft_table(), twiddle_table(), wave_table(), row)
-
-
-def forward_wind(whole, row):
+    )(whole, high, low, twiddle_table(), gain, scale, row)
+
+
+def forward_wind(whole, high, low, turn):
     return pl.pallas_call(
         wind_kernel,
-        out_shape=(like(padded(2), 2 * WIDE), like(BLOCK, WIDE)),
+        out_shape=like(padded(2), 2 * WIDE),
         in_specs=[in_vmem()] * 5,
-        out_specs=(in_vmem(),) * 2,
+        out_specs=in_vmem(),
         scratch_shapes=[pltpu.VMEM((padded(2), 2 * WIDE), jnp.float32)],
         compiler_params=PARAMS,
         cost_estimate=cost(2),
         name="forward_wind",
-    )(whole, dft_table(), twiddle_table(), wave_table(), row)
-
-
-def inverse(spec, wind, damp, far, near, row):
+    )(whole, high, low, twiddle_table(), turn)
+
+
+def inverse(spec, wind, far, near, high, low, across, along, row):
     return pl.pallas_call(
         inverse_kernel,
         out_shape=like(PARTS * CHUNK, LANES),
-        in_specs=[in_vmem()] * 9,
+        in_specs=[in_vmem()] * 10,
         out_specs=in_vmem(),
         scratch_shapes=[pltpu.VMEM((padded(3), 2 * WIDE), jnp.float32)] * 2 + [pltpu.VMEM((BLOCK, WIDE), jnp.float32)],
         compiler_params=PARAMS,
         cost_estimate=cost(3),
         name="inverse",
-    )(spec, wind, damp, far, near, dft_table(), twiddle_table(), wave_table(), row)
+    )(spec, wind, far, near, high, low, twiddle_table(), across, along, row)
 
 
 def unpack(turned, back, u, v, h):
@@ -532,8 +565,9 @@
         unpack_kernel,
         out_shape=(like(2 * SEG, LANES),) * 3,
         in_specs=[in_smem()] + [in_vmem()] * 4,
-        out_specs=(in_vmem(),) * 3,
-        scratch_shapes=[pltpu.VMEM((5, LANES, LANES), jnp.float32)],
+        out_specs=(pl.BlockSpec(memory_space=pltpu.HBM),) * 3,
+        scratch_shapes=[pltpu.VMEM((2 * SEG, LANES), jnp.float32)] * 3
+        + [pltpu.VMEM((2, 5, LANES, LANES), jnp.float32), pltpu.SemaphoreType.DMA((3,))],
         compiler_params=PARAMS,
         name="unpack",
     )(turned, back, u, v, h)
@@ -544,7 +578,7 @@
 
 
 def exchange(chunks):
-    moved = lax.all_to_all(chunks.reshape(PARTS, CHUNK, 1, LANES), "lon", 0, 0, tiled=True)
+    moved = lax.all_to_all(chunks.reshape(PARTS, CHUNK, 1, LANES), "lon", 0, 0, axis_index_groups=[ORDER], tiled=True)
     return moved.reshape(PARTS * CHUNK, LANES)
 
 
@@ -555,12 +589,14 @@
     row = row_of(lat * 16 + jnp.where(turned == 1, 15 - r, r))
     turned = turned.reshape(1)
     u, v, h = (jnp.swapaxes(x, 0, 1).reshape(2 * SEG, LANES) for x in (u, v, h))
+    high, low, gain, scale, turn, across, along = factors(row)
     whole = exchange(pack(turned, u, v, h))
-    spec, far, near = forward_mass(whole, row)
+    spec, far, near = forward_mass(whole, high, low, gain, scale, row)
     far = lax.ppermute(far, ("lon", "lat"), swaps(1))
     near = lax.ppermute(near, ("lon", "lat"), swaps(0))
-    wind, damp = forward_wind(whole, row)
-    outs = unpack(turned, exchange(inverse(spec, wind, damp, far, near, row)), u, v, h)
+    wind = forward_wind(whole, high, low, turn)
+    back = exchange(inverse(spec, wind, far, near, high, low, across, along, row))
+    outs = unpack(turned, back, u, v, h)
     return tuple(jnp.swapaxes(x.reshape(SEG, 2, LANES), 0, 1) for x in outs)
 
 

time: 104 us -> 96.9 us (0.932)
  waiting for transfers between devices: 34.3 us -> 25.1 us
  local copies, waits for them, and re-layouts: 0.73 us -> 2.13 us
    all_to_all x1, waiting for transfers between devices: 34.2 us -> 24 us  [exchange(): lax.all_to_all(chunks.reshape(PARTS, CHUNK, 1, LANES), 'lon', 0, 0, axis_...]
    all_to_all x1, starting transfers between devices: 16.8 us -> 18.5 us  [exchange(): lax.all_to_all(chunks.reshape(PARTS, CHUNK, 1, LANES), 'lon', 0, 0, axis_...]
    ppermute x1, starting transfers between devices: 3.53 us -> 1.95 us  [step(): near = lax.ppermute(near, ('lon', 'lat'), swaps(0))]
    unnamed x12, local copies, waits for them, and re-layouts: 0.03 us -> 1.43 us
where the time goes in v8:
time: 96.9 us; the launch traced here: 96.5 us
  blocking collectives  38.6 us (40%)
  waiting for transfers between devices  25.1 us (26%)
  starting transfers between devices  22.4 us (23%)
  Pallas kernels  7.55 us (8%)
  local copies, waits for them, and re-layouts  2.13 us (2%)
    all_to_all x1, blocking collectives, exchange(): lax.all_to_all(chunks.reshape(PARTS, CHUNK, 1, LANES), 'lon', 0, 0, axis_...  38.6 us
    all_to_all x1, waiting for transfers between devices, exchange(): lax.all_to_all(chunks.reshape(PARTS, CHUNK, 1, LANES), 'lon', 0, 0, axis_...  24 us
    all_to_all x1, starting transfers between devices, exchange(): lax.all_to_all(chunks.reshape(PARTS, CHUNK, 1, LANES), 'lon', 0, 0, axis_...  18.5 us
    pallas_call x1, Pallas kernels, pack(): pl.pallas_call(pack_kernel, out_shape=like(PARTS * CHUNK, LANES), in_spec...  2.27 us
    ppermute x1, starting transfers between devices, step(): near = lax.ppermute(near, ('lon', 'lat'), swaps(0))  1.95 us
  transfers between devices with their start and end apart: 3, of which 2 were waited for; matrix products, arithmetic and copies ran while one was open for 1% of the time, Pallas kernels for 1%

profile of v8, /device:TPU:1, one launch (start us, length us, event | category | flops | bytes accessed | tf_op | source)
XLA Modules:
  0.0 96.5 jit_solution(1584889588800453645)
XLA Ops:
  0.6 0.0 copy-start.5
  0.7 2.3 %pack.1 = f32[1088,128]{1,0:T(8,128)} custom-call(s32[1]{0:T(128)} %bitcast.turn_ref, f32[360,128]{1,0:T(8,128)} %bitcast.27, f32[360,128]{1,0:T(8,128)} %bitcast.29, f32[360,128]{1,0:T(8,128)} %bitcast.31), custom_call_target="tpu_custom_call" | custom-call | tf_op jit(solution)/shard_map/pack/pallas_call | solution.py:493
  2.9 0.0 copy-start.4
  2.9 18.5 %all-to-all-start = ((f32[32,34,1,128]{3,2,1,0:T(1,128)}), f32[32,34,1,128]{3,2,1,0:T(1,128)S(1)}, u32[]{:S(2)}, u32[]{:S(2)}) async-start(f32[32,34,1,128]{3,2,1,0:T(1,128)} %bitcast.33), calls=%async_computation | async-start | bytes 1114112 | tf_op jit(solution)/shard_map/all_to_all | solution.py:581
  21.5 0.7 constant_dynamic-slice_fusion.row_ref
  22.2 0.0 copy-done.5
  22.2 0.0 copy-start
  22.2 1.4 %copy-done = f32[768,512]{1,0:T(8,128)S(1)} copy-done((f32[768,512]{1,0:T(8,128)S(1)}, f32[768,512]{1,0:T(8,128)}, u32[]{:S(2)}) %copy-start) | copy-done | bytes 1572888
  23.6 0.5 factors.1
  24.1 24.0 %all-to-all-done = f32[32,34,1,128]{3,2,1,0:T(1,128)S(1)} async-done(((f32[32,34,1,128]{3,2,1,0:T(1,128)}), f32[32,34,1,128]{3,2,1,0:T(1,128)S(1)}, u32[]{:S(2)}, u32[]{:S(2)}) %all-to-all-start) | async-done | bytes 557088 | tf_op jit(solution)/shard_map/all_to_all | solution.py:581
  48.1 0.0 copy-done.4
  48.1 1.5 %forward_mass.1 = (f32[416,512]{1,0:T(8,128)S(1)}, f32[136,128]{1,0:T(8,128)S(1)}, f32[136,128]{1,0:T(8,128)S(1)}) custom-call(f32[1088,128]{1,0:T(8,128)S(1)} %bitcast.23, bf16[768,512]{1,0:T(8,128)(2,1)S(1)} %get-tuple-element.16.high_ref, bf16[768,512]{1,0:T(8,128)(2,1)S(1)} %get-tuple-element.17.low_ref, f32[34,384]{1,0:T(8,128)S(1)} %copy-done.4, ...), custom_call_target="tpu_custom_call" | custom-call | flops 654311424 | bytes 1703936 | tf_op jit(solution)/shard_map/forward_mass/pallas_call | solution.py:525
  49.6 1.9 %collective-permute-start = (f32[136,128]{1,0:T(8,128)S(1)}, f32[136,128]{1,0:T(8,128)S(1)}, u32[]{:S(2)}, u32[]{:S(2)}) collective-permute-start(f32[136,128]{1,0:T(8,128)S(1)} %get-tuple-element.22), channel_id=1, source_target_pairs={{224,208},{192,176},{160,144},{128,112},{96,80},{64,48},{32,16},{0... | collective-permute-start | bytes 208904 | tf_op jit(solution)/shard_map/ppermute | solution.py:595
  51.5 1.9 %collective-permute-start.1 = (f32[136,128]{1,0:T(8,128)S(1)}, f32[136,128]{1,0:T(8,128)S(1)}, u32[]{:S(2)}, u32[]{:S(2)}) collective-permute-start(f32[136,128]{1,0:T(8,128)S(1)} %get-tuple-element.23), channel_id=1, source_target_pairs={{240,224},{208,192},{176,160},{144,128},{112,96},{80,64},{48,32},{... | collective-permute-start | bytes 208904 | tf_op jit(solution)/shard_map/ppermute | solution.py:596
  53.5 0.7 forward_wind.1.wind_ref
  54.2 1.0 %collective-permute-done.far_ref = f32[136,128]{1,0:T(8,128)S(1)} collective-permute-done((f32[136,128]{1,0:T(8,128)S(1)}, f32[136,128]{1,0:T(8,128)S(1)}, u32[]{:S(2)}, u32[]{:S(2)}) %collective-permute-start) | collective-permute-done | bytes 69664 | tf_op jit(solution)/shard_map/ppermute | solution.py:595
  55.2 0.0 collective-permute-done.1.near_ref
  55.2 0.0 copy-start.1
  55.2 1.6 %inverse.1 = f32[1088,128]{1,0:T(8,128)S(1)} custom-call(f32[416,512]{1,0:T(8,128)S(1)} %get-tuple-element.20.spec_ref, f32[272,512]{1,0:T(8,128)S(1)} %forward_wind.1.wind_ref, f32[136,128]{1,0:T(8,128)S(1)} %collective-permute-done.far_ref, f32[136,128]{1,0:T(8,128)S(1)} %collective-permute-done.1.near_ref, ...), custom_call_target="tpu_custom_call" | custom-call | flops 654311424 | bytes 1703936 | tf_op jit(solution)/shard_map/inverse/pallas_call | solution.py:551
  56.8 38.6 %all_to_all.10 = f32[32,34,1,128]{3,2,1,0:T(1,128)S(1)} all-to-all(f32[32,34,1,128]{3,2,1,0:T(1,128)S(1)} %bitcast.26), channel_id=1, replica_groups={{320,336,352,368,384,400,416,432,448,464,480,496,0,16,32,48,64,80,96,11..., dimensions={0} | all-to-all | bytes 1114112 | tf_op jit(solution)/shard_map/all_to_all | solution.py:581
  95.4 0.0 copy-done.1
  95.5 0.0 copy-done.2
  95.5 0.0 copy-done.3
  95.5 1.0 %unpack.1 = (f32[360,128]{1,0:T(8,128)}, f32[360,128]{1,0:T(8,128)}, f32[360,128]{1,0:T(8,128)}) custom-call(s32[1]{0:T(128)} %bitcast.turn_ref, f32[1088,128]{1,0:T(8,128)S(1)} %bitcast.25, f32[360,128]{1,0:T(8,128)S(1)} %bitcast.28, f32[360,128]{1,0:T(8,128)S(1)} %bitcast.30, f32[360,128]{1,0:T(8,128)S(1)} %bitcast.32), custom_call_target="tpu_custom_call" | custom-call | tf_op jit(solution)/shard_map/unpack/pallas_call | solution.py:564
  (2 shorter events, 0.0 us)
Async XLA Ops:
  0.6 21.5 %copy-start.5 = (f32[51,256]{1,0:T(8,128)S(1)}, f32[51,256]{1,0:T(8,128)}, u32[]{:S(2)}) copy-start(f32[51,256]{1,0:T(8,128)} %constant.47.clone.wave_ref) | copy-start | bytes 156676
  2.9 45.2 %copy-start.4 = (f32[34,384]{1,0:T(8,128)S(1)}, f32[34,384]{1,0:T(8,128)}, u32[]{:S(2)}) copy-start(f32[34,384]{1,0:T(8,128)} %constant.48.clone.twiddle_ref) | copy-start | bytes 156676
  2.9 45.2 %all-to-all-start = ((f32[32,34,1,128]{3,2,1,0:T(1,128)}), f32[32,34,1,128]{3,2,1,0:T(1,128)S(1)}, u32[]{:S(2)}, u32[]{:S(2)}) async-start(f32[32,34,1,128]{3,2,1,0:T(1,128)} %bitcast.33), calls=%async_computation | async-start | bytes 1114112 | tf_op jit(solution)/shard_map/all_to_all | solution.py:581
  22.2 1.4 %copy-start = (f32[768,512]{1,0:T(8,128)S(1)}, f32[768,512]{1,0:T(8,128)}, u32[]{:S(2)}) copy-start(f32[768,512]{1,0:T(8,128)} %constant.46.clone.table_ref) | copy-start | bytes 4718596
  49.6 5.6 %collective-permute-start = (f32[136,128]{1,0:T(8,128)S(1)}, f32[136,128]{1,0:T(8,128)S(1)}, u32[]{:S(2)}, u32[]{:S(2)}) collective-permute-start(f32[136,128]{1,0:T(8,128)S(1)} %get-tuple-element.22), channel_id=1, source_target_pairs={{224,208},{192,176},{160,144},{128,112},{96,80},{64,48},{32,16},{0... | collective-permute-start | bytes 208904 | tf_op jit(solution)/shard_map/ppermute | solution.py:595
  51.5 3.7 %collective-permute-start.1 = (f32[136,128]{1,0:T(8,128)S(1)}, f32[136,128]{1,0:T(8,128)S(1)}, u32[]{:S(2)}, u32[]{:S(2)}) collective-permute-start(f32[136,128]{1,0:T(8,128)S(1)} %get-tuple-element.23), channel_id=1, source_target_pairs={{240,224},{208,192},{176,160},{144,128},{112,96},{80,64},{48,32},{... | collective-permute-start | bytes 208904 | tf_op jit(solution)/shard_map/ppermute | solution.py:596
  55.2 40.2 %copy-start.1 = (f32[2,180,128]{2,0,1:T(2,128)S(1)}, f32[2,180,128]{2,0,1:T(2,128)}, u32[]{:S(2)}) copy-start(f32[2,180,128]{2,0,1:T(2,128)} %param.9) | copy-start | bytes 552964
  55.2 40.2 %copy-start.2 = (f32[2,180,128]{2,0,1:T(2,128)S(1)}, f32[2,180,128]{2,0,1:T(2,128)}, u32[]{:S(2)}) copy-start(f32[2,180,128]{2,0,1:T(2,128)} %param.10) | copy-start | bytes 552964
  55.2 40.2 %copy-start.3 = (f32[2,180,128]{2,0,1:T(2,128)S(1)}, f32[2,180,128]{2,0,1:T(2,128)}, u32[]{:S(2)}) copy-start(f32[2,180,128]{2,0,1:T(2,128)} %param.11) | copy-start | bytes 552964

commit v9 on v8

--- a/solution.py
+++ b/solution.py
@@ -84,6 +84,7 @@
 PUSH_COEF = 0.25 / 2.0
 FIRST = 20
 ORDER = [(i + FIRST) % PARTS for i in range(PARTS)]
+ORDER[13], ORDER[26] = ORDER[26], ORDER[13]
 
 
 def add(x, y):

time: 96.9 us -> 95.1 us (0.981)
  waiting for transfers between devices: 25.1 us -> 22.7 us
  starting transfers between devices: 22.4 us -> 24.7 us
  blocking collectives: 38.6 us -> 36.9 us
    ppermute x1, starting transfers between devices: 1.92 us -> 4.26 us  [step(): far = lax.ppermute(far, ('lon', 'lat'), swaps(1))]
    all_to_all x1, waiting for transfers between devices: 24 us -> 22.2 us  [exchange(): lax.all_to_all(chunks.reshape(PARTS, CHUNK, 1, LANES), 'lon', 0, 0, axis_...]
    all_to_all x1, blocking collectives: 38.6 us -> 36.9 us  [exchange(): lax.all_to_all(chunks.reshape(PARTS, CHUNK, 1, LANES), 'lon', 0, 0, axis_...]
    ppermute x1, waiting for transfers between devices: 1.04 us -> 0.01 us  [step(): far = lax.ppermute(far, ('lon', 'lat'), swaps(1))]
where the time goes in v9:
time: 95.1 us; the launch traced here: 94.7 us
  blocking collectives  36.9 us (39%)
  starting transfers between devices  24.7 us (26%)
  waiting for transfers between devices  22.7 us (24%)
  Pallas kernels  7.55 us (8%)
  local copies, waits for them, and re-layouts  2.13 us (2%)
    all_to_all x1, blocking collectives, exchange(): lax.all_to_all(chunks.reshape(PARTS, CHUNK, 1, LANES), 'lon', 0, 0, axis_...  36.9 us
    all_to_all x1, waiting for transfers between devices, exchange(): lax.all_to_all(chunks.reshape(PARTS, CHUNK, 1, LANES), 'lon', 0, 0, axis_...  22.2 us
    all_to_all x1, starting transfers between devices, exchange(): lax.all_to_all(chunks.reshape(PARTS, CHUNK, 1, LANES), 'lon', 0, 0, axis_...  18.5 us
    ppermute x1, starting transfers between devices, step(): far = lax.ppermute(far, ('lon', 'lat'), swaps(1))  4.26 us
    pallas_call x1, Pallas kernels, pack(): pl.pallas_call(pack_kernel, out_shape=like(PARTS * CHUNK, LANES), in_spec...  2.27 us
    ppermute x1, starting transfers between devices, step(): near = lax.ppermute(near, ('lon', 'lat'), swaps(0))  1.92 us
  transfers between devices with their start and end apart: 3, of which 2 were waited for; matrix products, arithmetic and copies ran while one was open for 1% of the time, Pallas kernels for 1%

profile of v9, /device:TPU:1, one launch (start us, length us, event | category | flops | bytes accessed | tf_op | source)
XLA Modules:
  0.0 94.7 jit_solution(5379825744516540147)
XLA Ops:
  0.6 0.0 copy-start.5
  0.7 2.3 %pack.1 = f32[1088,128]{1,0:T(8,128)} custom-call(s32[1]{0:T(128)} %bitcast.turn_ref, f32[360,128]{1,0:T(8,128)} %bitcast.27, f32[360,128]{1,0:T(8,128)} %bitcast.29, f32[360,128]{1,0:T(8,128)} %bitcast.31), custom_call_target="tpu_custom_call" | custom-call | tf_op jit(solution)/shard_map/pack/pallas_call | solution.py:494
  2.9 0.0 copy-start.4
  2.9 18.5 %all-to-all-start = ((f32[32,34,1,128]{3,2,1,0:T(1,128)}), f32[32,34,1,128]{3,2,1,0:T(1,128)S(1)}, u32[]{:S(2)}, u32[]{:S(2)}) async-start(f32[32,34,1,128]{3,2,1,0:T(1,128)} %bitcast.33), calls=%async_computation | async-start | bytes 1114112 | tf_op jit(solution)/shard_map/all_to_all | solution.py:582
  21.5 0.7 constant_dynamic-slice_fusion.row_ref
  22.2 0.0 copy-done.5
  22.2 0.0 copy-start
  22.2 1.4 %copy-done = f32[768,512]{1,0:T(8,128)S(1)} copy-done((f32[768,512]{1,0:T(8,128)S(1)}, f32[768,512]{1,0:T(8,128)}, u32[]{:S(2)}) %copy-start) | copy-done | bytes 1572888
  23.6 0.5 factors.1
  24.1 22.2 %all-to-all-done = f32[32,34,1,128]{3,2,1,0:T(1,128)S(1)} async-done(((f32[32,34,1,128]{3,2,1,0:T(1,128)}), f32[32,34,1,128]{3,2,1,0:T(1,128)S(1)}, u32[]{:S(2)}, u32[]{:S(2)}) %all-to-all-start) | async-done | bytes 557088 | tf_op jit(solution)/shard_map/all_to_all | solution.py:582
  46.3 0.0 copy-done.4
  46.3 1.5 %forward_mass.1 = (f32[416,512]{1,0:T(8,128)S(1)}, f32[136,128]{1,0:T(8,128)S(1)}, f32[136,128]{1,0:T(8,128)S(1)}) custom-call(f32[1088,128]{1,0:T(8,128)S(1)} %bitcast.23, bf16[768,512]{1,0:T(8,128)(2,1)S(1)} %get-tuple-element.16.high_ref, bf16[768,512]{1,0:T(8,128)(2,1)S(1)} %get-tuple-element.17.low_ref, f32[34,384]{1,0:T(8,128)S(1)} %copy-done.4, ...), custom_call_target="tpu_custom_call" | custom-call | flops 654311424 | bytes 1703936 | tf_op jit(solution)/shard_map/forward_mass/pallas_call | solution.py:526
  47.8 4.3 %collective-permute-start = (f32[136,128]{1,0:T(8,128)S(1)}, f32[136,128]{1,0:T(8,128)S(1)}, u32[]{:S(2)}, u32[]{:S(2)}) collective-permute-start(f32[136,128]{1,0:T(8,128)S(1)} %get-tuple-element.22), channel_id=1, source_target_pairs={{224,208},{192,176},{160,144},{128,112},{96,80},{64,48},{32,16},{0... | collective-permute-start | bytes 208904 | tf_op jit(solution)/shard_map/ppermute | solution.py:596
  52.1 1.9 %collective-permute-start.1 = (f32[136,128]{1,0:T(8,128)S(1)}, f32[136,128]{1,0:T(8,128)S(1)}, u32[]{:S(2)}, u32[]{:S(2)}) collective-permute-start(f32[136,128]{1,0:T(8,128)S(1)} %get-tuple-element.23), channel_id=1, source_target_pairs={{240,224},{208,192},{176,160},{144,128},{112,96},{80,64},{48,32},{... | collective-permute-start | bytes 208904 | tf_op jit(solution)/shard_map/ppermute | solution.py:597
  54.0 0.7 forward_wind.1.wind_ref
  54.7 0.0 collective-permute-done.far_ref
  54.7 0.5 collective-permute-done.1.near_ref
  55.2 0.0 copy-start.2
  55.2 1.5 %inverse.1 = f32[1088,128]{1,0:T(8,128)S(1)} custom-call(f32[416,512]{1,0:T(8,128)S(1)} %get-tuple-element.20.spec_ref, f32[272,512]{1,0:T(8,128)S(1)} %forward_wind.1.wind_ref, f32[136,128]{1,0:T(8,128)S(1)} %collective-permute-done.far_ref, f32[136,128]{1,0:T(8,128)S(1)} %collective-permute-done.1.near_ref, ...), custom_call_target="tpu_custom_call" | custom-call | flops 654311424 | bytes 1703936 | tf_op jit(solution)/shard_map/inverse/pallas_call | solution.py:552
  56.8 36.9 %all_to_all.10 = f32[32,34,1,128]{3,2,1,0:T(1,128)S(1)} all-to-all(f32[32,34,1,128]{3,2,1,0:T(1,128)S(1)} %bitcast.26), channel_id=1, replica_groups={{320,336,352,368,384,400,416,432,448,464,480,496,0,224,32,48,64,80,96,1..., dimensions={0} | all-to-all | bytes 1114112 | tf_op jit(solution)/shard_map/all_to_all | solution.py:582
  93.7 0.0 copy-done.1
  93.7 0.0 copy-done.2
  93.7 0.0 copy-done.3
  93.7 1.0 %unpack.1 = (f32[360,128]{1,0:T(8,128)}, f32[360,128]{1,0:T(8,128)}, f32[360,128]{1,0:T(8,128)}) custom-call(s32[1]{0:T(128)} %bitcast.turn_ref, f32[1088,128]{1,0:T(8,128)S(1)} %bitcast.25, f32[360,128]{1,0:T(8,128)S(1)} %bitcast.28, f32[360,128]{1,0:T(8,128)S(1)} %bitcast.30, f32[360,128]{1,0:T(8,128)S(1)} %bitcast.32), custom_call_target="tpu_custom_call" | custom-call | tf_op jit(solution)/shard_map/unpack/pallas_call | solution.py:565
  (2 shorter events, 0.0 us)
Async XLA Ops:
  0.6 21.6 %copy-start.5 = (f32[51,256]{1,0:T(8,128)S(1)}, f32[51,256]{1,0:T(8,128)}, u32[]{:S(2)}) copy-start(f32[51,256]{1,0:T(8,128)} %constant.47.clone.wave_ref) | copy-start | bytes 156676
  2.9 43.4 %copy-start.4 = (f32[34,384]{1,0:T(8,128)S(1)}, f32[34,384]{1,0:T(8,128)}, u32[]{:S(2)}) copy-start(f32[34,384]{1,0:T(8,128)} %constant.48.clone.twiddle_ref) | copy-start | bytes 156676
  2.9 43.4 %all-to-all-start = ((f32[32,34,1,128]{3,2,1,0:T(1,128)}), f32[32,34,1,128]{3,2,1,0:T(1,128)S(1)}, u32[]{:S(2)}, u32[]{:S(2)}) async-start(f32[32,34,1,128]{3,2,1,0:T(1,128)} %bitcast.33), calls=%async_computation | async-start | bytes 1114112 | tf_op jit(solution)/shard_map/all_to_all | solution.py:582
  22.2 1.4 %copy-start = (f32[768,512]{1,0:T(8,128)S(1)}, f32[768,512]{1,0:T(8,128)}, u32[]{:S(2)}) copy-start(f32[768,512]{1,0:T(8,128)} %constant.46.clone.table_ref) | copy-start | bytes 4718596
  47.8 6.9 %collective-permute-start = (f32[136,128]{1,0:T(8,128)S(1)}, f32[136,128]{1,0:T(8,128)S(1)}, u32[]{:S(2)}, u32[]{:S(2)}) collective-permute-start(f32[136,128]{1,0:T(8,128)S(1)} %get-tuple-element.22), channel_id=1, source_target_pairs={{224,208},{192,176},{160,144},{128,112},{96,80},{64,48},{32,16},{0... | collective-permute-start | bytes 208904 | tf_op jit(solution)/shard_map/ppermute | solution.py:596
  52.1 3.2 %collective-permute-start.1 = (f32[136,128]{1,0:T(8,128)S(1)}, f32[136,128]{1,0:T(8,128)S(1)}, u32[]{:S(2)}, u32[]{:S(2)}) collective-permute-start(f32[136,128]{1,0:T(8,128)S(1)} %get-tuple-element.23), channel_id=1, source_target_pairs={{240,224},{208,192},{176,160},{144,128},{112,96},{80,64},{48,32},{... | collective-permute-start | bytes 208904 | tf_op jit(solution)/shard_map/ppermute | solution.py:597
  55.2 38.4 %copy-start.1 = (f32[2,180,128]{2,0,1:T(2,128)S(1)}, f32[2,180,128]{2,0,1:T(2,128)}, u32[]{:S(2)}) copy-start(f32[2,180,128]{2,0,1:T(2,128)} %param.9) | copy-start | bytes 552964
  55.2 38.4 %copy-start.2 = (f32[2,180,128]{2,0,1:T(2,128)S(1)}, f32[2,180,128]{2,0,1:T(2,128)}, u32[]{:S(2)}) copy-start(f32[2,180,128]{2,0,1:T(2,128)} %param.10) | copy-start | bytes 552964
  55.2 38.4 %copy-start.3 = (f32[2,180,128]{2,0,1:T(2,128)S(1)}, f32[2,180,128]{2,0,1:T(2,128)}, u32[]{:S(2)}) copy-start(f32[2,180,128]{2,0,1:T(2,128)} %param.11) | copy-start | bytes 552964

commit v10 on v9

--- a/solution.py
+++ b/solution.py
@@ -85,6 +85,7 @@
 FIRST = 20
 ORDER = [(i + FIRST) % PARTS for i in range(PARTS)]
 ORDER[13], ORDER[26] = ORDER[26], ORDER[13]
+ORDER[15], ORDER[31] = ORDER[31], ORDER[15]
 
 
 def add(x, y):

time: 95.1 us -> 95.1 us (level)
  no operation moved by 1% of the time
where the time goes in v10:
time: 95.1 us; the launch traced here: 94.7 us
  blocking collectives  37.3 us (39%)
  starting transfers between devices  24.3 us (26%)
  waiting for transfers between devices  22.7 us (24%)
  Pallas kernels  7.55 us (8%)
  local copies, waits for them, and re-layouts  2.13 us (2%)
    all_to_all x1, blocking collectives, exchange(): lax.all_to_all(chunks.reshape(PARTS, CHUNK, 1, LANES), 'lon', 0, 0, axis_...  37.3 us
    all_to_all x1, waiting for transfers between devices, exchange(): lax.all_to_all(chunks.reshape(PARTS, CHUNK, 1, LANES), 'lon', 0, 0, axis_...  22.2 us
    all_to_all x1, starting transfers between devices, exchange(): lax.all_to_all(chunks.reshape(PARTS, CHUNK, 1, LANES), 'lon', 0, 0, axis_...  18.5 us
    ppermute x1, starting transfers between devices, step(): far = lax.ppermute(far, ('lon', 'lat'), swaps(1))  3.85 us
    pallas_call x1, Pallas kernels, pack(): pl.pallas_call(pack_kernel, out_shape=like(PARTS * CHUNK, LANES), in_spec...  2.27 us
    ppermute x1, starting transfers between devices, step(): near = lax.ppermute(near, ('lon', 'lat'), swaps(0))  1.92 us
  transfers between devices with their start and end apart: 3, of which 2 were waited for; matrix products, arithmetic and copies ran while one was open for 1% of the time, Pallas kernels for 1%

profile of v10, /device:TPU:1, one launch (start us, length us, event | category | flops | bytes accessed | tf_op | source)
XLA Modules:
  0.0 94.7 jit_solution(7100420936886199430)
XLA Ops:
  0.6 0.0 copy-start.5
  0.7 2.3 %pack.1 = f32[1088,128]{1,0:T(8,128)} custom-call(s32[1]{0:T(128)} %bitcast.turn_ref, f32[360,128]{1,0:T(8,128)} %bitcast.27, f32[360,128]{1,0:T(8,128)} %bitcast.29, f32[360,128]{1,0:T(8,128)} %bitcast.31), custom_call_target="tpu_custom_call" | custom-call | tf_op jit(solution)/shard_map/pack/pallas_call | solution.py:495
  2.9 0.0 copy-start.4
  2.9 18.5 %all-to-all-start = ((f32[32,34,1,128]{3,2,1,0:T(1,128)}), f32[32,34,1,128]{3,2,1,0:T(1,128)S(1)}, u32[]{:S(2)}, u32[]{:S(2)}) async-start(f32[32,34,1,128]{3,2,1,0:T(1,128)} %bitcast.33), calls=%async_computation | async-start | bytes 1114112 | tf_op jit(solution)/shard_map/all_to_all | solution.py:583
  21.5 0.7 constant_dynamic-slice_fusion.row_ref
  22.2 0.0 copy-done.5
  22.2 0.0 copy-start
  22.2 1.4 %copy-done = f32[768,512]{1,0:T(8,128)S(1)} copy-done((f32[768,512]{1,0:T(8,128)S(1)}, f32[768,512]{1,0:T(8,128)}, u32[]{:S(2)}) %copy-start) | copy-done | bytes 1572888
  23.6 0.5 factors.1
  24.1 22.2 %all-to-all-done = f32[32,34,1,128]{3,2,1,0:T(1,128)S(1)} async-done(((f32[32,34,1,128]{3,2,1,0:T(1,128)}), f32[32,34,1,128]{3,2,1,0:T(1,128)S(1)}, u32[]{:S(2)}, u32[]{:S(2)}) %all-to-all-start) | async-done | bytes 557088 | tf_op jit(solution)/shard_map/all_to_all | solution.py:583
  46.3 0.0 copy-done.4
  46.3 1.5 %forward_mass.1 = (f32[416,512]{1,0:T(8,128)S(1)}, f32[136,128]{1,0:T(8,128)S(1)}, f32[136,128]{1,0:T(8,128)S(1)}) custom-call(f32[1088,128]{1,0:T(8,128)S(1)} %bitcast.23, bf16[768,512]{1,0:T(8,128)(2,1)S(1)} %get-tuple-element.16.high_ref, bf16[768,512]{1,0:T(8,128)(2,1)S(1)} %get-tuple-element.17.low_ref, f32[34,384]{1,0:T(8,128)S(1)} %copy-done.4, ...), custom_call_target="tpu_custom_call" | custom-call | flops 654311424 | bytes 1703936 | tf_op jit(solution)/shard_map/forward_mass/pallas_call | solution.py:527
  47.8 3.9 %collective-permute-start = (f32[136,128]{1,0:T(8,128)S(1)}, f32[136,128]{1,0:T(8,128)S(1)}, u32[]{:S(2)}, u32[]{:S(2)}) collective-permute-start(f32[136,128]{1,0:T(8,128)S(1)} %get-tuple-element.22), channel_id=1, source_target_pairs={{224,208},{192,176},{160,144},{128,112},{96,80},{64,48},{32,16},{0... | collective-permute-start | bytes 208904 | tf_op jit(solution)/shard_map/ppermute | solution.py:597
  51.7 1.9 %collective-permute-start.1 = (f32[136,128]{1,0:T(8,128)S(1)}, f32[136,128]{1,0:T(8,128)S(1)}, u32[]{:S(2)}, u32[]{:S(2)}) collective-permute-start(f32[136,128]{1,0:T(8,128)S(1)} %get-tuple-element.23), channel_id=1, source_target_pairs={{240,224},{208,192},{176,160},{144,128},{112,96},{80,64},{48,32},{... | collective-permute-start | bytes 208904 | tf_op jit(solution)/shard_map/ppermute | solution.py:598
  53.6 0.7 forward_wind.1.wind_ref
  54.3 0.0 collective-permute-done.far_ref
  54.3 0.5 collective-permute-done.1.near_ref
  54.8 0.0 copy-start.1
  54.8 1.5 %inverse.1 = f32[1088,128]{1,0:T(8,128)S(1)} custom-call(f32[416,512]{1,0:T(8,128)S(1)} %get-tuple-element.20.spec_ref, f32[272,512]{1,0:T(8,128)S(1)} %forward_wind.1.wind_ref, f32[136,128]{1,0:T(8,128)S(1)} %collective-permute-done.far_ref, f32[136,128]{1,0:T(8,128)S(1)} %collective-permute-done.1.near_ref, ...), custom_call_target="tpu_custom_call" | custom-call | flops 654311424 | bytes 1703936 | tf_op jit(solution)/shard_map/inverse/pallas_call | solution.py:553
  56.4 37.3 %all_to_all.10 = f32[32,34,1,128]{3,2,1,0:T(1,128)S(1)} all-to-all(f32[32,34,1,128]{3,2,1,0:T(1,128)S(1)} %bitcast.26), channel_id=1, replica_groups={{320,336,352,368,384,400,416,432,448,464,480,496,0,224,32,304,64,80,96,..., dimensions={0} | all-to-all | bytes 1114112 | tf_op jit(solution)/shard_map/all_to_all | solution.py:583
  93.7 0.0 copy-done.1
  93.7 0.0 copy-done.2
  93.7 0.0 copy-done.3
  93.7 1.0 %unpack.1 = (f32[360,128]{1,0:T(8,128)}, f32[360,128]{1,0:T(8,128)}, f32[360,128]{1,0:T(8,128)}) custom-call(s32[1]{0:T(128)} %bitcast.turn_ref, f32[1088,128]{1,0:T(8,128)S(1)} %bitcast.25, f32[360,128]{1,0:T(8,128)S(1)} %bitcast.28, f32[360,128]{1,0:T(8,128)S(1)} %bitcast.30, f32[360,128]{1,0:T(8,128)S(1)} %bitcast.32), custom_call_target="tpu_custom_call" | custom-call | tf_op jit(solution)/shard_map/unpack/pallas_call | solution.py:566
  (2 shorter events, 0.0 us)
Async XLA Ops:
  0.6 21.6 %copy-start.5 = (f32[51,256]{1,0:T(8,128)S(1)}, f32[51,256]{1,0:T(8,128)}, u32[]{:S(2)}) copy-start(f32[51,256]{1,0:T(8,128)} %constant.47.clone.wave_ref) | copy-start | bytes 156676
  2.9 43.4 %copy-start.4 = (f32[34,384]{1,0:T(8,128)S(1)}, f32[34,384]{1,0:T(8,128)}, u32[]{:S(2)}) copy-start(f32[34,384]{1,0:T(8,128)} %constant.48.clone.twiddle_ref) | copy-start | bytes 156676
  2.9 43.4 %all-to-all-start = ((f32[32,34,1,128]{3,2,1,0:T(1,128)}), f32[32,34,1,128]{3,2,1,0:T(1,128)S(1)}, u32[]{:S(2)}, u32[]{:S(2)}) async-start(f32[32,34,1,128]{3,2,1,0:T(1,128)} %bitcast.33), calls=%async_computation | async-start | bytes 1114112 | tf_op jit(solution)/shard_map/all_to_all | solution.py:583
  22.2 1.4 %copy-start = (f32[768,512]{1,0:T(8,128)S(1)}, f32[768,512]{1,0:T(8,128)}, u32[]{:S(2)}) copy-start(f32[768,512]{1,0:T(8,128)} %constant.46.clone.table_ref) | copy-start | bytes 4718596
  47.8 6.5 %collective-permute-start = (f32[136,128]{1,0:T(8,128)S(1)}, f32[136,128]{1,0:T(8,128)S(1)}, u32[]{:S(2)}, u32[]{:S(2)}) collective-permute-start(f32[136,128]{1,0:T(8,128)S(1)} %get-tuple-element.22), channel_id=1, source_target_pairs={{224,208},{192,176},{160,144},{128,112},{96,80},{64,48},{32,16},{0... | collective-permute-start | bytes 208904 | tf_op jit(solution)/shard_map/ppermute | solution.py:597
  51.7 3.2 %collective-permute-start.1 = (f32[136,128]{1,0:T(8,128)S(1)}, f32[136,128]{1,0:T(8,128)S(1)}, u32[]{:S(2)}, u32[]{:S(2)}) collective-permute-start(f32[136,128]{1,0:T(8,128)S(1)} %get-tuple-element.23), channel_id=1, source_target_pairs={{240,224},{208,192},{176,160},{144,128},{112,96},{80,64},{48,32},{... | collective-permute-start | bytes 208904 | tf_op jit(solution)/shard_map/ppermute | solution.py:598
  54.8 38.9 %copy-start.1 = (f32[2,180,128]{2,0,1:T(2,128)S(1)}, f32[2,180,128]{2,0,1:T(2,128)}, u32[]{:S(2)}) copy-start(f32[2,180,128]{2,0,1:T(2,128)} %param.9) | copy-start | bytes 552964
  54.8 38.9 %copy-start.2 = (f32[2,180,128]{2,0,1:T(2,128)S(1)}, f32[2,180,128]{2,0,1:T(2,128)}, u32[]{:S(2)}) copy-start(f32[2,180,128]{2,0,1:T(2,128)} %param.10) | copy-start | bytes 552964
  54.8 38.9 %copy-start.3 = (f32[2,180,128]{2,0,1:T(2,128)S(1)}, f32[2,180,128]{2,0,1:T(2,128)}, u32[]{:S(2)}) copy-start(f32[2,180,128]{2,0,1:T(2,128)} %param.11) | copy-start | bytes 552964
